TPU v7x, 512 devices: a whole 4x4x16 slice. The times are simulated.
512 devices in a mesh: gy: 16 (over z_hi, x, core), gx: 32 (over y, z_lo).
Axes of the slice: x: 4, y: 4, z: 16 (z_hi: 2, z_lo: 8; z = z_hi * 8 + z_lo), core: 2. Of those that a mesh axis runs over, the one named last changes fastest.
Arguments:
- heat_anomaly: float32 [75, 128, 4096], P(None, 'gy', 'gx'), may hold values from -6 to 6
- saltiness_anomaly: float32 [75, 128, 4096], P(None, 'gy', 'gx'), may hold values from -6 to 6
- eastward_transit_number: float32 [75, 128, 4096], P(None, 'gy', 'gx'), may hold values from -1.5 to 1.5
- poleward_transit_number: float32 [75, 128, 4096], P(None, 'gy', 'gx'), may hold values from -1.5 to 1.5
- rising_transit_number: float32 [75, 128, 4096], P(None, 'gy', 'gx'), may hold values from -1.5 to 1.5
- stacked_mixing_number: float32 [75, 128, 4096], P(None, 'gy', 'gx'), may hold values from 0.05 to 5
- neutral_mixing_number: float32 [128, 4096], P('gy', 'gx'), may hold values from 0.02 to 0.2
- ocean_strata_total: int32 [128, 4096], P('gy', 'gx'), may hold values from 0 to 75, as said below
Outputs:
- revised_heat_anomaly: float32 [75, 128, 4096], P(None, 'gy', 'gx')
- revised_saltiness: float32 [75, 128, 4096], P(None, 'gy', 'gx')
Inputs may be any that keep to these rules, and one draw needn't show every extreme that they name: Levels k >= ocean_strata_total of a column are land; the southernmost row is land.
All inputs are finite; a program needn't handle non-finite values.
Results may differ from a plain program's by a relative error of at most 0.00002.
Values sent between devices are 32-bit elements; how exact they have to be, the bound alone decides.
No kernel may reach another device: no remote copies, remote signals or barrier semaphores. Data moves between devices by JAX's collectives and lax.ppermute only.
A program may use at most 64 MiB of HBM per device.

v0:
```python
import jax
import jax.numpy as jnp
from jax import lax
from jax.sharding import PartitionSpec as P

thermal_coef = 0.1655
haline_coef = 0.76554
thermal_curve = 0.05952
haline_curve = 0.00054914
thermal_press = 0.0001497
haline_press = 1.109e-05
cabbeling = 0.0024341
bottom_depth = 5800.0
slope_limit = 1.0
strat_offset = 0.1


def shifted(value, axis, steps):
    count = lax.axis_size(axis)
    leading, last = (max(0, -steps), min(count, count - steps))
    return lax.ppermute(value, axis, [(source, source + steps) for source in range(leading, last)])


def passed_along(value, axis, steps):
    count = lax.axis_size(axis)
    pairs = [(source, (source + steps) % count) for source in range(count)]
    return lax.ppermute(value, axis, pairs)


def swapped(x, axis, bit):
    return lax.ppermute(x, axis, [(i, i ^ 1 << bit) for i in range(lax.axis_size(axis))])


def stratum_height_entry(level_count):
    level_index = jnp.arange(level_count, dtype=jnp.float32)
    return bottom_depth * ((level_index + 0.5) / level_count) ** 2


def density(temper, saline, strata_heights):
    return (
        -thermal_coef
        * (1.0 + 0.5 * thermal_curve * temper + thermal_press * strata_heights)
        * temper
        + haline_coef * (1.0 - 0.5 * haline_curve * saline - haline_press * strata_heights) * saline
        - cabbeling * temper * saline
    )


def column_diff(values_in, ocean_volume_flags):
    steps_up = (values_in[1:] - values_in[:-1]) * ocean_volume_flags[1:] * ocean_volume_flags[:-1]
    zeroed_stratum_sheet = jnp.zeros_like(values_in[:1])
    return 0.5 * (
        jnp.concatenate([zeroed_stratum_sheet, steps_up], 0)
        + jnp.concatenate([steps_up, zeroed_stratum_sheet], 0)
    )


def volume_scalar_carry(temper, saline, ocean_share, diffus, strata_heights):
    level_count = temper.shape[0]
    level_index = jnp.arange(level_count, dtype=jnp.float32).reshape(level_count, 1, 1)
    ocean_volume_flags = jnp.where(level_index < ocean_share, 1.0, 0.0).astype(temper.dtype)
    dens = density(temper, saline, strata_heights.reshape(level_count, 1, 1))
    return (
        temper,
        saline,
        ocean_volume_flags,
        dens,
        column_diff(temper, ocean_volume_flags),
        column_diff(saline, ocean_volume_flags),
        column_diff(dens, ocean_volume_flags),
        diffus,
    )


def face_flux(face_speed, left_cell, right_cell):
    face_wet = left_cell[2] * right_cell[2]
    face_diff = 0.5 * (left_cell[7] + right_cell[7])
    denominator = jnp.maximum(0.5 * (left_cell[6] + right_cell[6]), 0.0) + strat_offset
    slope_face = jnp.clip((right_cell[3] - left_cell[3]) / denominator, -slope_limit, slope_limit)
    forward = jnp.maximum(face_speed, 0.0)
    backward = jnp.minimum(face_speed, 0.0)
    flux_t = face_wet * (
        forward * left_cell[0]
        + backward * right_cell[0]
        - face_diff
        * (right_cell[0] - left_cell[0] - slope_face * 0.5 * (left_cell[4] + right_cell[4]))
    )
    flux_s = face_wet * (
        forward * left_cell[1]
        + backward * right_cell[1]
        - face_diff
        * (right_cell[1] - left_cell[1] - slope_face * 0.5 * (left_cell[5] + right_cell[5]))
    )
    return (flux_t, flux_s)


def tridiagonal_system_solver(rhs_t, rhs_s, vert_diff, ocean_volume_flags):
    coupling = vert_diff[1:] * ocean_volume_flags[1:] * ocean_volume_flags[:-1]
    zeroed_stratum_sheet = jnp.zeros_like(vert_diff[:1])
    coupling_above = jnp.concatenate([zeroed_stratum_sheet, coupling], 0)
    coupling_below = jnp.concatenate([coupling, zeroed_stratum_sheet], 0)
    center = 1.0 + coupling_above + coupling_below

    def forward(state_carry, level_items):
        prev_ratio, prev_t, prev_s = state_carry
        above_k, below_k, center_k, rhs_tk, rhs_sk = level_items
        pivot_value = center_k - above_k * prev_ratio
        next_ratio = below_k / pivot_value
        next_t = (rhs_tk + above_k * prev_t) / pivot_value
        next_s = (rhs_sk + above_k * prev_s) / pivot_value
        return ((next_ratio, next_t, next_s), (next_ratio, next_t, next_s))

    start_plane = jnp.zeros_like(rhs_t[0])
    _, (ratios, part_t, part_s) = lax.scan(
        forward,
        (start_plane, start_plane, start_plane),
        (coupling_above, coupling_below, center, rhs_t, rhs_s),
        unroll=True,
    )

    def backward(state_carry, level_items):
        below_t, below_s = state_carry
        ratio_k, part_tk, part_sk = level_items
        solved_t = part_tk + ratio_k * below_t
        solved_s = part_sk + ratio_k * below_s
        return ((solved_t, solved_s), (solved_t, solved_s))

    _, (solved_t, solved_s) = lax.scan(
        backward, (start_plane, start_plane), (ratios, part_t, part_s), reverse=True, unroll=True
    )
    return (solved_t, solved_s)


def march_scalar_fields(
    heat_anomaly,
    saltiness_anomaly,
    eastern_heat_entry,
    eastern_saltiness,
    upper_heat_entry,
    upper_saltiness,
    rising_transit_number,
    stacked_mixing_number,
    ocean_volume_flags,
):
    joint_ocean_flags = ocean_volume_flags[1:] * ocean_volume_flags[:-1]
    backward_substitution_pass = jnp.maximum(rising_transit_number[1:], 0.0)
    forward_elimination = jnp.minimum(rising_transit_number[1:], 0.0)
    zeroed_stratum_sheet = jnp.zeros_like(heat_anomaly[:1])
    surface_heat_entry = jnp.concatenate(
        [
            zeroed_stratum_sheet,
            joint_ocean_flags
            * (
                backward_substitution_pass * heat_anomaly[1:]
                + forward_elimination * heat_anomaly[:-1]
            ),
        ],
        0,
    )
    top_s = jnp.concatenate(
        [
            zeroed_stratum_sheet,
            joint_ocean_flags
            * (
                backward_substitution_pass * saltiness_anomaly[1:]
                + forward_elimination * saltiness_anomaly[:-1]
            ),
        ],
        0,
    )
    seabed_heat_entry = jnp.concatenate([surface_heat_entry[1:], zeroed_stratum_sheet], 0)
    bottom_s = jnp.concatenate([top_s[1:], zeroed_stratum_sheet], 0)
    partial_heat_estimate = (
        heat_anomaly
        - eastern_heat_entry
        - upper_heat_entry
        - (surface_heat_entry - seabed_heat_entry)
    )
    provisional_saltiness = (
        saltiness_anomaly - eastern_saltiness - upper_saltiness - (top_s - bottom_s)
    )
    return tridiagonal_system_solver(
        partial_heat_estimate, provisional_saltiness, stacked_mixing_number, ocean_volume_flags
    )


def extend(center, south_row, north_row, west_col, east_col):
    middle = jnp.concatenate([west_col[..., None], center, east_col[..., None]], -1)
    widths = [(0, 0)] * (south_row.ndim - 1) + [(1, 1)]
    south_pad = jnp.pad(south_row, widths)[..., None, :]
    north_pad = jnp.pad(north_row, widths)[..., None, :]
    return jnp.concatenate([south_pad, middle, north_pad], -2)


def local(
    heat_anomaly,
    saltiness_anomaly,
    eastward_transit_number,
    poleward_transit_number,
    rising_transit_number,
    stacked_mixing_number,
    neutral_mixing_number,
    ocean_strata_total,
):
    stratum_indices = heat_anomaly.shape[0]
    ocean_share = ocean_strata_total.astype(jnp.float32)
    top_pack = jnp.concatenate(
        [
            heat_anomaly[:, -1],
            saltiness_anomaly[:, -1],
            poleward_transit_number[:, -1],
            neutral_mixing_number[-1:],
            ocean_share[-1:],
        ],
        0,
    )
    bottom_pack = jnp.concatenate(
        [heat_anomaly[:, 0], saltiness_anomaly[:, 0], neutral_mixing_number[:1], ocean_share[:1]], 0
    )
    east_pack = jnp.concatenate(
        [
            heat_anomaly[:, :, -1],
            saltiness_anomaly[:, :, -1],
            eastward_transit_number[:, :, -1],
            neutral_mixing_number[None, :, -1],
            ocean_share[None, :, -1],
        ],
        0,
    )
    west_pack = jnp.concatenate(
        [
            heat_anomaly[:, :, 0],
            saltiness_anomaly[:, :, 0],
            neutral_mixing_number[None, :, 0],
            ocean_share[None, :, 0],
        ],
        0,
    )
    south_neighbour_cells = shifted(top_pack, "gy", 1)
    from_north = shifted(bottom_pack, "gy", -1)
    west_neighbour_cells = passed_along(east_pack, "gx", 1)
    east_neighbour_cells = passed_along(west_pack, "gx", -1)
    bit_list = list(range(lax.axis_size("gx").bit_length() - 1))
    mirror_pack = top_pack
    for which_bit in bit_list:
        mirror_pack = swapped(mirror_pack, "gx", which_bit)
    mirror_pack = mirror_pack[:, ::-1]
    is_top = lax.axis_index("gy") == lax.axis_size("gy") - 1
    upper_boundary_heat = jnp.where(
        is_top, mirror_pack[:stratum_indices], from_north[:stratum_indices]
    )
    north_salt = jnp.where(
        is_top,
        mirror_pack[stratum_indices : 2 * stratum_indices],
        from_north[stratum_indices : 2 * stratum_indices],
    )
    north_diff = jnp.where(
        is_top, mirror_pack[3 * stratum_indices], from_north[2 * stratum_indices]
    )
    north_wet = jnp.where(
        is_top, mirror_pack[3 * stratum_indices + 1], from_north[2 * stratum_indices + 1]
    )
    top_speed = jnp.where(
        is_top,
        0.5
        * (poleward_transit_number[:, -1] - mirror_pack[2 * stratum_indices : 3 * stratum_indices]),
        poleward_transit_number[:, -1],
    )
    temp_ext = extend(
        heat_anomaly,
        south_neighbour_cells[:stratum_indices],
        upper_boundary_heat,
        west_neighbour_cells[:stratum_indices],
        east_neighbour_cells[:stratum_indices],
    )
    salt_ext = extend(
        saltiness_anomaly,
        south_neighbour_cells[stratum_indices : 2 * stratum_indices],
        north_salt,
        west_neighbour_cells[stratum_indices : 2 * stratum_indices],
        east_neighbour_cells[stratum_indices : 2 * stratum_indices],
    )
    diff_ext = extend(
        neutral_mixing_number,
        south_neighbour_cells[3 * stratum_indices],
        north_diff,
        west_neighbour_cells[3 * stratum_indices],
        east_neighbour_cells[2 * stratum_indices],
    )
    wet_ext = extend(
        ocean_share,
        south_neighbour_cells[3 * stratum_indices + 1],
        north_wet,
        west_neighbour_cells[3 * stratum_indices + 1],
        east_neighbour_cells[2 * stratum_indices + 1],
    )
    cells_ext = volume_scalar_carry(
        temp_ext, salt_ext, wet_ext, diff_ext, stratum_height_entry(stratum_indices)
    )
    speed_x = jnp.concatenate(
        [
            west_neighbour_cells[2 * stratum_indices : 3 * stratum_indices][:, :, None],
            eastward_transit_number,
        ],
        2,
    )
    speed_y = jnp.concatenate(
        [
            south_neighbour_cells[2 * stratum_indices : 3 * stratum_indices][:, None, :],
            poleward_transit_number[:, :-1],
            top_speed[:, None, :],
        ],
        1,
    )
    heat_transport_along_x, flux_x_s = face_flux(
        speed_x,
        tuple((member[..., 1:-1, :-1] for member in cells_ext)),
        tuple((member[..., 1:-1, 1:] for member in cells_ext)),
    )
    heat_transport_along_y, flux_y_s = face_flux(
        speed_y,
        tuple((member[..., :-1, 1:-1] for member in cells_ext)),
        tuple((member[..., 1:, 1:-1] for member in cells_ext)),
    )
    eastern_heat_entry = heat_transport_along_x[..., 1:] - heat_transport_along_x[..., :-1]
    eastern_saltiness = flux_x_s[..., 1:] - flux_x_s[..., :-1]
    upper_heat_entry = heat_transport_along_y[:, 1:] - heat_transport_along_y[:, :-1]
    upper_saltiness = flux_y_s[:, 1:] - flux_y_s[:, :-1]
    ocean_volume_flags = cells_ext[2][:, 1:-1, 1:-1]
    revised_heat_anomaly, revised_saltiness = march_scalar_fields(
        heat_anomaly,
        saltiness_anomaly,
        eastern_heat_entry,
        eastern_saltiness,
        upper_heat_entry,
        upper_saltiness,
        rising_transit_number,
        stacked_mixing_number,
        ocean_volume_flags,
    )
    return (revised_heat_anomaly, revised_saltiness)


def solution(mesh):
    return jax.shard_map(
        local,
        mesh=mesh,
        in_specs=(
            P(None, "gy", "gx"),
            P(None, "gy", "gx"),
            P(None, "gy", "gx"),
            P(None, "gy", "gx"),
            P(None, "gy", "gx"),
            P(None, "gy", "gx"),
            P("gy", "gx"),
            P("gy", "gx"),
        ),
        out_specs=(P(None, "gy", "gx"), P(None, "gy", "gx")),
        check_vma=False,
    )
```

profile of v0, /device:TPU:480, one launch (start us, length us, event | category | flops | bytes accessed | tf_op | source)
XLA Modules:
  0.0 124.8 jit_solution(5847260927948505809)
XLA Ops:
  0.6 0.8 copy.126
  1.6 1.2 fusion.335
  2.9 1.1 fusion.336
  4.1 1.0 slice.1294
  5.2 0.8 fusion.341
  6.3 2.9 %collective-permute-start.3 = (f32[227,128]{0,1:T(8,128)S(1)}, f32[227,128]{0,1:T(8,128)S(1)}, u32[]{:S(2)}, u32[]{:S(2)}) collective-permute-start(f32[227,128]{0,1:T(8,128)S(1)} %concatenate.118), channel_id=1, source_target_pairs={{0,1},{1,0},{2,3},{3,2},{4,5},{5,4},{6,7},{7,6},{8,9},{9,8},{10,11... | collective-permute-start | bytes 348680 | tf_op jit(solution)/shard_map/ppermute | solution.py:31
  9.2 1.9 %collective-permute-start = (f32[227,128]{0,1:T(8,128)S(1)}, f32[227,128]{0,1:T(8,128)S(1)}, u32[]{:S(2)}, u32[]{:S(2)}) collective-permute-start(f32[227,128]{0,1:T(8,128)S(1)} %concatenate.118), channel_id=1, source_target_pairs={{0,32},{32,64},{64,96},{96,128},{128,160},{160,192},{192,224},{224... | collective-permute-start | bytes 348680 | tf_op jit(solution)/shard_map/ppermute | solution.py:21
  11.4 0.8 pad_maximum_fusion.20
  12.2 14.5 %collective-permute-start.8 = (f32[152,128]{0,1:T(8,128)}, f32[152,128]{0,1:T(8,128)S(1)}, u32[]{:S(2)}, u32[]{:S(2)}) collective-permute-start(f32[152,128]{0,1:T(8,128)} %pad_maximum_fusion.20), channel_id=1, source_target_pairs={{32,0},{64,32},{96,64},{128,96},{160,128},{192,160},{224,192},{256... | collective-permute-start | bytes 233480 | tf_op jit(solution)/shard_map/ppermute | solution.py:21
  28.3 7.8 %collective-permute-start.1 = (f32[227,8]{0,1:T(8,128)S(1)}, f32[227,8]{0,1:T(8,128)S(1)}, u32[]{:S(2)}, u32[]{:S(2)}) collective-permute-start(f32[227,8]{0,1:T(8,128)S(1)} %concatenate.119), channel_id=1, source_target_pairs={{0,1},{1,2},{2,3},{3,4},{4,5},{5,6},{6,7},{7,8},{8,9},{9,10},{10,1... | collective-permute-start | bytes 21800 | tf_op jit(solution)/shard_map/ppermute | solution.py:27
  36.7 1.9 %collective-permute-start.2 = (f32[152,8]{0,1:T(8,128)S(1)}, f32[152,8]{0,1:T(8,128)S(1)}, u32[]{:S(2)}, u32[]{:S(2)}) collective-permute-start(f32[152,8]{0,1:T(8,128)S(1)} %pad_maximum_fusion.28), channel_id=1, source_target_pairs={{0,31},{1,0},{2,1},{3,2},{4,3},{5,4},{6,5},{7,6},{8,7},{9,8},{10,9... | collective-permute-start | bytes 14600 | tf_op jit(solution)/shard_map/ppermute | solution.py:27
  39.8 10.0 %collective-permute-done.2 = f32[152,8]{0,1:T(8,128)S(1)} collective-permute-done((f32[152,8]{0,1:T(8,128)S(1)}, f32[152,8]{0,1:T(8,128)S(1)}, u32[]{:S(2)}, u32[]{:S(2)}) %collective-permute-start.2) | collective-permute-done | bytes 4896 | tf_op jit(solution)/shard_map/ppermute | solution.py:27
  50.2 0.9 copy.145
  51.1 1.9 %collective-permute-start.4 = (f32[227,128]{0,1:T(8,128)S(1)}, f32[227,128]{0,1:T(8,128)S(1)}, u32[]{:S(2)}, u32[]{:S(2)}) collective-permute-start(f32[227,128]{0,1:T(8,128)S(1)} %collective-permute-done.3), channel_id=1, source_target_pairs={{0,2},{1,3},{2,0},{3,1},{4,6},{5,7},{6,4},{7,5},{8,10},{9,11},{10,... | collective-permute-start | bytes 348680 | tf_op jit(solution)/shard_map/ppermute | solution.py:31
  53.1 5.7 %collective-permute-done.4 = f32[227,128]{0,1:T(8,128)S(1)} collective-permute-done((f32[227,128]{0,1:T(8,128)S(1)}, f32[227,128]{0,1:T(8,128)S(1)}, u32[]{:S(2)}, u32[]{:S(2)}) %collective-permute-start.4) | collective-permute-done | bytes 116256 | tf_op jit(solution)/shard_map/ppermute | solution.py:31
  58.9 1.9 %collective-permute-start.5 = (f32[227,128]{0,1:T(8,128)S(1)}, f32[227,128]{0,1:T(8,128)S(1)}, u32[]{:S(2)}, u32[]{:S(2)}) collective-permute-start(f32[227,128]{0,1:T(8,128)S(1)} %collective-permute-done.4), channel_id=1, source_target_pairs={{0,4},{1,5},{2,6},{3,7},{4,0},{5,1},{6,2},{7,3},{8,12},{9,13},{10,... | collective-permute-start | bytes 348680 | tf_op jit(solution)/shard_map/ppermute | solution.py:31
  61.1 0.9 copy.144
  62.0 0.9 copy.143
  62.9 0.7 fusion.49
  63.6 6.9 %collective-permute-done.5 = f32[227,128]{0,1:T(8,128)S(1)} collective-permute-done((f32[227,128]{0,1:T(8,128)S(1)}, f32[227,128]{0,1:T(8,128)S(1)}, u32[]{:S(2)}, u32[]{:S(2)}) %collective-permute-start.5) | collective-permute-done | bytes 116256 | tf_op jit(solution)/shard_map/ppermute | solution.py:31
  70.5 3.5 %collective-permute-start.6 = (f32[227,128]{0,1:T(8,128)S(1)}, f32[227,128]{0,1:T(8,128)S(1)}, u32[]{:S(2)}, u32[]{:S(2)}) collective-permute-start(f32[227,128]{0,1:T(8,128)S(1)} %collective-permute-done.5), channel_id=1, source_target_pairs={{0,8},{1,9},{2,10},{3,11},{4,12},{5,13},{6,14},{7,15},{8,0},{9,1},... | collective-permute-start | bytes 348680 | tf_op jit(solution)/shard_map/ppermute | solution.py:31
  74.1 3.2 %collective-permute-done.6 = f32[227,128]{0,1:T(8,128)S(1)} collective-permute-done((f32[227,128]{0,1:T(8,128)S(1)}, f32[227,128]{0,1:T(8,128)S(1)}, u32[]{:S(2)}, u32[]{:S(2)}) %collective-permute-start.6) | collective-permute-done | bytes 116256 | tf_op jit(solution)/shard_map/ppermute | solution.py:31
  77.3 4.8 %collective-permute-start.7 = (f32[227,128]{0,1:T(8,128)S(1)}, f32[227,128]{0,1:T(8,128)S(1)}, u32[]{:S(2)}, u32[]{:S(2)}) collective-permute-start(f32[227,128]{0,1:T(8,128)S(1)} %collective-permute-done.6), channel_id=1, source_target_pairs={{0,16},{1,17},{2,18},{3,19},{4,20},{5,21},{6,22},{7,23},{8,24},{9,... | collective-permute-start | bytes 348680 | tf_op jit(solution)/shard_map/ppermute | solution.py:31
  82.3 0.7 copy.150
  83.3 0.7 pad.44
  83.9 0.7 copy.156
  84.6 1.0 collective-permute-done.7
  85.8 0.7 fusion.45
  86.8 2.1 %add_multiply_fusion.3 = (f32[74,8,128]{2,1,0:T(8,128)}, f32[74,8,128]{2,1,0:T(8,128)}, f32[74,8,128]{2,1,0:T(8,128)S(1)}) fusion(f32[75,8,128]{2,1,0:T(8,128)S(1)} %copy-done, f32[75,8,128]{2,1,0:T(8,128)S(1)} %copy-done.28, f32[75,10,130]{2,1,0:T(8,128)S(1)} %fusion, f32[75,8,128]{2,1,0:T(8,128)S(1)} %copy-done.1, f32[75,8,128]{2,1,0:T(8,128)} %param.13), kind=kLoop, calls=%fused_computation.238 | loop fusion | flops 985088 | bytes 3334144 | tf_op jit(solution)/shard_map/mul | solution.py:163
  88.9 0.7 slice_divide_fusion.29
  89.7 1.3 %bitcast_divide_fusion.9 = (f32[8,128]{1,0:T(8,128)}, f32[8,128]{1,0:T(8,128)}, f32[8,128]{1,0:T(8,128)S(1)}, f32[8,128]{1,0:T(8,128)}, f32[8,128]{1,0:T(8,128)}...) fusion(f32[74,8,128]{2,1,0:T(8,128)S(1)} %get-tuple-element.407, ...), kind=kLoop, calls=%fused_computation.515 | loop fusion | flops 200704 | bytes 872448 | tf_op jit(solution)/shard_map/eval_jaxpr/div | solution.py:108
  90.9 0.7 fusion.338
  91.9 0.7 copy.151
  93.7 3.0 %pad_maximum_fusion = (f32[75,10,130]{2,1,0:T(8,128)S(1)}, f32[75,10,130]{2,1,0:T(8,128)S(1)}) fusion(f32[75,1,130]{2,1,0:T(1,128)S(1)} %copy-done.23, f32[75,8,1]{2,1,0:T(8,128)S(1)} %copy-done.9, f32[75,8,128]{2,1,0:T(8,128)S(1)} %copy-done.1, f32[75,8,1]{2,1,0:T(8,128)S(1)} %copy-done.11, f32[75,1,130]{2,1,0:T(1,128)S(1)} %copy-done.21, ...), kind=kLoop, calls=%fused_computation | loop fusion | flops 2145000 | bytes 1560600 | tf_op jit(solution)/shard_map/concatenate | solution.py:192
  97.4 1.2 add_multiply_fusion
  98.6 1.2 add_multiply_fusion.2
  99.8 1.2 add_multiply_fusion.1
  101.7 1.5 %slice.1352 = f32[75,128]{0,1:T(8,128)} reverse(f32[75,128]{0,1:T(8,128)} %get-tuple-element.427), dimensions={1} | reverse | bytes 76800 | tf_op jit(solution)/shard_map/slice | solution.py:266
  103.1 1.5 %select_bitcast_fusion = f32[75,1,128]{0,2,1:T(8,128)} fusion(f32[75,128]{0,1:T(8,128)} %slice.1352, pred[]{:T(512)S(6)} %eq.3, f32[75,1,128]{0,2,1:T(8,128)} %copy-done.25), kind=kLoop, calls=%fused_computation.256 | loop fusion | flops 28800 | bytes 115201 | tf_op jit(solution)/shard_map/broadcast_in_dim | solution.py:311
  104.6 1.5 %copy.157 = f32[75,1,128]{2,1,0:T(1,128)} copy(f32[75,1,128]{0,2,1:T(8,128)} %select_bitcast_fusion) | data formatting | bytes 76800 | tf_op jit(solution)/shard_map/broadcast_in_dim | solution.py:311
  106.2 4.0 %fusion.16 = (f32[75,8,129]{2,1,0:T(8,128)S(1)}, f32[75,8,129]{2,1,0:T(8,128)S(1)}) fusion(f32[75,10,130]{2,1,0:T(8,128)} %add_multiply_fusion, f32[75,8,1]{2,1,0:T(8,128)} %copy-done.5, f32[75,8,128]{2,1,0:T(8,128)S(1)} %copy-done, f32[75,8,1]{2,1,0:T(8,128)} %copy-done.7, f32[75,8,128]{2,1,0:T(8,128)} %param.10, f32[75,8,1]{2,1,0:T(8,128)} %copy.143, ...), kind=kLoop, calls=%fused_computation.34 | loop fusion | flops 1857600 | bytes 3721728 | tf_op jit(solution)/shard_map/mul | solution.py:88
  110.4 0.8 fusion.32
  112.2 1.8 %fusion.11 = (f32[75,9,128]{2,1,0:T(8,128)S(1)}, f32[75,9,128]{2,1,0:T(8,128)S(1)}) fusion(f32[75,10,130]{2,1,0:T(8,128)S(1)} %copy-done.2, f32[75,1,130]{2,1,0:T(1,128)S(1)} %copy.155, f32[75,8,1]{2,1,0:T(8,128)S(1)} %copy-done.6, f32[75,8,128]{2,1,0:T(8,128)S(1)} %copy-done, f32[75,8,1]{2,1,0:T(8,128)S(1)} %copy-done.8, f32[75,1,130]{2,1,0:T(1,128)S(1)} %copy.154, ...), kind=kLoop, calls=%fused_computation.22 | loop fusion | flops 2505600 | bytes 4196208 | tf_op jit(solution)/shard_map/mul | solution.py:88
  114.1 1.2 fusion.21
  116.6 1.4 %fusion.65 = (f32[8,128]{1,0:T(8,128)S(1)}, f32[8,128]{1,0:T(8,128)S(1)}, f32[8,128]{1,0:T(8,128)S(1)}, f32[8,128]{1,0:T(8,128)S(1)}, f32[8,128]{1,0:T(8,128)S(1...) fusion(f32[75,8,128]{2,1,0:T(8,128)S(1)} %get-tuple-element.520, ...), kind=kLoop, calls=%fused_computation.308 | loop fusion | flops 245760 | bytes 1167360 | tf_op jit(solution)/shard_map/eval_jaxpr/div | solution.py:110
  118.2 1.3 %fusion.140 = (f32[8,128]{1,0:T(8,128)S(1)}, f32[8,128]{1,0:T(8,128)S(1)}, f32[8,128]{1,0:T(8,128)S(1)}, f32[8,128]{1,0:T(8,128)S(1)}, f32[8,128]{1,0:T(8,128)S(...) fusion(f32[8,128]{1,0:T(8,128)S(1)} %get-tuple-element.178, ...), kind=kLoop, calls=%fused_computation.469 | loop fusion | flops 225280 | bytes 1122304 | tf_op jit(solution)/shard_map/eval_jaxpr/div | solution.py:109
  123.4 0.7 copy-done.106
  124.1 0.7 copy-done.107
  (391 shorter events, 13.1 us)
Async XLA Ops:
  0.6 26.1 %copy-start.1 = (f32[75,8,128]{2,1,0:T(8,128)S(1)}, f32[75,8,128]{2,1,0:T(8,128)}, u32[]{:S(2)}) copy-start(f32[75,8,128]{2,1,0:T(8,128)} %param.8) | copy-start | bytes 921604
  5.2 21.7 %copy-start = (f32[75,8,128]{2,1,0:T(8,128)S(1)}, f32[75,8,128]{2,1,0:T(8,128)}, u32[]{:S(2)}) copy-start(f32[75,8,128]{2,1,0:T(8,128)} %param.9) | copy-start | bytes 921604
  6.3 44.8 %collective-permute-start.3 = (f32[227,128]{0,1:T(8,128)S(1)}, f32[227,128]{0,1:T(8,128)S(1)}, u32[]{:S(2)}, u32[]{:S(2)}) collective-permute-start(f32[227,128]{0,1:T(8,128)S(1)} %concatenate.118), channel_id=1, source_target_pairs={{0,1},{1,0},{2,3},{3,2},{4,5},{5,4},{6,7},{7,6},{8,9},{9,8},{10,11... | collective-permute-start | bytes 348680 | tf_op jit(solution)/shard_map/ppermute | solution.py:31
  9.2 64.8 %collective-permute-start = (f32[227,128]{0,1:T(8,128)S(1)}, f32[227,128]{0,1:T(8,128)S(1)}, u32[]{:S(2)}, u32[]{:S(2)}) collective-permute-start(f32[227,128]{0,1:T(8,128)S(1)} %concatenate.118), channel_id=1, source_target_pairs={{0,32},{32,64},{64,96},{96,128},{128,160},{160,192},{192,224},{224... | collective-permute-start | bytes 348680 | tf_op jit(solution)/shard_map/ppermute | solution.py:21
  12.2 73.6 %collective-permute-start.8 = (f32[152,128]{0,1:T(8,128)}, f32[152,128]{0,1:T(8,128)S(1)}, u32[]{:S(2)}, u32[]{:S(2)}) collective-permute-start(f32[152,128]{0,1:T(8,128)} %pad_maximum_fusion.20), channel_id=1, source_target_pairs={{32,0},{64,32},{96,64},{128,96},{160,128},{192,160},{224,192},{256... | collective-permute-start | bytes 233480 | tf_op jit(solution)/shard_map/ppermute | solution.py:21
  28.3 24.7 %collective-permute-start.1 = (f32[227,8]{0,1:T(8,128)S(1)}, f32[227,8]{0,1:T(8,128)S(1)}, u32[]{:S(2)}, u32[]{:S(2)}) collective-permute-start(f32[227,8]{0,1:T(8,128)S(1)} %concatenate.119), channel_id=1, source_target_pairs={{0,1},{1,2},{2,3},{3,4},{4,5},{5,6},{6,7},{7,8},{8,9},{9,10},{10,1... | collective-permute-start | bytes 21800 | tf_op jit(solution)/shard_map/ppermute | solution.py:27
  36.7 13.1 %collective-permute-start.2 = (f32[152,8]{0,1:T(8,128)S(1)}, f32[152,8]{0,1:T(8,128)S(1)}, u32[]{:S(2)}, u32[]{:S(2)}) collective-permute-start(f32[152,8]{0,1:T(8,128)S(1)} %pad_maximum_fusion.28), channel_id=1, source_target_pairs={{0,31},{1,0},{2,1},{3,2},{4,3},{5,4},{6,5},{7,6},{8,7},{9,8},{10,9... | collective-permute-start | bytes 14600 | tf_op jit(solution)/shard_map/ppermute | solution.py:27
  50.0 24.0 %copy-start.97 = (f32[8,1]{1,0:T(8,128)}, f32[8,1]{1,0:T(8,128)S(1)}, u32[]{:S(2)}) copy-start(f32[8,1]{1,0:T(8,128)S(1)} %get-tuple-element.442) | copy-start | bytes 100
  50.2 42.5 %copy-start.5 = (f32[75,8,1]{2,1,0:T(8,128)}, f32[75,8,1]{2,1,0:T(8,128)S(1)}, u32[]{:S(2)}) copy-start(f32[75,8,1]{2,1,0:T(8,128)S(1)} %copy.153) | copy-start | bytes 7204
  51.1 7.7 %collective-permute-start.4 = (f32[227,128]{0,1:T(8,128)S(1)}, f32[227,128]{0,1:T(8,128)S(1)}, u32[]{:S(2)}, u32[]{:S(2)}) collective-permute-start(f32[227,128]{0,1:T(8,128)S(1)} %collective-permute-done.3), channel_id=1, source_target_pairs={{0,2},{1,3},{2,0},{3,1},{4,6},{5,7},{6,4},{7,5},{8,10},{9,11},{10,... | collective-permute-start | bytes 348680 | tf_op jit(solution)/shard_map/ppermute | solution.py:31
  58.9 11.6 %collective-permute-start.5 = (f32[227,128]{0,1:T(8,128)S(1)}, f32[227,128]{0,1:T(8,128)S(1)}, u32[]{:S(2)}, u32[]{:S(2)}) collective-permute-start(f32[227,128]{0,1:T(8,128)S(1)} %collective-permute-done.4), channel_id=1, source_target_pairs={{0,4},{1,5},{2,6},{3,7},{4,0},{5,1},{6,2},{7,3},{8,12},{9,13},{10,... | collective-permute-start | bytes 348680 | tf_op jit(solution)/shard_map/ppermute | solution.py:31
  60.8 13.1 %copy-start.99 = (f32[8,1]{1,0:T(8,128)}, f32[8,1]{1,0:T(8,128)S(1)}, u32[]{:S(2)}) copy-start(f32[8,1]{1,0:T(8,128)S(1)} %get-tuple-element.440) | copy-start | bytes 100
  61.1 31.6 %copy-start.7 = (f32[75,8,1]{2,1,0:T(8,128)}, f32[75,8,1]{2,1,0:T(8,128)S(1)}, u32[]{:S(2)}) copy-start(f32[75,8,1]{2,1,0:T(8,128)S(1)} %copy.152) | copy-start | bytes 7204
  70.5 6.8 %collective-permute-start.6 = (f32[227,128]{0,1:T(8,128)S(1)}, f32[227,128]{0,1:T(8,128)S(1)}, u32[]{:S(2)}, u32[]{:S(2)}) collective-permute-start(f32[227,128]{0,1:T(8,128)S(1)} %collective-permute-done.5), channel_id=1, source_target_pairs={{0,8},{1,9},{2,10},{3,11},{4,12},{5,13},{6,14},{7,15},{8,0},{9,1},... | collective-permute-start | bytes 348680 | tf_op jit(solution)/shard_map/ppermute | solution.py:31
  77.3 8.4 %collective-permute-start.7 = (f32[227,128]{0,1:T(8,128)S(1)}, f32[227,128]{0,1:T(8,128)S(1)}, u32[]{:S(2)}, u32[]{:S(2)}) collective-permute-start(f32[227,128]{0,1:T(8,128)S(1)} %collective-permute-done.6), channel_id=1, source_target_pairs={{0,16},{1,17},{2,18},{3,19},{4,20},{5,21},{6,22},{7,23},{8,24},{9,... | collective-permute-start | bytes 348680 | tf_op jit(solution)/shard_map/ppermute | solution.py:31
  82.3 4.5 %copy-start.28 = (f32[75,8,128]{2,1,0:T(8,128)S(1)}, f32[75,8,128]{2,1,0:T(8,128)}, u32[]{:S(2)}) copy-start(f32[75,8,128]{2,1,0:T(8,128)} %param.12) | copy-start | bytes 921604
  106.2 4.1 %copy-start.4 = (f32[75,10,130]{2,1,0:T(8,128)S(1)}, f32[75,10,130]{2,1,0:T(8,128)}, u32[]{:S(2)}) copy-start(f32[75,10,130]{2,1,0:T(8,128)} %add_multiply_fusion.1) | copy-start | bytes 1170004
  106.2 4.1 %copy-start.10 = (f32[75,8,1]{2,1,0:T(8,128)S(1)}, f32[75,8,1]{2,1,0:T(8,128)}, u32[]{:S(2)}) copy-start(f32[75,8,1]{2,1,0:T(8,128)} %copy.145) | copy-start | bytes 7204
  106.2 4.1 %copy-start.12 = (f32[75,8,1]{2,1,0:T(8,128)S(1)}, f32[75,8,1]{2,1,0:T(8,128)}, u32[]{:S(2)}) copy-start(f32[75,8,1]{2,1,0:T(8,128)} %copy.144) | copy-start | bytes 7204
  106.2 4.1 %copy-start.16 = (f32[75,8,128]{2,1,0:T(8,128)S(1)}, f32[75,8,128]{2,1,0:T(8,128)}, u32[]{:S(2)}) copy-start(f32[75,8,128]{2,1,0:T(8,128)} %param.10) | copy-start | bytes 921604
  106.2 4.1 %copy-start.17 = (f32[75,8,1]{2,1,0:T(8,128)S(1)}, f32[75,8,1]{2,1,0:T(8,128)}, u32[]{:S(2)}) copy-start(f32[75,8,1]{2,1,0:T(8,128)} %copy.143) | copy-start | bytes 7204
  106.2 4.1 %copy-start.74 = (f32[8,129]{1,0:T(8,128)S(1)}, f32[8,129]{1,0:T(8,128)}, u32[]{:S(2)}) copy-start(f32[8,129]{1,0:T(8,128)} %fusion.49) | copy-start | bytes 12388
  110.3 1.7 %copy-start.3 = (f32[75,10,130]{2,1,0:T(8,128)S(1)}, f32[75,10,130]{2,1,0:T(8,128)}, u32[]{:S(2)}) copy-start(f32[75,10,130]{2,1,0:T(8,128)} %add_multiply_fusion.2) | copy-start | bytes 1170004
  110.4 1.7 %copy-start.6 = (f32[75,8,1]{2,1,0:T(8,128)S(1)}, f32[75,8,1]{2,1,0:T(8,128)}, u32[]{:S(2)}) copy-start(f32[75,8,1]{2,1,0:T(8,128)} %copy-done.5) | copy-start | bytes 7204
  110.4 1.8 %copy-start.8 = (f32[75,8,1]{2,1,0:T(8,128)S(1)}, f32[75,8,1]{2,1,0:T(8,128)}, u32[]{:S(2)}) copy-start(f32[75,8,1]{2,1,0:T(8,128)} %copy-done.7) | copy-start | bytes 7204
  110.4 1.9 %copy-start.18 = (f32[75,8,128]{2,1,0:T(8,128)S(1)}, f32[75,8,128]{2,1,0:T(8,128)}, u32[]{:S(2)}) copy-start(f32[75,8,128]{2,1,0:T(8,128)} %param.11) | copy-start | bytes 921604
  110.4 1.8 %copy-start.26 = (f32[75,1,128]{2,1,0:T(1,128)S(1)}, f32[75,1,128]{2,1,0:T(1,128)}, u32[]{:S(2)}) copy-start(f32[75,1,128]{2,1,0:T(1,128)} %copy.156) | copy-start | bytes 115204
  110.4 1.8 %copy-start.27 = (f32[75,1,128]{2,1,0:T(1,128)S(1)}, f32[75,1,128]{2,1,0:T(1,128)}, u32[]{:S(2)}) copy-start(f32[75,1,128]{2,1,0:T(1,128)} %copy.157) | copy-start | bytes 115204
  112.2 1.8 %copy-start.22 = (f32[75,1,130]{2,1,0:T(1,128)S(1)}, f32[75,1,130]{2,1,0:T(1,128)}, u32[]{:S(2)}) copy-start(f32[75,1,130]{2,1,0:T(1,128)} %copy.150) | copy-start | bytes 117004
  112.2 1.8 %copy-start.24 = (f32[75,1,130]{2,1,0:T(1,128)S(1)}, f32[75,1,130]{2,1,0:T(1,128)}, u32[]{:S(2)}) copy-start(f32[75,1,130]{2,1,0:T(1,128)} %copy.151) | copy-start | bytes 117004
  116.0 2.2 %copy-start.66 = (f32[8,128]{1,0:T(8,128)S(1)}, f32[8,128]{1,0:T(8,128)}, u32[]{:S(2)}) copy-start(f32[8,128]{1,0:T(8,128)} %get-tuple-element.392) | copy-start | bytes 12292
  116.0 2.2 %copy-start.67 = (f32[8,128]{1,0:T(8,128)S(1)}, f32[8,128]{1,0:T(8,128)}, u32[]{:S(2)}) copy-start(f32[8,128]{1,0:T(8,128)} %get-tuple-element.395) | copy-start | bytes 12292
  118.0 1.6 %copy-start.68 = (f32[8,128]{1,0:T(8,128)S(1)}, f32[8,128]{1,0:T(8,128)}, u32[]{:S(2)}) copy-start(f32[8,128]{1,0:T(8,128)} %get-tuple-element.398) | copy-start | bytes 12292
  118.0 1.6 %copy-start.69 = (f32[8,128]{1,0:T(8,128)S(1)}, f32[8,128]{1,0:T(8,128)}, u32[]{:S(2)}) copy-start(f32[8,128]{1,0:T(8,128)} %get-tuple-element.401) | copy-start | bytes 12292
  118.0 1.6 %copy-start.70 = (f32[8,128]{1,0:T(8,128)S(1)}, f32[8,128]{1,0:T(8,128)}, u32[]{:S(2)}) copy-start(f32[8,128]{1,0:T(8,128)} %get-tuple-element.404) | copy-start | bytes 12292
  118.0 1.6 %copy-start.71 = (f32[8,128]{1,0:T(8,128)S(1)}, f32[8,128]{1,0:T(8,128)}, u32[]{:S(2)}) copy-start(f32[8,128]{1,0:T(8,128)} %get-tuple-element.324) | copy-start | bytes 12292
  118.0 1.6 %copy-start.75 = (f32[8,128]{1,0:T(8,128)S(1)}, f32[8,128]{1,0:T(8,128)}, u32[]{:S(2)}) copy-start(f32[8,128]{1,0:T(8,128)} %get-tuple-element.327) | copy-start | bytes 12292
  118.0 1.6 %copy-start.76 = (f32[8,128]{1,0:T(8,128)S(1)}, f32[8,128]{1,0:T(8,128)}, u32[]{:S(2)}) copy-start(f32[8,128]{1,0:T(8,128)} %get-tuple-element.330) | copy-start | bytes 12292
  118.0 1.6 %copy-start.77 = (f32[8,128]{1,0:T(8,128)S(1)}, f32[8,128]{1,0:T(8,128)}, u32[]{:S(2)}) copy-start(f32[8,128]{1,0:T(8,128)} %get-tuple-element.333) | copy-start | bytes 12292
  118.1 1.6 %copy-start.78 = (f32[8,128]{1,0:T(8,128)S(1)}, f32[8,128]{1,0:T(8,128)}, u32[]{:S(2)}) copy-start(f32[8,128]{1,0:T(8,128)} %get-tuple-element.336) | copy-start | bytes 12292
  118.1 1.6 %copy-start.79 = (f32[8,128]{1,0:T(8,128)S(1)}, f32[8,128]{1,0:T(8,128)}, u32[]{:S(2)}) copy-start(f32[8,128]{1,0:T(8,128)} %get-tuple-element.339) | copy-start | bytes 12292
  118.1 1.6 %copy-start.80 = (f32[8,128]{1,0:T(8,128)S(1)}, f32[8,128]{1,0:T(8,128)}, u32[]{:S(2)}) copy-start(f32[8,128]{1,0:T(8,128)} %get-tuple-element.342) | copy-start | bytes 12292
  118.1 1.6 %copy-start.81 = (f32[8,128]{1,0:T(8,128)S(1)}, f32[8,128]{1,0:T(8,128)}, u32[]{:S(2)}) copy-start(f32[8,128]{1,0:T(8,128)} %get-tuple-element.345) | copy-start | bytes 12292
  118.1 1.6 %copy-start.82 = (f32[8,128]{1,0:T(8,128)S(1)}, f32[8,128]{1,0:T(8,128)}, u32[]{:S(2)}) copy-start(f32[8,128]{1,0:T(8,128)} %get-tuple-element.348) | copy-start | bytes 12292
  118.1 1.6 %copy-start.83 = (f32[8,128]{1,0:T(8,128)S(1)}, f32[8,128]{1,0:T(8,128)}, u32[]{:S(2)}) copy-start(f32[8,128]{1,0:T(8,128)} %get-tuple-element.351) | copy-start | bytes 12292
  118.1 1.6 %copy-start.84 = (f32[8,128]{1,0:T(8,128)S(1)}, f32[8,128]{1,0:T(8,128)}, u32[]{:S(2)}) copy-start(f32[8,128]{1,0:T(8,128)} %get-tuple-element.354) | copy-start | bytes 12292
  118.1 1.6 %copy-start.85 = (f32[8,128]{1,0:T(8,128)S(1)}, f32[8,128]{1,0:T(8,128)}, u32[]{:S(2)}) copy-start(f32[8,128]{1,0:T(8,128)} %get-tuple-element.357) | copy-start | bytes 12292
  118.1 1.6 %copy-start.87 = (f32[8,128]{1,0:T(8,128)S(1)}, f32[8,128]{1,0:T(8,128)}, u32[]{:S(2)}) copy-start(f32[8,128]{1,0:T(8,128)} %get-tuple-element.390) | copy-start | bytes 12292
  (69 other events, 69.2 us)
where the time goes:
time: 126 us; the launch traced here: 125 us
  starting transfers between devices  41.2 us (33%)
  other arithmetic  30.6 us (24%)
  waiting for transfers between devices  26.9 us (21%)
  local copies, waits for them, and re-layouts  23 us (18%)
  between operations  3.21 us (3%)
    ppermute x5, waiting for transfers between devices, swapped(): lax.ppermute(x, axis, [(i, i ^ 1 << bit) for i in range(lax.axis_size(axi...  16.9 us
    ppermute x2, starting transfers between devices, shifted(): lax.ppermute(value, axis, [(source, source + steps) for source in range(l...  16.4 us
    ppermute x5, starting transfers between devices, swapped(): lax.ppermute(x, axis, [(i, i ^ 1 << bit) for i in range(lax.axis_size(axi...  15 us
    ppermute x2, waiting for transfers between devices, passed_along(): return lax.ppermute(value, axis, pairs)  9.97 us
    ppermute x2, starting transfers between devices, passed_along(): return lax.ppermute(value, axis, pairs)  9.75 us
    unnamed x299, local copies, waits for them, and re-layouts  6.18 us
    mul x2, other arithmetic, face_flux(): face_wet * (forward * left_cell[1] + backward * right_cell[1] - face_diff...  5.82 us
    concatenate x3, other arithmetic, extend(): return jnp.concatenate([south_pad, middle, north_pad], -2)  3.69 us
  transfers between devices with their start and end apart: 9, of which 5 were waited for; matrix products, arithmetic and copies ran while one was open for 9% of the time, Pallas kernels for 0%

commit v1 on v0

v1 whole, which is shorter than its diff:
```python
import functools

import jax
import jax.numpy as jnp
from jax import lax
from jax.experimental import pallas as pl
from jax.experimental.pallas import tpu as pltpu
from jax.sharding import PartitionSpec as P

thermal_coef = 0.1655
haline_coef = 0.76554
thermal_curve = 0.05952
haline_curve = 0.00054914
thermal_press = 0.0001497
haline_press = 1.109e-05
cabbeling = 0.0024341
bottom_depth = 5800.0
slope_limit = 1.0
strat_offset = 0.1

ROWS = 8
LANES = 128
GRID_AXES = ("gy", "gx")


def padded(levels):
    return -(-(levels + 2) // 8) * 8


def density(temper, saline, strata_height):
    heat_slope = -thermal_coef * (1.0 + thermal_press * strata_height)
    salt_slope = haline_coef * (1.0 - haline_press * strata_height)
    return (
        heat_slope - (0.5 * thermal_coef * thermal_curve) * temper - cabbeling * saline
    ) * temper + (salt_slope - (0.5 * haline_coef * haline_curve) * saline) * saline


def face_flux(speed, half_diffus, wet, left, right):
    denominator = jnp.maximum(0.25 * (left[5] + right[5]), 0.0) + strat_offset
    slope = jnp.clip((right[2] - left[2]) / denominator, -slope_limit, slope_limit)
    quarter = 0.25 * slope
    forward = speed > 0.0

    def one(i):
        carried = speed * jnp.where(forward, left[i], right[i])
        mixed = half_diffus * (right[i] - left[i] - quarter * (left[3 + i] + right[3 + i]))
        return jnp.where(wet, carried - mixed, 0.0)

    return one(0), one(1)


def pack_kernel(levels, t_ref, s_ref, u_ref, v_ref, diff_ref, depth_ref, a_ref, b_ref, xa_ref, xb_ref):
    block = padded(levels)
    gy, gx = lax.axis_index("gy"), lax.axis_index("gx")
    y_even, x_even = gy % 2 == 0, gx % 2 == 0
    is_top = gy == lax.axis_size("gy") - 1
    lane = lax.broadcasted_iota(jnp.int32, (block, LANES), 1)
    source = jnp.where(is_top, LANES - 1 - lane, lane)
    depth = depth_ref[...].astype(jnp.float32)
    diff = diff_ref[...]
    zero = jnp.zeros((block - levels - 2, LANES), jnp.float32)

    def rows(ref, r):
        return ref[pl.ds(r, levels, stride=ROWS), :]

    def part(ref, r, first):
        tail = [diff[r : r + 1], depth[r : r + 1], zero] if first else [jnp.zeros((block - levels, LANES), jnp.float32)]
        return jnp.concatenate([rows(ref, r)] + tail, 0)

    top = [part(t_ref, 7, True), part(s_ref, 7, False), part(v_ref, 7, False)]
    low = [part(t_ref, 0, True), part(s_ref, 0, False), jnp.zeros((block, LANES), jnp.float32)]
    for i in range(3):
        a_ref[i * block : (i + 1) * block] = jnp.where(y_even, top[i], low[i])
        b_ref[i * block : (i + 1) * block] = jnp.take_along_axis(
            jnp.where(y_even, low[i], top[i]), source, axis=1, mode="promise_in_bounds"
        )

    one_lane = lax.broadcasted_iota(jnp.int32, (ROWS, LANES), 1)

    def columns(ref, c, first):
        out = jnp.zeros((ROWS, LANES), jnp.float32)
        for k in range(levels):
            moved = pltpu.roll(ref[k * ROWS : (k + 1) * ROWS], (k - c) % LANES, 1)
            out = jnp.where(one_lane == k, moved, out)
        if first:
            out = jnp.where(one_lane == levels, pltpu.roll(diff, (levels - c) % LANES, 1), out)
            out = jnp.where(one_lane == levels + 1, pltpu.roll(depth, (levels + 1 - c) % LANES, 1), out)
        return out

    east = [columns(t_ref, 127, True), columns(s_ref, 127, False), columns(u_ref, 127, False)]
    west = [columns(t_ref, 0, True), columns(s_ref, 0, False), jnp.zeros((ROWS, LANES), jnp.float32)]
    for i in range(3):
        xa_ref[i * ROWS : (i + 1) * ROWS] = jnp.where(x_even, east[i], west[i])
        xb_ref[i * ROWS : (i + 1) * ROWS] = jnp.where(x_even, west[i], east[i])


def inner_kernel(
    levels, group, t_ref, s_ref, u_ref, v_ref, w_ref, kap_ref, diff_ref, depth_ref,
    star_t_ref, star_s_ref, inv_ref, low_ref, ratio_ref, own_ref,
):
    block = padded(levels)
    depth = depth_ref[...]
    diff = diff_ref[...]
    lane = lax.broadcasted_iota(jnp.int32, (ROWS, LANES), 1)
    row = lax.broadcasted_iota(jnp.int32, (ROWS, LANES), 0)

    def east(x):
        return pltpu.roll(x, LANES - 1, 1)

    def west(x):
        return pltpu.roll(x, 1, 1)

    def north(x):
        return pltpu.roll(x, ROWS - 1, 0)

    def south(x):
        return pltpu.roll(x, 1, 0)

    depth_x = jnp.where(lane == LANES - 1, 0, jnp.minimum(depth, east(depth)))
    depth_y = jnp.where(row == ROWS - 1, 0, jnp.minimum(depth, north(depth)))
    diff_x = 0.5 * (diff + east(diff))
    diff_y = 0.5 * (diff + north(diff))

    def at(ref, k):
        return ref[k]

    def height(k):
        part = (k.astype(jnp.float32) + 0.5) / levels
        return bottom_depth * (part * part)

    def level(k, carry):
        t, s, dens, step_t, step_s, step_d, top_t, top_s = carry
        below = jnp.minimum(k + 1, levels - 1)
        open_below = k + 1 < depth
        t1, s1 = at(t_ref, below), at(s_ref, below)
        dens1 = density(t1, s1, height(below))
        next_t = jnp.where(open_below, t1 - t, 0.0)
        next_s = jnp.where(open_below, s1 - s, 0.0)
        next_d = jnp.where(open_below, dens1 - dens, 0.0)
        w1 = at(w_ref, below)
        up = w1 > 0.0
        low_t = jnp.where(open_below, w1 * jnp.where(up, t1, t), 0.0)
        low_s = jnp.where(open_below, w1 * jnp.where(up, s1, s), 0.0)
        here = (t, s, dens, step_t + next_t, step_s + next_s, step_d + next_d)
        fx_t, fx_s = face_flux(at(u_ref, k), diff_x, k < depth_x, here, tuple(map(east, here)))
        fy_t, fy_s = face_flux(at(v_ref, k), diff_y, k < depth_y, here, tuple(map(north, here)))
        star_t_ref[k] = t - (fx_t - west(fx_t)) - (fy_t - south(fy_t)) - (top_t - low_t)
        star_s_ref[k] = s - (fx_s - west(fx_s)) - (fy_s - south(fy_s)) - (top_s - low_s)
        return t1, s1, dens1, next_t, next_s, next_d, low_t, low_s

    zero = jnp.zeros((ROWS, LANES), jnp.float32)
    t0, s0 = t_ref[0], s_ref[0]
    first = (t0, s0, density(t0, s0, bottom_depth * (0.5 / levels) ** 2), zero, zero, zero, zero, zero)

    def some(i, carry):
        for j in range(group):
            carry = level(i * group + j, carry)
        return carry

    lax.fori_loop(0, levels // group, some, first)

    middle = levels // 2

    def coupling(k):
        return jnp.where(k < depth, kap_ref[k], 0.0)

    def eliminate(j, carry):
        above, ratio, below, ratio_up = carry
        k = j
        under = coupling(k + 1)
        inv = 1.0 / (1.0 + above + under - above * ratio)
        inv_ref[k] = inv
        low_ref[k] = above * inv
        ratio = under * inv
        ratio_ref[k] = ratio
        k = levels - 1 - j
        over = coupling(k)
        inv = 1.0 / (1.0 + over + below - below * ratio_up)
        inv_ref[k] = inv
        low_ref[k] = below * inv
        ratio_up = over * inv
        ratio_ref[k] = ratio_up
        return under, ratio, over, ratio_up

    above, ratio, below, ratio_up = lax.fori_loop(0, middle, eliminate, (zero, zero, zero, zero))
    inv = 1.0 / (1.0 + above + below - above * ratio - below * ratio_up)
    inv_ref[middle] = inv
    low_ref[middle] = above * inv
    ratio_ref[middle] = below * inv

    gy = lax.axis_index("gy")
    y_even = gy % 2 == 0
    tail = jnp.zeros((block - levels, LANES), jnp.float32)
    extra = jnp.zeros((block - levels - 2, LANES), jnp.float32)
    depth_f = depth.astype(jnp.float32)
    for i, ref in enumerate((t_ref, s_ref, v_ref)):
        flat = ref.reshape(levels * ROWS, LANES)
        for place, keep_top in ((0, y_even), (1, jnp.logical_not(y_even))):
            top = flat[pl.ds(ROWS - 1, levels, stride=ROWS), :]
            low = flat[pl.ds(0, levels, stride=ROWS), :]
            end = tail
            if i == 0:
                end = jnp.concatenate(
                    [
                        jnp.where(keep_top, diff[ROWS - 1 :], diff[:1]),
                        jnp.where(keep_top, depth_f[ROWS - 1 :], depth_f[:1]),
                        extra,
                    ],
                    0,
                )
            own_ref[place, i] = jnp.concatenate([jnp.where(keep_top, top, low), end], 0)


def column_sums(x, open_here, axis):
    size = x.shape[axis]
    step = jnp.where(open_here, x - pltpu.roll(x, 1, axis), 0.0)
    return step + pltpu.roll(step, size - 1, axis)


def side(temper, saline, depth, index, heights, axis):
    dens = density(temper, saline, heights)
    open_here = jnp.logical_and(index >= 1, index < depth)
    return (
        temper,
        saline,
        dens,
        column_sums(temper, open_here, axis),
        column_sums(saline, open_here, axis),
        column_sums(dens, open_here, axis),
    )


def edge_flux(levels, axis, index, own, got, own_left, fold):
    part = (index.astype(jnp.float32) + 0.5) / levels
    heights = bottom_depth * (part * part)
    left = [jnp.where(own_left, o, g) for o, g in zip(own, got)]
    right = [jnp.where(own_left, g, o) for o, g in zip(own, got)]
    speed = left[2]
    if fold is not None:
        speed = jnp.where(fold, 0.5 * (own[2] - got[2]), speed)
    wet = index.astype(jnp.float32) < jnp.minimum(left[4], right[4])
    level = index.astype(jnp.float32)
    return face_flux(
        speed,
        0.5 * (left[3] + right[3]),
        wet,
        side(left[0], left[1], left[4], level, heights, axis),
        side(right[0], right[1], right[4], level, heights, axis),
    )


def final_kernel(
    levels, got_a, got_b, got_xa, got_xb, own_ref, own_xa, own_xb,
    star_t_ref, star_s_ref, inv_ref, low_ref, ratio_ref,
    out_t_ref, out_s_ref, north_ref, south_ref,
):
    block = padded(levels)
    gy, gx = lax.axis_index("gy"), lax.axis_index("gx")
    y_even, x_even = gy % 2 == 0, gx % 2 == 0
    y_odd, x_odd = jnp.logical_not(y_even), jnp.logical_not(x_even)
    is_top = gy == lax.axis_size("gy") - 1

    index = lax.broadcasted_iota(jnp.int32, (block, LANES), 0)

    def rows(ref):
        t, s, q = ref[0], ref[1], ref[2]
        return t, s, q, t[levels : levels + 1], t[levels + 1 : levels + 2]

    flux_a = edge_flux(levels, 0, index, rows(own_ref.at[0]), rows(got_a), y_even, None)
    flux_b = edge_flux(levels, 0, index, rows(own_ref.at[1]), rows(got_b), y_odd, is_top)
    for i in range(2):
        north_ref[i] = -jnp.where(y_even, flux_a[i], flux_b[i])
        south_ref[i] = jnp.where(y_even, flux_b[i], flux_a[i])

    lane = lax.broadcasted_iota(jnp.int32, (ROWS, LANES), 1)
    row = lax.broadcasted_iota(jnp.int32, (ROWS, LANES), 0)

    def cols(ref):
        t, s, q = ref[0], ref[1], ref[2]
        return t, s, q, t[:, levels : levels + 1], t[:, levels + 1 : levels + 2]

    flux_xa = edge_flux(levels, 1, lane, cols(own_xa), cols(got_xa), x_even, None)
    flux_xb = edge_flux(levels, 1, lane, cols(own_xb), cols(got_xb), x_odd, None)
    east = [-jnp.where(x_even, flux_xa[i], flux_xb[i]) for i in range(2)]
    west = [jnp.where(x_even, flux_xb[i], flux_xa[i]) for i in range(2)]
    last_lane, first_lane = lane == LANES - 1, lane == 0
    last_row, first_row = row == ROWS - 1, row == 0

    def right_side(i, k):
        ref = (star_t_ref, star_s_ref)[i]
        x_part = jnp.where(
            last_lane,
            pltpu.roll(east[i], (LANES - 1 - k) % LANES, 1),
            jnp.where(first_lane, pltpu.roll(west[i], (-k) % LANES, 1), 0.0),
        )
        y_part = jnp.where(
            last_row,
            north_ref[i, k : k + 1, :],
            jnp.where(first_row, south_ref[i, k : k + 1, :], 0.0),
        )
        return (ref[k] + (x_part + y_part)) * inv_ref[k]

    outs = (out_t_ref, out_s_ref)
    middle = levels // 2
    zero = jnp.zeros((ROWS, LANES), jnp.float32)
    upper, lower = [zero, zero], [zero, zero]
    for j in range(middle):
        for i in range(2):
            upper[i] = right_side(i, j) + low_ref[j] * upper[i]
            outs[i][j] = upper[i]
            k = levels - 1 - j
            lower[i] = right_side(i, k) + low_ref[k] * lower[i]
            outs[i][k] = lower[i]
    for i in range(2):
        solved = right_side(i, middle) + low_ref[middle] * upper[i] + ratio_ref[middle] * lower[i]
        outs[i][middle] = solved
        upper[i] = lower[i] = solved
    for j in range(1, middle + 1):
        for i in range(2):
            k = middle - j
            upper[i] = outs[i][k] + ratio_ref[k] * upper[i]
            outs[i][k] = upper[i]
            k = middle + j
            lower[i] = outs[i][k] + ratio_ref[k] * lower[i]
            outs[i][k] = lower[i]


def call(kernel, outs, n_in, scratch=(), flops=0, name=None):
    return pl.pallas_call(
        kernel,
        out_shape=[jax.ShapeDtypeStruct(s, jnp.float32) for s in outs],
        in_specs=[pl.BlockSpec(memory_space=pltpu.VMEM)] * n_in,
        out_specs=[pl.BlockSpec(memory_space=pltpu.VMEM)] * len(outs),
        scratch_shapes=[pltpu.VMEM(s, jnp.float32) for s in scratch],
        compiler_params=pltpu.CompilerParams(vmem_limit_bytes=24 * 1024 * 1024),
        cost_estimate=pl.CostEstimate(flops=flops, bytes_accessed=4 * 1024 * 1024, transcendentals=0),
        name=name,
    )


def local(pairs, heat, salt, u, v, w, kap, diff, depth):
    levels, rows, lanes = heat.shape
    block = padded(levels)

    def flat(x):
        return x.reshape(levels * rows, lanes)

    pack_a, pack_b, pack_xa, pack_xb = call(
        functools.partial(pack_kernel, levels),
        [(3 * block, lanes)] * 2 + [(3 * rows, lanes)] * 2, 6, name="pack",
    )(flat(heat), flat(salt), flat(u), flat(v), diff, depth)
    got_b = lax.ppermute(pack_b, GRID_AXES, pairs["b"])
    got_xb = lax.ppermute(pack_xb, "gx", pairs["xb"])
    got_xa = lax.ppermute(pack_xa, "gx", pairs["xa"])
    got_a = lax.ppermute(pack_a, GRID_AXES, pairs["a"])
    cube = (levels, rows, lanes)
    group = next(g for g in (5, 3, 2, 1) if levels % g == 0)
    star_t, star_s, inv, low, ratio, own = call(
        functools.partial(inner_kernel, levels, group),
        [cube] * 5 + [(2, 3, block, lanes)], 8, flops=40_000_000, name="inner",
    )(heat, salt, u, v, w, kap, diff, depth)
    three = (3, rows, lanes)
    return call(
        functools.partial(final_kernel, levels),
        [cube] * 2, 12, scratch=[(2, block, lanes)] * 2, name="final",
    )(
        got_a.reshape(3, block, lanes), got_b.reshape(3, block, lanes),
        got_xa.reshape(three), got_xb.reshape(three),
        own, pack_xa.reshape(three), pack_xb.reshape(three),
        star_t, star_s, inv, low, ratio,
    )


def solution(mesh):
    ny, nx = mesh.shape["gy"], mesh.shape["gx"]

    def at(y, x):
        return y * nx + x

    pairs = {
        "a": [(at(y, x), at(y ^ 1, x)) for y in range(ny) for x in range(nx)],
        "b": [(at(y, x), at(((y + 1) ^ 1) - 1, x)) for y in range(1, ny - 1) for x in range(nx)]
        + [(at(ny - 1, x), at(ny - 1, nx - 1 - x)) for x in range(nx)],
        "xa": [(x, x ^ 1) for x in range(nx)],
        "xb": [(x, (((x + 1) ^ 1) - 1) % nx) for x in range(nx)],
    }
    cube = P(None, "gy", "gx")
    sheet = P("gy", "gx")
    return jax.shard_map(
        functools.partial(local, pairs),
        mesh=mesh,
        in_specs=(cube,) * 6 + (sheet, sheet),
        out_specs=(cube, cube),
        check_vma=False,
    )
```

time: 126 us -> 42.1 us (0.33)
  the two profiles are of different devices: /device:TPU:480 before, /device:TPU:7 now
where the time goes in v1:
time: 42.1 us; the launch traced here: 41.7 us
  starting transfers between devices  28.3 us (67%)
  Pallas kernels  5.84 us (14%)
  local copies, waits for them, and re-layouts  5.23 us (12%)
  waiting for transfers between devices  1.62 us (4%)
  between operations  0.72 us (2%)
    ppermute x1, starting transfers between devices, local(): got_b = lax.ppermute(pack_b, GRID_AXES, pairs['b'])  15.3 us
    ppermute x1, starting transfers between devices, local(): got_xb = lax.ppermute(pack_xb, 'gx', pairs['xb'])  7.81 us
    unnamed x16, local copies, waits for them, and re-layouts  5.23 us
    pallas_call x1, Pallas kernels, local(): call(functools.partial(inner_kernel, levels, group), [cube] * 5 + [(2, 3,...  3.68 us
    ppermute x1, starting transfers between devices, local(): got_xa = lax.ppermute(pack_xa, 'gx', pairs['xa'])  2.65 us
    ppermute x1, starting transfers between devices, local(): got_a = lax.ppermute(pack_a, GRID_AXES, pairs['a'])  2.58 us
    pallas_call x1, Pallas kernels, local(): call(functools.partial(final_kernel, levels), [cube] * 2, 12, scratch=[(2...  1.64 us
    ppermute x1, waiting for transfers between devices, local(): got_xb = lax.ppermute(pack_xb, 'gx', pairs['xb'])  1.61 us
  transfers between devices with their start and end apart: 4, of which 1 were waited for; matrix products, arithmetic and copies ran while one was open for 0% of the time, Pallas kernels for 9%

profile of v1, /device:TPU:7, one launch (start us, length us, event | category | flops | bytes accessed | tf_op | source)
XLA Modules:
  0.0 41.7 jit_solution(6462583010383559744)
XLA Ops:
  0.6 0.0 copy-start.6
  0.6 0.7 %copy-done.6 = f32[8,128]{1,0:T(8,128)S(1)} copy-done((f32[8,128]{1,0:T(8,128)S(1)}, f32[8,128]{1,0:T(8,128)}, u32[]{:S(2)}) %copy-start.6) | copy-done | bytes 4120
  1.3 0.0 copy-start
  1.3 1.0 %copy-done = f32[75,8,128]{2,1,0:T(8,128)S(1)} copy-done((f32[75,8,128]{2,1,0:T(8,128)S(1)}, f32[75,8,128]{2,1,0:T(8,128)}, u32[]{:S(2)}) %copy-start) | copy-done | bytes 307224
  2.3 0.0 copy-start.1
  2.3 1.0 %copy-done.1 = f32[75,8,128]{2,1,0:T(8,128)S(1)} copy-done((f32[75,8,128]{2,1,0:T(8,128)S(1)}, f32[75,8,128]{2,1,0:T(8,128)}, u32[]{:S(2)}) %copy-start.1) | copy-done | bytes 307224
  3.3 0.0 copy-start.2
  3.3 1.0 %copy-done.2 = f32[75,8,128]{2,1,0:T(8,128)S(1)} copy-done((f32[75,8,128]{2,1,0:T(8,128)S(1)}, f32[75,8,128]{2,1,0:T(8,128)}, u32[]{:S(2)}) %copy-start.2) | copy-done | bytes 307224
  4.2 0.0 copy-start.3
  4.2 1.0 %copy-done.3 = f32[75,8,128]{2,1,0:T(8,128)S(1)} copy-done((f32[75,8,128]{2,1,0:T(8,128)S(1)}, f32[75,8,128]{2,1,0:T(8,128)}, u32[]{:S(2)}) %copy-start.3) | copy-done | bytes 307224
  5.2 0.0 copy-start.7
  5.2 0.7 %copy-done.7 = s32[8,128]{1,0:T(8,128)S(1)} copy-done((s32[8,128]{1,0:T(8,128)S(1)}, s32[8,128]{1,0:T(8,128)}, u32[]{:S(2)}) %copy-start.7) | copy-done | bytes 4120
  5.9 0.0 copy-start.4
  5.9 0.0 copy-start.5
  5.9 0.5 %pack.1 = (f32[240,128]{1,0:T(8,128)S(1)}, f32[240,128]{1,0:T(8,128)S(1)}, f32[24,128]{1,0:T(8,128)S(1)}, f32[24,128]{1,0:T(8,128)S(1)}) custom-call(f32[600,128]{1,0:T(8,128)S(1)} %bitcast.10, f32[600,128]{1,0:T(8,128)S(1)} %bitcast.11, f32[600,128]{1,0:T(8,128)S(1)} %bitcast.12, f32[600,128]{1,0:T(8,128)S(1)} %bitcast.13, f32[8,128]{1,0:T(8,128)S(1)} %copy-done.6, ...), custom_call_target="tpu_custom_call" | custom-call | bytes 4194304 | tf_op jit(solution)/shard_map/pack/pallas_call | solution.py:348
  6.4 2.6 %collective-permute-start = (f32[240,128]{1,0:T(8,128)S(1)}, f32[240,128]{1,0:T(8,128)S(1)}, u32[]{:S(2)}, u32[]{:S(2)}) collective-permute-start(f32[240,128]{1,0:T(8,128)S(1)} %get-tuple-element.12), channel_id=1, source_target_pairs={{0,32},{1,33},{2,34},{3,35},{4,36},{5,37},{6,38},{7,39},{8,40},{9,... | collective-permute-start | bytes 368648 | tf_op jit(solution)/shard_map/ppermute | solution.py:355
  9.0 15.3 %collective-permute-start.1 = (f32[240,128]{1,0:T(8,128)S(1)}, f32[240,128]{1,0:T(8,128)S(1)}, u32[]{:S(2)}, u32[]{:S(2)}) collective-permute-start(f32[240,128]{1,0:T(8,128)S(1)} %get-tuple-element.13), channel_id=1, source_target_pairs={{32,64},{33,65},{34,66},{35,67},{36,68},{37,69},{38,70},{39,71},{4... | collective-permute-start | bytes 368648 | tf_op jit(solution)/shard_map/ppermute | solution.py:352
  24.3 2.6 %collective-permute-start.2 = (f32[24,128]{1,0:T(8,128)S(1)}, f32[24,128]{1,0:T(8,128)S(1)}, u32[]{:S(2)}, u32[]{:S(2)}) collective-permute-start(f32[24,128]{1,0:T(8,128)S(1)} %get-tuple-element.14), channel_id=1, source_target_pairs={{0,1},{1,0},{2,3},{3,2},{4,5},{5,4},{6,7},{7,6},{8,9},{9,8},{10,11... | collective-permute-start | bytes 36872 | tf_op jit(solution)/shard_map/ppermute | solution.py:354
  26.9 7.8 %collective-permute-start.3 = (f32[24,128]{1,0:T(8,128)S(1)}, f32[24,128]{1,0:T(8,128)S(1)}, u32[]{:S(2)}, u32[]{:S(2)}) collective-permute-start(f32[24,128]{1,0:T(8,128)S(1)} %get-tuple-element.15), channel_id=1, source_target_pairs={{0,31},{1,2},{2,1},{3,4},{4,3},{5,6},{6,5},{7,8},{8,7},{9,10},{10,... | collective-permute-start | bytes 36872 | tf_op jit(solution)/shard_map/ppermute | solution.py:353
  34.7 0.0 copy-done.4
  34.7 0.0 copy-done.5
  34.8 3.7 %inner.1 = (f32[75,8,128]{2,1,0:T(8,128)S(1)}, f32[75,8,128]{2,1,0:T(8,128)S(1)}, f32[75,8,128]{2,1,0:T(8,128)S(1)}, f32[75,8,128]{2,1,0:T(8,128)S(1)}, f32[75,8...) custom-call(f32[75,8,128]{2,1,0:T(8,128)S(1)} %copy-done, f32[75,8,128]{2,1,0:T(8,128)S(1)} %copy-done.1, ...), custom_call_target="tpu_custom_call" | custom-call | flops 40000000 | bytes 4194304 | tf_op jit(solution)/shard_map/inner/pallas_call | solution.py:358
  38.4 0.0 collective-permute-done.2
  38.5 1.6 %collective-permute-done.3 = f32[24,128]{1,0:T(8,128)S(1)} collective-permute-done((f32[24,128]{1,0:T(8,128)S(1)}, f32[24,128]{1,0:T(8,128)S(1)}, u32[]{:S(2)}, u32[]{:S(2)}) %collective-permute-start.3) | collective-permute-done | bytes 12320 | tf_op jit(solution)/shard_map/ppermute | solution.py:353
  40.1 0.0 collective-permute-done
  40.1 0.0 collective-permute-done.1
  40.1 1.6 %final.1 = (f32[75,8,128]{2,1,0:T(8,128)}, f32[75,8,128]{2,1,0:T(8,128)}) custom-call(f32[3,80,128]{2,1,0:T(8,128)S(1)} %bitcast.14, f32[3,80,128]{2,1,0:T(8,128)S(1)} %bitcast.15, f32[3,8,128]{2,1,0:T(8,128)S(1)} %bitcast.18, f32[3,8,128]{2,1,0:T(8,128)S(1)} %bitcast.19, f32[2,3,80,128]{3,2,1,0:T(8,128)S(1)} %get-tuple-element.16.own_ref, ...), custom_call_target="tpu_custom_call" | custom-call | bytes 4194304 | tf_op jit(solution)/shard_map/final/pallas_call | solution.py:363
Async XLA Ops:
  0.6 0.7 %copy-start.6 = (f32[8,128]{1,0:T(8,128)S(1)}, f32[8,128]{1,0:T(8,128)}, u32[]{:S(2)}) copy-start(f32[8,128]{1,0:T(8,128)} %diff_ref.3) | copy-start | bytes 12292
  1.3 1.0 %copy-start = (f32[75,8,128]{2,1,0:T(8,128)S(1)}, f32[75,8,128]{2,1,0:T(8,128)}, u32[]{:S(2)}) copy-start(f32[75,8,128]{2,1,0:T(8,128)} %t_ref.1) | copy-start | bytes 921604
  2.3 1.0 %copy-start.1 = (f32[75,8,128]{2,1,0:T(8,128)S(1)}, f32[75,8,128]{2,1,0:T(8,128)}, u32[]{:S(2)}) copy-start(f32[75,8,128]{2,1,0:T(8,128)} %s_ref.1) | copy-start | bytes 921604
  3.3 1.0 %copy-start.2 = (f32[75,8,128]{2,1,0:T(8,128)S(1)}, f32[75,8,128]{2,1,0:T(8,128)}, u32[]{:S(2)}) copy-start(f32[75,8,128]{2,1,0:T(8,128)} %u_ref.1) | copy-start | bytes 921604
  4.2 1.0 %copy-start.3 = (f32[75,8,128]{2,1,0:T(8,128)S(1)}, f32[75,8,128]{2,1,0:T(8,128)}, u32[]{:S(2)}) copy-start(f32[75,8,128]{2,1,0:T(8,128)} %v_ref.1) | copy-start | bytes 921604
  5.2 0.7 %copy-start.7 = (s32[8,128]{1,0:T(8,128)S(1)}, s32[8,128]{1,0:T(8,128)}, u32[]{:S(2)}) copy-start(s32[8,128]{1,0:T(8,128)} %depth_ref.3) | copy-start | bytes 12292
  5.9 28.9 %copy-start.4 = (f32[75,8,128]{2,1,0:T(8,128)S(1)}, f32[75,8,128]{2,1,0:T(8,128)}, u32[]{:S(2)}) copy-start(f32[75,8,128]{2,1,0:T(8,128)} %w_ref.1) | copy-start | bytes 921604
  5.9 28.9 %copy-start.5 = (f32[75,8,128]{2,1,0:T(8,128)S(1)}, f32[75,8,128]{2,1,0:T(8,128)}, u32[]{:S(2)}) copy-start(f32[75,8,128]{2,1,0:T(8,128)} %kap_ref.1) | copy-start | bytes 921604
  6.4 33.7 %collective-permute-start = (f32[240,128]{1,0:T(8,128)S(1)}, f32[240,128]{1,0:T(8,128)S(1)}, u32[]{:S(2)}, u32[]{:S(2)}) collective-permute-start(f32[240,128]{1,0:T(8,128)S(1)} %get-tuple-element.12), channel_id=1, source_target_pairs={{0,32},{1,33},{2,34},{3,35},{4,36},{5,37},{6,38},{7,39},{8,40},{9,... | collective-permute-start | bytes 368648 | tf_op jit(solution)/shard_map/ppermute | solution.py:355
  9.0 31.1 %collective-permute-start.1 = (f32[240,128]{1,0:T(8,128)S(1)}, f32[240,128]{1,0:T(8,128)S(1)}, u32[]{:S(2)}, u32[]{:S(2)}) collective-permute-start(f32[240,128]{1,0:T(8,128)S(1)} %get-tuple-element.13), channel_id=1, source_target_pairs={{32,64},{33,65},{34,66},{35,67},{36,68},{37,69},{38,70},{39,71},{4... | collective-permute-start | bytes 368648 | tf_op jit(solution)/shard_map/ppermute | solution.py:352
  24.3 14.2 %collective-permute-start.2 = (f32[24,128]{1,0:T(8,128)S(1)}, f32[24,128]{1,0:T(8,128)S(1)}, u32[]{:S(2)}, u32[]{:S(2)}) collective-permute-start(f32[24,128]{1,0:T(8,128)S(1)} %get-tuple-element.14), channel_id=1, source_target_pairs={{0,1},{1,0},{2,3},{3,2},{4,5},{5,4},{6,7},{7,6},{8,9},{9,8},{10,11... | collective-permute-start | bytes 36872 | tf_op jit(solution)/shard_map/ppermute | solution.py:354
  26.9 13.2 %collective-permute-start.3 = (f32[24,128]{1,0:T(8,128)S(1)}, f32[24,128]{1,0:T(8,128)S(1)}, u32[]{:S(2)}, u32[]{:S(2)}) collective-permute-start(f32[24,128]{1,0:T(8,128)S(1)} %get-tuple-element.15), channel_id=1, source_target_pairs={{0,31},{1,2},{2,1},{3,4},{4,3},{5,6},{6,5},{7,8},{8,7},{9,10},{10,... | collective-permute-start | bytes 36872 | tf_op jit(solution)/shard_map/ppermute | solution.py:353

commit v2 on v1

--- a/solution.py
+++ b/solution.py
@@ -49,33 +49,63 @@
     return one(0), one(1)
 
 
-def pack_kernel(levels, t_ref, s_ref, u_ref, v_ref, diff_ref, depth_ref, a_ref, b_ref, xa_ref, xb_ref):
+def fetch(sources, targets, sems):
+    copies = [pltpu.make_async_copy(a, b, sems.at[i]) for i, (a, b) in enumerate(zip(sources, targets))]
+    for copy in copies:
+        copy.start()
+    return copies
+
+
+def pack_kernel(
+    levels, t_hbm, s_hbm, v_hbm, u_hbm, diff_hbm, depth_hbm, a_ref, b_ref, xb_ref, xa_ref,
+    t_ref, s_ref, v_ref, u_ref, diff_ref, depth_ref, sems,
+):
+    copies = fetch(
+        (t_hbm, s_hbm, v_hbm, u_hbm, diff_hbm, depth_hbm),
+        (t_ref, s_ref, v_ref, u_ref, diff_ref, depth_ref),
+        sems,
+    )
     block = padded(levels)
     gy, gx = lax.axis_index("gy"), lax.axis_index("gx")
     y_even, x_even = gy % 2 == 0, gx % 2 == 0
     is_top = gy == lax.axis_size("gy") - 1
     lane = lax.broadcasted_iota(jnp.int32, (block, LANES), 1)
     source = jnp.where(is_top, LANES - 1 - lane, lane)
+    one_lane = lax.broadcasted_iota(jnp.int32, (ROWS, LANES), 1)
+    copies[4].wait()
+    copies[5].wait()
     depth = depth_ref[...].astype(jnp.float32)
     diff = diff_ref[...]
     zero = jnp.zeros((block - levels - 2, LANES), jnp.float32)
-
-    def rows(ref, r):
-        return ref[pl.ds(r, levels, stride=ROWS), :]
-
-    def part(ref, r, first):
-        tail = [diff[r : r + 1], depth[r : r + 1], zero] if first else [jnp.zeros((block - levels, LANES), jnp.float32)]
-        return jnp.concatenate([rows(ref, r)] + tail, 0)
-
-    top = [part(t_ref, 7, True), part(s_ref, 7, False), part(v_ref, 7, False)]
-    low = [part(t_ref, 0, True), part(s_ref, 0, False), jnp.zeros((block, LANES), jnp.float32)]
-    for i in range(3):
-        a_ref[i * block : (i + 1) * block] = jnp.where(y_even, top[i], low[i])
+    tail = jnp.zeros((block - levels, LANES), jnp.float32)
+
+    def row_part(ref, i):
+        top = ref[pl.ds(ROWS - 1, levels, stride=ROWS), :]
+        low = ref[pl.ds(0, levels, stride=ROWS), :]
+        end = tail
+        if i == 0:
+            end = jnp.concatenate(
+                [
+                    jnp.where(y_even, diff[:1], diff[ROWS - 1 :]),
+                    jnp.where(y_even, depth[:1], depth[ROWS - 1 :]),
+                    zero,
+                ],
+                0,
+            )
+        chosen = jnp.concatenate([jnp.where(y_even, low, top), end], 0)
+        if i == 0:
+            end = jnp.concatenate(
+                [
+                    jnp.where(y_even, diff[ROWS - 1 :], diff[:1]),
+                    jnp.where(y_even, depth[ROWS - 1 :], depth[:1]),
+                    zero,
+                ],
+                0,
+            )
+        a_ref[i * block : (i + 1) * block] = jnp.concatenate([jnp.where(y_even, top, low), end], 0)
         b_ref[i * block : (i + 1) * block] = jnp.take_along_axis(
-            jnp.where(y_even, low[i], top[i]), source, axis=1, mode="promise_in_bounds"
+            chosen, source, axis=1, mode="promise_in_bounds"
         )
-
-    one_lane = lax.broadcasted_iota(jnp.int32, (ROWS, LANES), 1)
 
     def columns(ref, c, first):
         out = jnp.zeros((ROWS, LANES), jnp.float32)
@@ -87,17 +117,34 @@
             out = jnp.where(one_lane == levels + 1, pltpu.roll(depth, (levels + 1 - c) % LANES, 1), out)
         return out
 
-    east = [columns(t_ref, 127, True), columns(s_ref, 127, False), columns(u_ref, 127, False)]
-    west = [columns(t_ref, 0, True), columns(s_ref, 0, False), jnp.zeros((ROWS, LANES), jnp.float32)]
-    for i in range(3):
-        xa_ref[i * ROWS : (i + 1) * ROWS] = jnp.where(x_even, east[i], west[i])
-        xb_ref[i * ROWS : (i + 1) * ROWS] = jnp.where(x_even, west[i], east[i])
+    def column_part(ref, i):
+        east = columns(ref, LANES - 1, i == 0)
+        west = columns(ref, 0, i == 0) if i < 2 else jnp.zeros((ROWS, LANES), jnp.float32)
+        xa_ref[i * ROWS : (i + 1) * ROWS] = jnp.where(x_even, east, west)
+        xb_ref[i * ROWS : (i + 1) * ROWS] = jnp.where(x_even, west, east)
+
+    for i, ref in enumerate((t_ref, s_ref)):
+        copies[i].wait()
+        row_part(ref, i)
+        column_part(ref, i)
+    copies[2].wait()
+    row_part(v_ref, 2)
+    copies[3].wait()
+    column_part(u_ref, 2)
 
 
 def inner_kernel(
-    levels, group, t_ref, s_ref, u_ref, v_ref, w_ref, kap_ref, diff_ref, depth_ref,
-    star_t_ref, star_s_ref, inv_ref, low_ref, ratio_ref, own_ref,
+    levels, group, t_hbm, s_hbm, u_hbm, v_hbm, w_hbm, kap_hbm, diff_hbm, depth_hbm,
+    star_t_ref, star_s_ref, inv_ref, low_ref, ratio_ref, own_a_ref, own_b_ref,
+    t_ref, s_ref, u_ref, v_ref, w_ref, kap_ref, diff_ref, depth_ref, sems,
 ):
+    copies = fetch(
+        (t_hbm, s_hbm, u_hbm, v_hbm, w_hbm, kap_hbm, diff_hbm, depth_hbm),
+        (t_ref, s_ref, u_ref, v_ref, w_ref, kap_ref, diff_ref, depth_ref),
+        sems,
+    )
+    for copy in copies:
+        copy.wait()
     block = padded(levels)
     depth = depth_ref[...]
     diff = diff_ref[...]
@@ -195,7 +242,7 @@
     depth_f = depth.astype(jnp.float32)
     for i, ref in enumerate((t_ref, s_ref, v_ref)):
         flat = ref.reshape(levels * ROWS, LANES)
-        for place, keep_top in ((0, y_even), (1, jnp.logical_not(y_even))):
+        for own_ref, keep_top in ((own_a_ref, y_even), (own_b_ref, jnp.logical_not(y_even))):
             top = flat[pl.ds(ROWS - 1, levels, stride=ROWS), :]
             low = flat[pl.ds(0, levels, stride=ROWS), :]
             end = tail
@@ -208,7 +255,7 @@
                     ],
                     0,
                 )
-            own_ref[place, i] = jnp.concatenate([jnp.where(keep_top, top, low), end], 0)
+            own_ref[i * block : (i + 1) * block] = jnp.concatenate([jnp.where(keep_top, top, low), end], 0)
 
 
 def column_sums(x, open_here, axis):
@@ -250,7 +297,7 @@
 
 
 def final_kernel(
-    levels, got_a, got_b, got_xa, got_xb, own_ref, own_xa, own_xb,
+    levels, cut, got_a, got_b, got_xa, got_xb, got_relay, own_a, own_b, own_xa, own_xb,
     star_t_ref, star_s_ref, inv_ref, low_ref, ratio_ref,
     out_t_ref, out_s_ref, north_ref, south_ref,
 ):
@@ -262,12 +309,14 @@
 
     index = lax.broadcasted_iota(jnp.int32, (block, LANES), 0)
 
+    corner = jnp.logical_and(is_far_row(gy), is_far_column(gx, cut))
+
     def rows(ref):
-        t, s, q = ref[0], ref[1], ref[2]
+        t, s, q = (ref[i * block : (i + 1) * block] for i in range(3))
         return t, s, q, t[levels : levels + 1], t[levels + 1 : levels + 2]
 
-    flux_a = edge_flux(levels, 0, index, rows(own_ref.at[0]), rows(got_a), y_even, None)
-    flux_b = edge_flux(levels, 0, index, rows(own_ref.at[1]), rows(got_b), y_odd, is_top)
+    flux_a = edge_flux(levels, 0, index, rows(own_a), rows(got_a), y_even, None)
+    flux_b = edge_flux(levels, 0, index, rows(own_b), rows(got_b), y_odd, is_top)
     for i in range(2):
         north_ref[i] = -jnp.where(y_even, flux_a[i], flux_b[i])
         south_ref[i] = jnp.where(y_even, flux_b[i], flux_a[i])
@@ -275,12 +324,17 @@
     lane = lax.broadcasted_iota(jnp.int32, (ROWS, LANES), 1)
     row = lax.broadcasted_iota(jnp.int32, (ROWS, LANES), 0)
 
-    def cols(ref):
-        t, s, q = ref[0], ref[1], ref[2]
+    def cols(ref, other=None):
+        t, s, q = (
+            ref[i * ROWS : (i + 1) * ROWS]
+            if other is None
+            else jnp.where(corner, other[i * ROWS : (i + 1) * ROWS], ref[i * ROWS : (i + 1) * ROWS])
+            for i in range(3)
+        )
         return t, s, q, t[:, levels : levels + 1], t[:, levels + 1 : levels + 2]
 
     flux_xa = edge_flux(levels, 1, lane, cols(own_xa), cols(got_xa), x_even, None)
-    flux_xb = edge_flux(levels, 1, lane, cols(own_xb), cols(got_xb), x_odd, None)
+    flux_xb = edge_flux(levels, 1, lane, cols(own_xb), cols(got_xb, got_relay), x_odd, None)
     east = [-jnp.where(x_even, flux_xa[i], flux_xb[i]) for i in range(2)]
     west = [jnp.where(x_even, flux_xb[i], flux_xa[i]) for i in range(2)]
     last_lane, first_lane = lane == LANES - 1, lane == 0
@@ -325,69 +379,96 @@
             outs[i][k] = lower[i]
 
 
-def call(kernel, outs, n_in, scratch=(), flops=0, name=None):
+def call(kernel, outs, operands, memory, scratch=(), flops=0, name=None):
     return pl.pallas_call(
         kernel,
         out_shape=[jax.ShapeDtypeStruct(s, jnp.float32) for s in outs],
-        in_specs=[pl.BlockSpec(memory_space=pltpu.VMEM)] * n_in,
+        in_specs=[pl.BlockSpec(memory_space=memory)] * len(operands),
         out_specs=[pl.BlockSpec(memory_space=pltpu.VMEM)] * len(outs),
-        scratch_shapes=[pltpu.VMEM(s, jnp.float32) for s in scratch],
+        scratch_shapes=list(scratch),
         compiler_params=pltpu.CompilerParams(vmem_limit_bytes=24 * 1024 * 1024),
         cost_estimate=pl.CostEstimate(flops=flops, bytes_accessed=4 * 1024 * 1024, transcendentals=0),
         name=name,
-    )
-
-
-def local(pairs, heat, salt, u, v, w, kap, diff, depth):
+    )(*operands)
+
+
+def local(pairs, cut, heat, salt, u, v, w, kap, diff, depth):
     levels, rows, lanes = heat.shape
     block = padded(levels)
+    cube, wide, thin = (levels, rows, lanes), (3 * block, lanes), (3 * rows, lanes)
 
     def flat(x):
         return x.reshape(levels * rows, lanes)
 
-    pack_a, pack_b, pack_xa, pack_xb = call(
-        functools.partial(pack_kernel, levels),
-        [(3 * block, lanes)] * 2 + [(3 * rows, lanes)] * 2, 6, name="pack",
-    )(flat(heat), flat(salt), flat(u), flat(v), diff, depth)
-    got_b = lax.ppermute(pack_b, GRID_AXES, pairs["b"])
-    got_xb = lax.ppermute(pack_xb, "gx", pairs["xb"])
-    got_xa = lax.ppermute(pack_xa, "gx", pairs["xa"])
-    got_a = lax.ppermute(pack_a, GRID_AXES, pairs["a"])
-    cube = (levels, rows, lanes)
+    def room(operands):
+        return [pltpu.VMEM(x.shape, x.dtype) for x in operands] + [pltpu.SemaphoreType.DMA((len(operands),))]
+
+    def moved(x, which):
+        return lax.ppermute(x, GRID_AXES, pairs[which])
+
+    operands = tuple(pltpu.with_memory_space_constraint(x, pltpu.HBM) for x in (flat(heat), flat(salt), flat(v), flat(u), diff, depth))
+    pack_a, pack_b, pack_xb, pack_xa = call(
+        functools.partial(pack_kernel, levels), [wide, wide, thin, thin], operands, pltpu.HBM, room(operands), name="pack"
+    )
+    got_a = moved(pack_a, "a")
+    got_b = moved(pack_b, "b")
+    relayed = moved(pack_xb, "relay")
+    got_xb = moved(pack_xb, "xb")
+    got_xa = moved(pack_xa, "xa")
     group = next(g for g in (5, 3, 2, 1) if levels % g == 0)
-    star_t, star_s, inv, low, ratio, own = call(
+    operands = tuple(pltpu.with_memory_space_constraint(x, pltpu.HBM) for x in (heat, salt, u, v, w, kap, diff, depth))
+    star_t, star_s, inv, low, ratio, own_a, own_b = call(
         functools.partial(inner_kernel, levels, group),
-        [cube] * 5 + [(2, 3, block, lanes)], 8, flops=40_000_000, name="inner",
-    )(heat, salt, u, v, w, kap, diff, depth)
-    three = (3, rows, lanes)
+        [cube] * 5 + [wide, wide], operands, pltpu.HBM, room(operands), flops=40_000_000, name="inner",
+    )
+    relayed, star_t = lax.optimization_barrier((relayed, star_t))
+    got_relay = moved(relayed, "hand_on")
+    operands = (
+        got_a, got_b, got_xa, got_xb, got_relay, own_a, own_b, pack_xa, pack_xb,
+        star_t, star_s, inv, low, ratio,
+    )
     return call(
-        functools.partial(final_kernel, levels),
-        [cube] * 2, 12, scratch=[(2, block, lanes)] * 2, name="final",
-    )(
-        got_a.reshape(3, block, lanes), got_b.reshape(3, block, lanes),
-        got_xa.reshape(three), got_xb.reshape(three),
-        own, pack_xa.reshape(three), pack_xb.reshape(three),
-        star_t, star_s, inv, low, ratio,
-    )
+        functools.partial(final_kernel, levels, cut),
+        [cube] * 2, operands, pltpu.VMEM, [pltpu.VMEM((2, block, lanes), jnp.float32)] * 2, name="final",
+    )
+
+
+def is_far_row(y):
+    ny = lax.axis_size("gy")
+    return (y == ny // 2 - 1) | (y == ny // 2) | (y == ny - 1)
+
+
+def is_far_column(x, cut):
+    return (x % cut == 0) | (x % cut == cut - 1)
 
 
 def solution(mesh):
     ny, nx = mesh.shape["gy"], mesh.shape["gx"]
+    cut = nx // 4
+    far_rows = (ny // 2 - 1, ny // 2, ny - 1)
+    far_columns = [x for x in range(nx) if x % cut in (0, cut - 1)]
 
     def at(y, x):
         return y * nx + x
 
+    def beside(x):
+        return (((x + 1) ^ 1) - 1) % nx
+
+    second = [(y, ((y + 1) ^ 1) - 1, x, x) for y in range(1, ny - 1) for x in range(nx)]
+    second += [(ny - 1, ny - 1, x, nx - 1 - x) for x in range(nx)]
+    corners = [(y, x) for y in far_rows for x in far_columns]
     pairs = {
         "a": [(at(y, x), at(y ^ 1, x)) for y in range(ny) for x in range(nx)],
-        "b": [(at(y, x), at(((y + 1) ^ 1) - 1, x)) for y in range(1, ny - 1) for x in range(nx)]
-        + [(at(ny - 1, x), at(ny - 1, nx - 1 - x)) for x in range(nx)],
-        "xa": [(x, x ^ 1) for x in range(nx)],
-        "xb": [(x, (((x + 1) ^ 1) - 1) % nx) for x in range(nx)],
+        "b": [(at(y, x), at(to_y, to_x)) for y, to_y, x, to_x in second],
+        "xa": [(at(y, x), at(y, x ^ 1)) for y in range(ny) for x in range(nx)],
+        "xb": [(at(y, x), at(y, beside(x))) for y in range(ny) for x in range(nx) if (y, x) not in corners],
+        "relay": [(at(y, x), at(y ^ 1, beside(x))) for y, x in corners],
+        "hand_on": [(at(y ^ 1, x), at(y, x)) for y, x in corners],
     }
     cube = P(None, "gy", "gx")
     sheet = P("gy", "gx")
     return jax.shard_map(
-        functools.partial(local, pairs),
+        functools.partial(local, pairs, cut),
         mesh=mesh,
         in_specs=(cube,) * 6 + (sheet, sheet),
         out_specs=(cube, cube),

time: 42.1 us -> 36.4 us (0.86)
  local copies, waits for them, and re-layouts: 5.23 us -> 0 us
  starting transfers between devices: 28.3 us -> 25.1 us
  Pallas kernels: 5.84 us -> 8.61 us
    unnamed x16 -> x0, local copies, waits for them, and re-layouts: 5.23 us -> none
    ppermute x4 -> x6, starting transfers between devices: 28.3 us -> 25.1 us  [moved(): return lax.ppermute(x, GRID_AXES, pairs[which])]
    pallas_call x3, Pallas kernels: 5.84 us -> 8.61 us  [call(): pl.pallas_call(kernel, out_shape=[jax.ShapeDtypeStruct(s, jnp.float32) fo...]
    ppermute x4 -> x6, waiting for transfers between devices: 1.62 us -> 1.76 us  [moved(): return lax.ppermute(x, GRID_AXES, pairs[which])]
  transfers between devices with their start and end apart: 4 -> 6, of which waited for: 1 -> 1; matrix products, arithmetic and copies ran while one was open for 0% -> 0% of each run, Pallas kernels for 9% -> 14%
where the time goes in v2:
time: 36.4 us; the launch traced here: 36.2 us
  starting transfers between devices  25.1 us (69%)
  Pallas kernels  8.61 us (24%)
  waiting for transfers between devices  1.76 us (5%)
  between operations  0.72 us (2%)
    ppermute x6, starting transfers between devices, moved(): return lax.ppermute(x, GRID_AXES, pairs[which])  25.1 us
    pallas_call x3, Pallas kernels, call(): pl.pallas_call(kernel, out_shape=[jax.ShapeDtypeStruct(s, jnp.float32) fo...  8.61 us
    ppermute x6, waiting for transfers between devices, moved(): return lax.ppermute(x, GRID_AXES, pairs[which])  1.76 us
  transfers between devices with their start and end apart: 6, of which 1 were waited for; matrix products, arithmetic and copies ran while one was open for 0% of the time, Pallas kernels for 14%

profile of v2, /device:TPU:7, one launch (start us, length us, event | category | flops | bytes accessed | tf_op | source)
XLA Modules:
  0.0 36.2 jit_solution(9355862155093904047)
XLA Ops:
  0.6 1.9 %pack.1 = (f32[240,128]{1,0:T(8,128)S(1)}, f32[240,128]{1,0:T(8,128)S(1)}, f32[24,128]{1,0:T(8,128)S(1)}, f32[24,128]{1,0:T(8,128)S(1)}) custom-call(f32[600,128]{1,0:T(8,128)} %bitcast.4, f32[600,128]{1,0:T(8,128)} %bitcast.5, f32[600,128]{1,0:T(8,128)} %bitcast.6, f32[600,128]{1,0:T(8,128)} %bitcast.7, f32[8,128]{1,0:T(8,128)} %diff_hbm.3, s32[8,128]{1,0:T(8,128)} %depth_hbm.3), custom_call_target="tpu_custom_call" | custom-call | bytes 4194304 | tf_op jit(solution)/shard_map/pack/pallas_call | solution.py:383
  2.5 2.6 %collective-permute-start = (f32[240,128]{1,0:T(8,128)S(1)}, f32[240,128]{1,0:T(8,128)S(1)}, u32[]{:S(2)}, u32[]{:S(2)}) collective-permute-start(f32[240,128]{1,0:T(8,128)S(1)} %get-tuple-element.15), channel_id=1, source_target_pairs={{0,32},{1,33},{2,34},{3,35},{4,36},{5,37},{6,38},{7,39},{8,40},{9,... | collective-permute-start | bytes 368648 | tf_op jit(solution)/shard_map/ppermute | solution.py:407
  5.1 15.3 %collective-permute-start.1 = (f32[240,128]{1,0:T(8,128)S(1)}, f32[240,128]{1,0:T(8,128)S(1)}, u32[]{:S(2)}, u32[]{:S(2)}) collective-permute-start(f32[240,128]{1,0:T(8,128)S(1)} %get-tuple-element.16), channel_id=1, source_target_pairs={{32,64},{33,65},{34,66},{35,67},{36,68},{37,69},{38,70},{39,71},{4... | collective-permute-start | bytes 368648 | tf_op jit(solution)/shard_map/ppermute | solution.py:407
  20.3 2.8 %collective-permute-start.4 = (f32[24,128]{1,0:T(8,128)S(1)}, f32[24,128]{1,0:T(8,128)S(1)}, u32[]{:S(2)}, u32[]{:S(2)}) collective-permute-start(f32[24,128]{1,0:T(8,128)S(1)} %get-tuple-element.18.own_xb), channel_id=1, source_target_pairs={{224,223},{231,200},{232,199},{239,208},{240,207},{247,216},{248,2... | collective-permute-start | bytes 36872 | tf_op jit(solution)/shard_map/ppermute | solution.py:407
  23.2 0.7 %collective-permute-start.3 = (f32[24,128]{1,0:T(8,128)S(1)}, f32[24,128]{1,0:T(8,128)S(1)}, u32[]{:S(2)}, u32[]{:S(2)}) collective-permute-start(f32[24,128]{1,0:T(8,128)S(1)} %get-tuple-element.18.own_xb), channel_id=1, source_target_pairs={{0,31},{1,2},{2,1},{3,4},{4,3},{5,6},{6,5},{7,8},{8,7},{9,10},{10,... | collective-permute-start | bytes 36872 | tf_op jit(solution)/shard_map/ppermute | solution.py:407
  23.8 2.5 %collective-permute-start.2 = (f32[24,128]{1,0:T(8,128)S(1)}, f32[24,128]{1,0:T(8,128)S(1)}, u32[]{:S(2)}, u32[]{:S(2)}) collective-permute-start(f32[24,128]{1,0:T(8,128)S(1)} %get-tuple-element.17.own_xa), channel_id=1, source_target_pairs={{0,1},{1,0},{2,3},{3,2},{4,5},{5,4},{6,7},{7,6},{8,9},{9,8},{10,11... | collective-permute-start | bytes 36872 | tf_op jit(solution)/shard_map/ppermute | solution.py:407
  26.3 5.1 %inner.1 = (f32[75,8,128]{2,1,0:T(8,128)S(1)}, f32[75,8,128]{2,1,0:T(8,128)S(1)}, f32[75,8,128]{2,1,0:T(8,128)S(1)}, f32[75,8,128]{2,1,0:T(8,128)S(1)}, f32[75,8...) custom-call(f32[75,8,128]{2,1,0:T(8,128)} %t_hbm.1, f32[75,8,128]{2,1,0:T(8,128)} %s_hbm.1, ...), custom_call_target="tpu_custom_call" | custom-call | flops 40000000 | bytes 4194304 | tf_op jit(solution)/shard_map/inner/pallas_call | solution.py:383
  31.5 0.0 collective-permute-done.4
  31.5 1.3 %collective-permute-start.5 = (f32[24,128]{1,0:T(8,128)S(1)}, f32[24,128]{1,0:T(8,128)S(1)}, u32[]{:S(2)}, u32[]{:S(2)}) collective-permute-start(f32[24,128]{1,0:T(8,128)S(1)} %collective-permute-done.4), channel_id=1, source_target_pairs={{192,224},{199,231},{200,232},{207,239},{208,240},{215,247},{216,2... | collective-permute-start | bytes 36872 | tf_op jit(solution)/shard_map/ppermute | solution.py:407
  32.8 0.0 collective-permute-done.2.got_xa
  32.8 0.0 collective-permute-done.3.got_xb
  32.8 1.8 %collective-permute-done.5.got_relay = f32[24,128]{1,0:T(8,128)S(1)} collective-permute-done((f32[24,128]{1,0:T(8,128)S(1)}, f32[24,128]{1,0:T(8,128)S(1)}, u32[]{:S(2)}, u32[]{:S(2)}) %collective-permute-start.5) | collective-permute-done | bytes 12320 | tf_op jit(solution)/shard_map/ppermute | solution.py:407
  34.5 0.0 collective-permute-done.got_a
  34.5 0.0 collective-permute-done.1.got_b
  34.5 1.6 %final.1 = (f32[75,8,128]{2,1,0:T(8,128)}, f32[75,8,128]{2,1,0:T(8,128)}) custom-call(f32[240,128]{1,0:T(8,128)S(1)} %collective-permute-done.got_a, f32[240,128]{1,0:T(8,128)S(1)} %collective-permute-done.1.got_b, f32[24,128]{1,0:T(8,128)S(1)} %collective-permute-done.2.got_xa, f32[24,128]{1,0:T(8,128)S(1)} %collective-permute-done.3.got_xb, ...), custom_call_target="tpu_custom_call" | custom-call | bytes 4194304 | tf_op jit(solution)/shard_map/final/pallas_call | solution.py:383
Async XLA Ops:
  2.5 32.1 %collective-permute-start = (f32[240,128]{1,0:T(8,128)S(1)}, f32[240,128]{1,0:T(8,128)S(1)}, u32[]{:S(2)}, u32[]{:S(2)}) collective-permute-start(f32[240,128]{1,0:T(8,128)S(1)} %get-tuple-element.15), channel_id=1, source_target_pairs={{0,32},{1,33},{2,34},{3,35},{4,36},{5,37},{6,38},{7,39},{8,40},{9,... | collective-permute-start | bytes 368648 | tf_op jit(solution)/shard_map/ppermute | solution.py:407
  5.1 29.5 %collective-permute-start.1 = (f32[240,128]{1,0:T(8,128)S(1)}, f32[240,128]{1,0:T(8,128)S(1)}, u32[]{:S(2)}, u32[]{:S(2)}) collective-permute-start(f32[240,128]{1,0:T(8,128)S(1)} %get-tuple-element.16), channel_id=1, source_target_pairs={{32,64},{33,65},{34,66},{35,67},{36,68},{37,69},{38,70},{39,71},{4... | collective-permute-start | bytes 368648 | tf_op jit(solution)/shard_map/ppermute | solution.py:407
  20.3 11.1 %collective-permute-start.4 = (f32[24,128]{1,0:T(8,128)S(1)}, f32[24,128]{1,0:T(8,128)S(1)}, u32[]{:S(2)}, u32[]{:S(2)}) collective-permute-start(f32[24,128]{1,0:T(8,128)S(1)} %get-tuple-element.18.own_xb), channel_id=1, source_target_pairs={{224,223},{231,200},{232,199},{239,208},{240,207},{247,216},{248,2... | collective-permute-start | bytes 36872 | tf_op jit(solution)/shard_map/ppermute | solution.py:407
  23.2 9.6 %collective-permute-start.3 = (f32[24,128]{1,0:T(8,128)S(1)}, f32[24,128]{1,0:T(8,128)S(1)}, u32[]{:S(2)}, u32[]{:S(2)}) collective-permute-start(f32[24,128]{1,0:T(8,128)S(1)} %get-tuple-element.18.own_xb), channel_id=1, source_target_pairs={{0,31},{1,2},{2,1},{3,4},{4,3},{5,6},{6,5},{7,8},{8,7},{9,10},{10,... | collective-permute-start | bytes 36872 | tf_op jit(solution)/shard_map/ppermute | solution.py:407
  23.8 8.9 %collective-permute-start.2 = (f32[24,128]{1,0:T(8,128)S(1)}, f32[24,128]{1,0:T(8,128)S(1)}, u32[]{:S(2)}, u32[]{:S(2)}) collective-permute-start(f32[24,128]{1,0:T(8,128)S(1)} %get-tuple-element.17.own_xa), channel_id=1, source_target_pairs={{0,1},{1,0},{2,3},{3,2},{4,5},{5,4},{6,7},{7,6},{8,9},{9,8},{10,11... | collective-permute-start | bytes 36872 | tf_op jit(solution)/shard_map/ppermute | solution.py:407
  31.5 3.1 %collective-permute-start.5 = (f32[24,128]{1,0:T(8,128)S(1)}, f32[24,128]{1,0:T(8,128)S(1)}, u32[]{:S(2)}, u32[]{:S(2)}) collective-permute-start(f32[24,128]{1,0:T(8,128)S(1)} %collective-permute-done.4), channel_id=1, source_target_pairs={{192,224},{199,231},{200,232},{207,239},{208,240},{215,247},{216,2... | collective-permute-start | bytes 36872 | tf_op jit(solution)/shard_map/ppermute | solution.py:407

commit v3 on v2

--- a/solution.py
+++ b/solution.py
@@ -35,10 +35,13 @@
     ) * temper + (salt_slope - (0.5 * haline_coef * haline_curve) * saline) * saline
 
 
+def quotient(top, bottom):
+    return top / bottom
+
+
 def face_flux(speed, half_diffus, wet, left, right):
-    denominator = jnp.maximum(0.25 * (left[5] + right[5]), 0.0) + strat_offset
-    slope = jnp.clip((right[2] - left[2]) / denominator, -slope_limit, slope_limit)
-    quarter = 0.25 * slope
+    steps = jnp.maximum(left[5] + right[5], 0.0) + 4.0 * strat_offset
+    quarter = jnp.clip(quotient(right[2] - left[2], steps), -0.25 * slope_limit, 0.25 * slope_limit)
     forward = speed > 0.0
 
     def one(i):
@@ -57,12 +60,12 @@
 
 
 def pack_kernel(
-    levels, t_hbm, s_hbm, v_hbm, u_hbm, diff_hbm, depth_hbm, a_ref, b_ref, xb_ref, xa_ref,
-    t_ref, s_ref, v_ref, u_ref, diff_ref, depth_ref, sems,
+    levels, t_hbm, s_hbm, v_hbm, u_hbm, diff_hbm, depth_hbm,
+    b_ref, xb_ref, xa_ref, a_ref, t_ref, s_ref, v_ref, u_ref, diff_ref, depth_ref, sems,
 ):
     copies = fetch(
         (t_hbm, s_hbm, v_hbm, u_hbm, diff_hbm, depth_hbm),
-        (t_ref, s_ref, v_ref, u_ref, diff_ref, depth_ref),
+        [ref.at[pl.ds(0, levels)] for ref in (t_ref, s_ref, v_ref, u_ref)] + [diff_ref, depth_ref],
         sems,
     )
     block = padded(levels)
@@ -76,41 +79,31 @@
     copies[5].wait()
     depth = depth_ref[...].astype(jnp.float32)
     diff = diff_ref[...]
-    zero = jnp.zeros((block - levels - 2, LANES), jnp.float32)
-    tail = jnp.zeros((block - levels, LANES), jnp.float32)
+    for ref in (t_ref, s_ref, v_ref, u_ref):
+        ref[levels:] = jnp.zeros((block - levels, ROWS, LANES), jnp.float32)
+    index = lax.broadcasted_iota(jnp.int32, (block, LANES), 0)
 
     def row_part(ref, i):
-        top = ref[pl.ds(ROWS - 1, levels, stride=ROWS), :]
-        low = ref[pl.ds(0, levels, stride=ROWS), :]
-        end = tail
+        ref = ref.reshape(block * ROWS, LANES)
+        top = ref[pl.ds(ROWS - 1, block, stride=ROWS), :]
+        low = ref[pl.ds(0, block, stride=ROWS), :]
+        near, far = jnp.where(y_even, top, low), jnp.where(y_even, low, top)
         if i == 0:
-            end = jnp.concatenate(
-                [
-                    jnp.where(y_even, diff[:1], diff[ROWS - 1 :]),
-                    jnp.where(y_even, depth[:1], depth[ROWS - 1 :]),
-                    zero,
-                ],
-                0,
-            )
-        chosen = jnp.concatenate([jnp.where(y_even, low, top), end], 0)
-        if i == 0:
-            end = jnp.concatenate(
-                [
-                    jnp.where(y_even, diff[ROWS - 1 :], diff[:1]),
-                    jnp.where(y_even, depth[ROWS - 1 :], depth[:1]),
-                    zero,
-                ],
-                0,
-            )
-        a_ref[i * block : (i + 1) * block] = jnp.concatenate([jnp.where(y_even, top, low), end], 0)
-        b_ref[i * block : (i + 1) * block] = jnp.take_along_axis(
-            chosen, source, axis=1, mode="promise_in_bounds"
-        )
+            for name, value in ((levels, diff), (levels + 1, depth)):
+                near = jnp.where(index == name, jnp.where(y_even, value[ROWS - 1 :], value[:1]), near)
+                far = jnp.where(index == name, jnp.where(y_even, value[:1], value[ROWS - 1 :]), far)
+        b_ref[i * block : (i + 1) * block] = jnp.take_along_axis(far, source, axis=1, mode="promise_in_bounds")
+        if i < 2:
+            a_ref[i * block : (i + 1) * block] = near
+        else:
+            whole = levels // ROWS * ROWS
+            a_ref[2 * block :] = near[:whole]
+            a_ref[block - (levels - whole) : block] = near[whole:levels]
 
     def columns(ref, c, first):
         out = jnp.zeros((ROWS, LANES), jnp.float32)
         for k in range(levels):
-            moved = pltpu.roll(ref[k * ROWS : (k + 1) * ROWS], (k - c) % LANES, 1)
+            moved = pltpu.roll(ref[k], (k - c) % LANES, 1)
             out = jnp.where(one_lane == k, moved, out)
         if first:
             out = jnp.where(one_lane == levels, pltpu.roll(diff, (levels - c) % LANES, 1), out)
@@ -133,18 +126,30 @@
     column_part(u_ref, 2)
 
 
-def inner_kernel(
-    levels, group, t_hbm, s_hbm, u_hbm, v_hbm, w_hbm, kap_hbm, diff_hbm, depth_hbm,
+def starts_early(gy, gx, cut):
+    ny = lax.axis_size("gy")
+    return jnp.logical_and(gy < ny // 2, gx % cut < cut // 2)
+
+
+def early_kernel(levels, group, cut, *refs):
+    @pl.when(starts_early(lax.axis_index("gy"), lax.axis_index("gx"), cut))
+    def _():
+        inner(levels, group, *refs)
+
+
+def late_kernel(levels, group, cut, *refs):
+    n_in, n_out = 8, 7
+    ins, outs = refs[:n_in], refs[n_in + n_out :]
+
+    @pl.when(jnp.logical_not(starts_early(lax.axis_index("gy"), lax.axis_index("gx"), cut)))
+    def _():
+        inner(levels, group, *ins, *outs)
+
+
+def inner(
+    levels, group, t_ref, s_ref, u_ref, v_ref, w_ref, kap_ref, diff_ref, depth_ref,
     star_t_ref, star_s_ref, inv_ref, low_ref, ratio_ref, own_a_ref, own_b_ref,
-    t_ref, s_ref, u_ref, v_ref, w_ref, kap_ref, diff_ref, depth_ref, sems,
 ):
-    copies = fetch(
-        (t_hbm, s_hbm, u_hbm, v_hbm, w_hbm, kap_hbm, diff_hbm, depth_hbm),
-        (t_ref, s_ref, u_ref, v_ref, w_ref, kap_ref, diff_ref, depth_ref),
-        sems,
-    )
-    for copy in copies:
-        copy.wait()
     block = padded(levels)
     depth = depth_ref[...]
     diff = diff_ref[...]
@@ -199,13 +204,6 @@
     t0, s0 = t_ref[0], s_ref[0]
     first = (t0, s0, density(t0, s0, bottom_depth * (0.5 / levels) ** 2), zero, zero, zero, zero, zero)
 
-    def some(i, carry):
-        for j in range(group):
-            carry = level(i * group + j, carry)
-        return carry
-
-    lax.fori_loop(0, levels // group, some, first)
-
     middle = levels // 2
 
     def coupling(k):
@@ -215,21 +213,42 @@
         above, ratio, below, ratio_up = carry
         k = j
         under = coupling(k + 1)
-        inv = 1.0 / (1.0 + above + under - above * ratio)
+        inv = quotient(1.0, 1.0 + above + under - above * ratio)
         inv_ref[k] = inv
         low_ref[k] = above * inv
         ratio = under * inv
         ratio_ref[k] = ratio
         k = levels - 1 - j
         over = coupling(k)
-        inv = 1.0 / (1.0 + over + below - below * ratio_up)
+        inv = quotient(1.0, 1.0 + over + below - below * ratio_up)
         inv_ref[k] = inv
         low_ref[k] = below * inv
         ratio_up = over * inv
         ratio_ref[k] = ratio_up
         return under, ratio, over, ratio_up
 
-    above, ratio, below, ratio_up = lax.fori_loop(0, middle, eliminate, (zero, zero, zero, zero))
+    rounds = levels // group
+    pairs = -(-middle // rounds)
+    whole = middle // pairs
+
+    def both(i, carry):
+        one, two = carry
+        for j in range(group):
+            one = level(i * group + j, one)
+            if j < pairs:
+                two = eliminate(i * pairs + j, two)
+        return one, two
+
+    def some(i, carry):
+        for j in range(group):
+            carry = level(i * group + j, carry)
+        return carry
+
+    carry, elimination = lax.fori_loop(0, whole, both, (first, (zero, zero, zero, zero)))
+    lax.fori_loop(whole, rounds, some, carry)
+    for j in range(whole * pairs, middle):
+        elimination = eliminate(jnp.int32(j), elimination)
+    above, ratio, below, ratio_up = elimination
     inv = 1.0 / (1.0 + above + below - above * ratio - below * ratio_up)
     inv_ref[middle] = inv
     low_ref[middle] = above * inv
@@ -237,25 +256,18 @@
 
     gy = lax.axis_index("gy")
     y_even = gy % 2 == 0
-    tail = jnp.zeros((block - levels, LANES), jnp.float32)
-    extra = jnp.zeros((block - levels - 2, LANES), jnp.float32)
     depth_f = depth.astype(jnp.float32)
+    index = lax.broadcasted_iota(jnp.int32, (block, LANES), 0)
     for i, ref in enumerate((t_ref, s_ref, v_ref)):
-        flat = ref.reshape(levels * ROWS, LANES)
+        flat = ref.reshape(block * ROWS, LANES)
+        top = flat[pl.ds(ROWS - 1, block, stride=ROWS), :]
+        low = flat[pl.ds(0, block, stride=ROWS), :]
         for own_ref, keep_top in ((own_a_ref, y_even), (own_b_ref, jnp.logical_not(y_even))):
-            top = flat[pl.ds(ROWS - 1, levels, stride=ROWS), :]
-            low = flat[pl.ds(0, levels, stride=ROWS), :]
-            end = tail
+            own = jnp.where(keep_top, top, low)
             if i == 0:
-                end = jnp.concatenate(
-                    [
-                        jnp.where(keep_top, diff[ROWS - 1 :], diff[:1]),
-                        jnp.where(keep_top, depth_f[ROWS - 1 :], depth_f[:1]),
-                        extra,
-                    ],
-                    0,
-                )
-            own_ref[i * block : (i + 1) * block] = jnp.concatenate([jnp.where(keep_top, top, low), end], 0)
+                for name, value in ((levels, diff), (levels + 1, depth_f)):
+                    own = jnp.where(index == name, jnp.where(keep_top, value[ROWS - 1 :], value[:1]), own)
+            own_ref[i * block : (i + 1) * block] = own
 
 
 def column_sums(x, open_here, axis):
@@ -297,7 +309,7 @@
 
 
 def final_kernel(
-    levels, cut, got_a, got_b, got_xa, got_xb, got_relay, own_a, own_b, own_xa, own_xb,
+    levels, cut, got_b, got_relay, got_xb, got_xa, got_a, own_a, own_b, own_xa, own_xb,
     star_t_ref, star_s_ref, inv_ref, low_ref, ratio_ref,
     out_t_ref, out_s_ref, north_ref, south_ref,
 ):
@@ -315,7 +327,13 @@
         t, s, q = (ref[i * block : (i + 1) * block] for i in range(3))
         return t, s, q, t[levels : levels + 1], t[levels + 1 : levels + 2]
 
-    flux_a = edge_flux(levels, 0, index, rows(own_a), rows(got_a), y_even, None)
+    whole = levels // ROWS * ROWS
+    t, s = got_a[:block], got_a[block : 2 * block]
+    q = jnp.concatenate(
+        [got_a[2 * block :], t[block - (levels - whole) :], jnp.zeros((block - levels, LANES), jnp.float32)], 0
+    )
+    near = t, s, q, t[levels : levels + 1], t[levels + 1 : levels + 2]
+    flux_a = edge_flux(levels, 0, index, rows(own_a), near, y_even, None)
     flux_b = edge_flux(levels, 0, index, rows(own_b), rows(got_b), y_odd, is_top)
     for i in range(2):
         north_ref[i] = -jnp.where(y_even, flux_a[i], flux_b[i])
@@ -379,13 +397,14 @@
             outs[i][k] = lower[i]
 
 
-def call(kernel, outs, operands, memory, scratch=(), flops=0, name=None):
+def call(kernel, outs, operands, memory, scratch=(), flops=0, name=None, aliases=None):
     return pl.pallas_call(
         kernel,
-        out_shape=[jax.ShapeDtypeStruct(s, jnp.float32) for s in outs],
+        out_shape=[jax.ShapeDtypeStruct(getattr(s, "shape", s), getattr(s, "dtype", jnp.float32)) for s in outs],
         in_specs=[pl.BlockSpec(memory_space=memory)] * len(operands),
         out_specs=[pl.BlockSpec(memory_space=pltpu.VMEM)] * len(outs),
         scratch_shapes=list(scratch),
+        input_output_aliases=aliases or {},
         compiler_params=pltpu.CompilerParams(vmem_limit_bytes=24 * 1024 * 1024),
         cost_estimate=pl.CostEstimate(flops=flops, bytes_accessed=4 * 1024 * 1024, transcendentals=0),
         name=name,
@@ -396,35 +415,36 @@
     levels, rows, lanes = heat.shape
     block = padded(levels)
     cube, wide, thin = (levels, rows, lanes), (3 * block, lanes), (3 * rows, lanes)
-
-    def flat(x):
-        return x.reshape(levels * rows, lanes)
-
-    def room(operands):
-        return [pltpu.VMEM(x.shape, x.dtype) for x in operands] + [pltpu.SemaphoreType.DMA((len(operands),))]
+    compact = (2 * block + levels // rows * rows, lanes)
 
     def moved(x, which):
         return lax.ppermute(x, GRID_AXES, pairs[which])
 
-    operands = tuple(pltpu.with_memory_space_constraint(x, pltpu.HBM) for x in (flat(heat), flat(salt), flat(v), flat(u), diff, depth))
-    pack_a, pack_b, pack_xb, pack_xa = call(
-        functools.partial(pack_kernel, levels), [wide, wide, thin, thin], operands, pltpu.HBM, room(operands), name="pack"
-    )
-    got_a = moved(pack_a, "a")
+    operands = tuple(pltpu.with_memory_space_constraint(x, pltpu.HBM) for x in (heat, salt, v, u, diff, depth))
+    pack_b, pack_xb, pack_xa, pack_a, heat, salt, v, u, diff, depth = call(
+        functools.partial(pack_kernel, levels), [wide, thin, thin, compact] + [(block, rows, lanes)] * 4 + [diff.shape, depth],
+        operands, pltpu.HBM, [pltpu.SemaphoreType.DMA((6,))], name="pack",
+    )
+    group = next(g for g in (5, 3, 2, 1) if levels % g == 0)
+    operands = (heat, salt, u, v, w, kap, diff, depth)
+    results = [cube] * 5 + [wide, wide]
+    early = list(
+        call(functools.partial(early_kernel, levels, group, cut), results, operands, pltpu.VMEM, name="early")
+    )
+    pack_b, early[0] = lax.optimization_barrier((pack_b, early[0]))
     got_b = moved(pack_b, "b")
     relayed = moved(pack_xb, "relay")
     got_xb = moved(pack_xb, "xb")
     got_xa = moved(pack_xa, "xa")
-    group = next(g for g in (5, 3, 2, 1) if levels % g == 0)
-    operands = tuple(pltpu.with_memory_space_constraint(x, pltpu.HBM) for x in (heat, salt, u, v, w, kap, diff, depth))
+    got_a = moved(pack_a, "a")
     star_t, star_s, inv, low, ratio, own_a, own_b = call(
-        functools.partial(inner_kernel, levels, group),
-        [cube] * 5 + [wide, wide], operands, pltpu.HBM, room(operands), flops=40_000_000, name="inner",
+        functools.partial(late_kernel, levels, group, cut), results, operands + tuple(early), pltpu.VMEM,
+        flops=1_142_000_000, name="late", aliases={8 + i: i for i in range(7)},
     )
     relayed, star_t = lax.optimization_barrier((relayed, star_t))
     got_relay = moved(relayed, "hand_on")
     operands = (
-        got_a, got_b, got_xa, got_xb, got_relay, own_a, own_b, pack_xa, pack_xb,
+        got_b, got_relay, got_xb, got_xa, got_a, own_a, own_b, pack_xa, pack_xb,
         star_t, star_s, inv, low, ratio,
     )
     return call(

time: 36.4 us -> 31.7 us (0.87)
  starting transfers between devices: 25.1 us -> 21.9 us
  Pallas kernels: 8.61 us -> 6.78 us
    ppermute x6, starting transfers between devices: 25.1 us -> 21.9 us  [moved(): return lax.ppermute(x, GRID_AXES, pairs[which])]
    pallas_call x3 -> x4, Pallas kernels: 8.61 us -> 6.78 us  [call(): pl.pallas_call(kernel, out_shape=[jax.ShapeDtypeStruct(getattr(s, 'shape'...]
  transfers between devices with their start and end apart: 6 -> 6, of which waited for: 1 -> 1; matrix products, arithmetic and copies ran while one was open for 0% -> 0% of each run, Pallas kernels for 14% -> 0%
where the time goes in v3:
time: 31.7 us; the launch traced here: 31.4 us
  starting transfers between devices  21.9 us (69%)
  Pallas kernels  6.78 us (21%)
  waiting for transfers between devices  1.98 us (6%)
  between operations  0.76 us (2%)
    ppermute x6, starting transfers between devices, moved(): return lax.ppermute(x, GRID_AXES, pairs[which])  21.9 us
    pallas_call x4, Pallas kernels, call(): pl.pallas_call(kernel, out_shape=[jax.ShapeDtypeStruct(getattr(s, 'shape'...  6.78 us
    ppermute x6, waiting for transfers between devices, moved(): return lax.ppermute(x, GRID_AXES, pairs[which])  1.98 us
  transfers between devices with their start and end apart: 6, of which 1 were waited for; matrix products, arithmetic and copies ran while one was open for 0% of the time, Pallas kernels for 0%

profile of v3, /device:TPU:7, one launch (start us, length us, event | category | flops | bytes accessed | tf_op | source)
XLA Modules:
  0.0 31.4 jit_solution(3778867329876619943)
XLA Ops:
  0.6 0.0 copy-start
  0.6 0.0 copy-start.1
  0.7 1.9 %pack.1 = (f32[240,128]{1,0:T(8,128)S(1)}, f32[24,128]{1,0:T(8,128)S(1)}, f32[24,128]{1,0:T(8,128)S(1)}, f32[232,128]{1,0:T(8,128)S(1)}, f32[80,8,128]{2,1,0:T(8...) custom-call(f32[75,8,128]{2,1,0:T(8,128)} %t_hbm.1, ...), custom_call_target="tpu_custom_call" | custom-call | bytes 4194304 | tf_op jit(solution)/shard_map/pack/pallas_call | solution.py:401
  2.6 0.0 copy-done
  2.6 0.0 copy-done.1
  2.6 3.2 %early.1 = (f32[75,8,128]{2,1,0:T(8,128)S(1)}, f32[75,8,128]{2,1,0:T(8,128)S(1)}, f32[75,8,128]{2,1,0:T(8,128)S(1)}, f32[75,8,128]{2,1,0:T(8,128)S(1)}, f32[75,8...) custom-call(f32[80,8,128]{2,1,0:T(8,128)S(1)} %get-tuple-element.31.refs_0_, ...), custom_call_target="tpu_custom_call" | custom-call | bytes 4194304 | tf_op jit(solution)/shard_map/early/pallas_call | solution.py:401
  5.8 12.7 %collective-permute-start = (f32[240,128]{1,0:T(8,128)S(1)}, f32[240,128]{1,0:T(8,128)S(1)}, u32[]{:S(2)}, u32[]{:S(2)}) collective-permute-start(f32[240,128]{1,0:T(8,128)S(1)} %get-tuple-element.38), channel_id=1, source_target_pairs={{32,64},{33,65},{34,66},{35,67},{36,68},{37,69},{38,70},{39,71},{4... | collective-permute-start | bytes 368648 | tf_op jit(solution)/shard_map/ppermute | solution.py:421
  18.6 2.1 %collective-permute-start.1 = (f32[24,128]{1,0:T(8,128)S(1)}, f32[24,128]{1,0:T(8,128)S(1)}, u32[]{:S(2)}, u32[]{:S(2)}) collective-permute-start(f32[24,128]{1,0:T(8,128)S(1)} %get-tuple-element.39.own_xb), channel_id=1, source_target_pairs={{224,223},{231,200},{232,199},{239,208},{240,207},{247,216},{248,2... | collective-permute-start | bytes 36872 | tf_op jit(solution)/shard_map/ppermute | solution.py:421
  20.7 0.7 %collective-permute-start.3 = (f32[24,128]{1,0:T(8,128)S(1)}, f32[24,128]{1,0:T(8,128)S(1)}, u32[]{:S(2)}, u32[]{:S(2)}) collective-permute-start(f32[24,128]{1,0:T(8,128)S(1)} %get-tuple-element.39.own_xb), channel_id=1, source_target_pairs={{0,31},{1,2},{2,1},{3,4},{4,3},{5,6},{6,5},{7,8},{8,7},{9,10},{10,... | collective-permute-start | bytes 36872 | tf_op jit(solution)/shard_map/ppermute | solution.py:421
  21.4 3.1 %collective-permute-start.4 = (f32[24,128]{1,0:T(8,128)S(1)}, f32[24,128]{1,0:T(8,128)S(1)}, u32[]{:S(2)}, u32[]{:S(2)}) collective-permute-start(f32[24,128]{1,0:T(8,128)S(1)} %get-tuple-element.49.own_xa), channel_id=1, source_target_pairs={{0,1},{1,0},{2,3},{3,2},{4,5},{5,4},{6,7},{7,6},{8,9},{9,8},{10,11... | collective-permute-start | bytes 36872 | tf_op jit(solution)/shard_map/ppermute | solution.py:421
  24.5 1.9 %collective-permute-start.5 = (f32[232,128]{1,0:T(8,128)S(1)}, f32[232,128]{1,0:T(8,128)S(1)}, u32[]{:S(2)}, u32[]{:S(2)}) collective-permute-start(f32[232,128]{1,0:T(8,128)S(1)} %get-tuple-element.50), channel_id=1, source_target_pairs={{0,32},{1,33},{2,34},{3,35},{4,36},{5,37},{6,38},{7,39},{8,40},{9,... | collective-permute-start | bytes 356360 | tf_op jit(solution)/shard_map/ppermute | solution.py:421
  26.5 0.0 collective-permute-done.1
  26.5 1.3 %collective-permute-start.2 = (f32[24,128]{1,0:T(8,128)S(1)}, f32[24,128]{1,0:T(8,128)S(1)}, u32[]{:S(2)}, u32[]{:S(2)}) collective-permute-start(f32[24,128]{1,0:T(8,128)S(1)} %collective-permute-done.1), channel_id=1, source_target_pairs={{192,224},{199,231},{200,232},{207,239},{208,240},{215,247},{216,2... | collective-permute-start | bytes 36872 | tf_op jit(solution)/shard_map/ppermute | solution.py:421
  27.8 0.0 collective-permute-done.3.got_xb
  27.8 0.0 collective-permute-done.4.got_xa
  27.8 2.0 %collective-permute-done.2.got_relay = f32[24,128]{1,0:T(8,128)S(1)} collective-permute-done((f32[24,128]{1,0:T(8,128)S(1)}, f32[24,128]{1,0:T(8,128)S(1)}, u32[]{:S(2)}, u32[]{:S(2)}) %collective-permute-start.2) | collective-permute-done | bytes 12320 | tf_op jit(solution)/shard_map/ppermute | solution.py:421
  29.8 0.0 collective-permute-done.5.got_a
  29.8 0.0 collective-permute-done.got_b
  29.8 1.6 %final.1 = (f32[75,8,128]{2,1,0:T(8,128)}, f32[75,8,128]{2,1,0:T(8,128)}) custom-call(f32[240,128]{1,0:T(8,128)S(1)} %collective-permute-done.got_b, f32[24,128]{1,0:T(8,128)S(1)} %collective-permute-done.2.got_relay, f32[24,128]{1,0:T(8,128)S(1)} %collective-permute-done.3.got_xb, f32[24,128]{1,0:T(8,128)S(1)} %collective-permute-done.4.got_xa, ...), custom_call_target="tpu_custom_call" | custom-call | bytes 4194304 | tf_op jit(solution)/shard_map/final/pallas_call | solution.py:401
  (1 shorter events, 0.0 us)
Async XLA Ops:
  0.6 2.0 %copy-start = (f32[75,8,128]{2,1,0:T(8,128)S(1)}, f32[75,8,128]{2,1,0:T(8,128)}, u32[]{:S(2)}) copy-start(f32[75,8,128]{2,1,0:T(8,128)} %refs_4_.3) | copy-start | bytes 921604
  0.6 2.0 %copy-start.1 = (f32[75,8,128]{2,1,0:T(8,128)S(1)}, f32[75,8,128]{2,1,0:T(8,128)}, u32[]{:S(2)}) copy-start(f32[75,8,128]{2,1,0:T(8,128)} %refs_5_.3) | copy-start | bytes 921604
  5.8 24.0 %collective-permute-start = (f32[240,128]{1,0:T(8,128)S(1)}, f32[240,128]{1,0:T(8,128)S(1)}, u32[]{:S(2)}, u32[]{:S(2)}) collective-permute-start(f32[240,128]{1,0:T(8,128)S(1)} %get-tuple-element.38), channel_id=1, source_target_pairs={{32,64},{33,65},{34,66},{35,67},{36,68},{37,69},{38,70},{39,71},{4... | collective-permute-start | bytes 368648 | tf_op jit(solution)/shard_map/ppermute | solution.py:421
  18.6 7.9 %collective-permute-start.1 = (f32[24,128]{1,0:T(8,128)S(1)}, f32[24,128]{1,0:T(8,128)S(1)}, u32[]{:S(2)}, u32[]{:S(2)}) collective-permute-start(f32[24,128]{1,0:T(8,128)S(1)} %get-tuple-element.39.own_xb), channel_id=1, source_target_pairs={{224,223},{231,200},{232,199},{239,208},{240,207},{247,216},{248,2... | collective-permute-start | bytes 36872 | tf_op jit(solution)/shard_map/ppermute | solution.py:421
  20.7 7.1 %collective-permute-start.3 = (f32[24,128]{1,0:T(8,128)S(1)}, f32[24,128]{1,0:T(8,128)S(1)}, u32[]{:S(2)}, u32[]{:S(2)}) collective-permute-start(f32[24,128]{1,0:T(8,128)S(1)} %get-tuple-element.39.own_xb), channel_id=1, source_target_pairs={{0,31},{1,2},{2,1},{3,4},{4,3},{5,6},{6,5},{7,8},{8,7},{9,10},{10,... | collective-permute-start | bytes 36872 | tf_op jit(solution)/shard_map/ppermute | solution.py:421
  21.4 6.4 %collective-permute-start.4 = (f32[24,128]{1,0:T(8,128)S(1)}, f32[24,128]{1,0:T(8,128)S(1)}, u32[]{:S(2)}, u32[]{:S(2)}) collective-permute-start(f32[24,128]{1,0:T(8,128)S(1)} %get-tuple-element.49.own_xa), channel_id=1, source_target_pairs={{0,1},{1,0},{2,3},{3,2},{4,5},{5,4},{6,7},{7,6},{8,9},{9,8},{10,11... | collective-permute-start | bytes 36872 | tf_op jit(solution)/shard_map/ppermute | solution.py:421
  24.5 5.3 %collective-permute-start.5 = (f32[232,128]{1,0:T(8,128)S(1)}, f32[232,128]{1,0:T(8,128)S(1)}, u32[]{:S(2)}, u32[]{:S(2)}) collective-permute-start(f32[232,128]{1,0:T(8,128)S(1)} %get-tuple-element.50), channel_id=1, source_target_pairs={{0,32},{1,33},{2,34},{3,35},{4,36},{5,37},{6,38},{7,39},{8,40},{9,... | collective-permute-start | bytes 356360 | tf_op jit(solution)/shard_map/ppermute | solution.py:421
  26.5 3.3 %collective-permute-start.2 = (f32[24,128]{1,0:T(8,128)S(1)}, f32[24,128]{1,0:T(8,128)S(1)}, u32[]{:S(2)}, u32[]{:S(2)}) collective-permute-start(f32[24,128]{1,0:T(8,128)S(1)} %collective-permute-done.1), channel_id=1, source_target_pairs={{192,224},{199,231},{200,232},{207,239},{208,240},{215,247},{216,2... | collective-permute-start | bytes 36872 | tf_op jit(solution)/shard_map/ppermute | solution.py:421

commit v4 on v3

--- a/solution.py
+++ b/solution.py
@@ -61,7 +61,7 @@
 
 def pack_kernel(
     levels, t_hbm, s_hbm, v_hbm, u_hbm, diff_hbm, depth_hbm,
-    b_ref, xb_ref, xa_ref, a_ref, t_ref, s_ref, v_ref, u_ref, diff_ref, depth_ref, sems,
+    b_ref, xb_ref, xa_ref, a_ref, own_xa_ref, own_xb_ref, t_ref, s_ref, v_ref, u_ref, diff_ref, depth_ref, sems,
 ):
     copies = fetch(
         (t_hbm, s_hbm, v_hbm, u_hbm, diff_hbm, depth_hbm),
@@ -100,29 +100,34 @@
             a_ref[2 * block :] = near[:whole]
             a_ref[block - (levels - whole) : block] = near[whole:levels]
 
-    def columns(ref, c, first):
-        out = jnp.zeros((ROWS, LANES), jnp.float32)
-        for k in range(levels):
-            moved = pltpu.roll(ref[k], (k - c) % LANES, 1)
-            out = jnp.where(one_lane == k, moved, out)
-        if first:
-            out = jnp.where(one_lane == levels, pltpu.roll(diff, (levels - c) % LANES, 1), out)
-            out = jnp.where(one_lane == levels + 1, pltpu.roll(depth, (levels + 1 - c) % LANES, 1), out)
-        return out
-
     def column_part(ref, i):
-        east = columns(ref, LANES - 1, i == 0)
-        west = columns(ref, 0, i == 0) if i < 2 else jnp.zeros((ROWS, LANES), jnp.float32)
-        xa_ref[i * ROWS : (i + 1) * ROWS] = jnp.where(x_even, east, west)
-        xb_ref[i * ROWS : (i + 1) * ROWS] = jnp.where(x_even, west, east)
-
+        planes = [ref[k] for k in range(levels)]
+        if i == 0:
+            planes += [diff, depth]
+        zero = jnp.zeros((ROWS, LANES), jnp.float32)
+        east, west = [zero] * 4, [zero] * 4
+        for k, plane in enumerate(planes):
+            moved = pltpu.roll(plane, k + 1, 1)
+            east[k % 4] = jnp.where(one_lane == k, moved, east[k % 4])
+            if i < 2:
+                west[k % 4] = jnp.where(one_lane == k + 1, moved, west[k % 4])
+        east = (east[0] + east[1]) + (east[2] + east[3])
+        west = (west[0] + west[1]) + (west[2] + west[3])
+        part = slice(i * ROWS, (i + 1) * ROWS)
+        own_xa_ref[part] = jnp.where(x_even, east, west)
+        own_xb_ref[part] = jnp.where(x_even, west, east)
+        east, west = pltpu.roll(east, 1, 1), pltpu.roll(west, LANES - 1, 1)
+        xa_ref[part] = jnp.where(x_even, east, west)
+        xb_ref[part] = jnp.where(x_even, west, east)
+
+    copies[0].wait()
+    copies[1].wait()
     for i, ref in enumerate((t_ref, s_ref)):
-        copies[i].wait()
         row_part(ref, i)
         column_part(ref, i)
     copies[2].wait()
+    copies[3].wait()
     row_part(v_ref, 2)
-    copies[3].wait()
     column_part(u_ref, 2)
 
 
@@ -138,7 +143,7 @@
 
 
 def late_kernel(levels, group, cut, *refs):
-    n_in, n_out = 8, 7
+    n_in, n_out = 10, 9
     ins, outs = refs[:n_in], refs[n_in + n_out :]
 
     @pl.when(jnp.logical_not(starts_early(lax.axis_index("gy"), lax.axis_index("gx"), cut)))
@@ -148,7 +153,8 @@
 
 def inner(
     levels, group, t_ref, s_ref, u_ref, v_ref, w_ref, kap_ref, diff_ref, depth_ref,
-    star_t_ref, star_s_ref, inv_ref, low_ref, ratio_ref, own_a_ref, own_b_ref,
+    own_xa_ref, own_xb_ref, star_t_ref, star_s_ref, inv_ref, low_ref, ratio_ref, own_a_ref, own_b_ref,
+    side_xa_ref, side_xb_ref,
 ):
     block = padded(levels)
     depth = depth_ref[...]
@@ -258,16 +264,31 @@
     y_even = gy % 2 == 0
     depth_f = depth.astype(jnp.float32)
     index = lax.broadcasted_iota(jnp.int32, (block, LANES), 0)
-    for i, ref in enumerate((t_ref, s_ref, v_ref)):
-        flat = ref.reshape(block * ROWS, LANES)
-        top = flat[pl.ds(ROWS - 1, block, stride=ROWS), :]
-        low = flat[pl.ds(0, block, stride=ROWS), :]
-        for own_ref, keep_top in ((own_a_ref, y_even), (own_b_ref, jnp.logical_not(y_even))):
-            own = jnp.where(keep_top, top, low)
+    heights = level_heights(index, levels)
+    flats = [ref.reshape(block * ROWS, LANES) for ref in (t_ref, s_ref, v_ref)]
+    tops = [flat[pl.ds(ROWS - 1, block, stride=ROWS), :] for flat in flats]
+    lows = [flat[pl.ds(0, block, stride=ROWS), :] for flat in flats]
+    for own_ref, keep_top in ((own_a_ref, y_even), (own_b_ref, jnp.logical_not(y_even))):
+        t, s, q = (jnp.where(keep_top, top, low) for top, low in zip(tops, lows))
+        edge_diff, edge_depth = (
+            jnp.where(keep_top, value[ROWS - 1 :], value[:1]) for value in (diff, depth_f)
+        )
+        for i, field in enumerate(side(t, s, edge_depth, index.astype(jnp.float32), heights, 0) + (q,)):
             if i == 0:
-                for name, value in ((levels, diff), (levels + 1, depth_f)):
-                    own = jnp.where(index == name, jnp.where(keep_top, value[ROWS - 1 :], value[:1]), own)
-            own_ref[i * block : (i + 1) * block] = own
+                field = jnp.where(index == levels, edge_diff, jnp.where(index == levels + 1, edge_depth, field))
+            own_ref[i * block : (i + 1) * block] = field
+    x_even = lax.axis_index("gx") % 2 == 0
+    for own_ref, side_ref, own_left in ((own_xa_ref, side_xa_ref, x_even), (own_xb_ref, side_xb_ref, jnp.logical_not(x_even))):
+        t, s, q = (own_ref[i * ROWS : (i + 1) * ROWS] for i in range(3))
+        ahead = jnp.where(own_left, 0, 1)
+        values = column_side(t, s, levels, ahead) + (q,) + edge_values(t, levels, ahead)
+        for i, value in enumerate(values):
+            side_ref[i * ROWS : (i + 1) * ROWS] = value
+
+
+def level_heights(index, levels):
+    part = (index.astype(jnp.float32) + 0.5) / levels
+    return bottom_depth * (part * part)
 
 
 def column_sums(x, open_here, axis):
@@ -289,86 +310,124 @@
     )
 
 
-def edge_flux(levels, axis, index, own, got, own_left, fold):
-    part = (index.astype(jnp.float32) + 0.5) / levels
-    heights = bottom_depth * (part * part)
-    left = [jnp.where(own_left, o, g) for o, g in zip(own, got)]
-    right = [jnp.where(own_left, g, o) for o, g in zip(own, got)]
-    speed = left[2]
+def edge_values(t, levels, ahead):
+    one, two, three = (t[:, levels + i : levels + i + 1] for i in range(3))
+    first, second = jnp.where(ahead == 0, one, two), jnp.where(ahead == 0, two, three)
+    return jnp.broadcast_to(first, t.shape), jnp.broadcast_to(second, t.shape)
+
+
+def column_side(t, s, levels, ahead):
+    depth = edge_values(t, levels, ahead)[1]
+    level = lax.broadcasted_iota(jnp.int32, t.shape, 1) - ahead
+    here, over, under = (
+        (
+            pltpu.roll(t, shift, 1) if shift else t,
+            pltpu.roll(s, shift, 1) if shift else s,
+            level_heights(level - move, levels),
+        )
+        for shift, move in ((0, 0), (1, 1), (LANES - 1, -1))
+    )
+    level = level.astype(jnp.float32)
+    open_here = jnp.logical_and(level >= 1.0, level < depth)
+    open_under = level + 1.0 < depth
+    here, over, under = (x[:2] + (density(*x),) for x in (here, over, under))
+    sums = tuple(
+        jnp.where(open_here, h - o, 0.0) + jnp.where(open_under, u - h, 0.0) for h, o, u in zip(here, over, under)
+    )
+    return here + sums
+
+
+def edge_change(own, got, own_speed, got_speed, diffus, wet, own_left, fold=None):
+    sign = jnp.where(own_left, 1.0, -1.0)
+    speed = jnp.where(own_left, own_speed, got_speed)
     if fold is not None:
-        speed = jnp.where(fold, 0.5 * (own[2] - got[2]), speed)
-    wet = index.astype(jnp.float32) < jnp.minimum(left[4], right[4])
-    level = index.astype(jnp.float32)
-    return face_flux(
-        speed,
-        0.5 * (left[3] + right[3]),
-        wet,
-        side(left[0], left[1], left[4], level, heights, axis),
-        side(right[0], right[1], right[4], level, heights, axis),
-    )
+        speed = jnp.where(fold, 0.5 * (own_speed - got_speed), speed)
+    outward = sign * speed
+    steps = jnp.maximum(own[5] + got[5], 0.0) + 4.0 * strat_offset
+    quarter = jnp.clip(quotient(got[2] - own[2], steps), -0.25 * slope_limit, 0.25 * slope_limit)
+    leaves = outward > 0.0
+
+    def one(i):
+        carried = outward * jnp.where(leaves, own[i], got[i])
+        mixed = diffus * (got[i] - own[i] - quarter * (own[3 + i] + got[3 + i]))
+        return jnp.where(wet, mixed - carried, 0.0)
+
+    return one(0), one(1)
 
 
 def final_kernel(
-    levels, cut, got_b, got_relay, got_xb, got_xa, got_a, own_a, own_b, own_xa, own_xb,
+    levels, cut, got_direct, got_b, got_relay, got_xb, got_xa, got_a, own_a, own_b, side_xa, side_xb, _,
     star_t_ref, star_s_ref, inv_ref, low_ref, ratio_ref,
-    out_t_ref, out_s_ref, north_ref, south_ref,
+    out_t_ref, out_s_ref, change_ref,
 ):
     block = padded(levels)
     gy, gx = lax.axis_index("gy"), lax.axis_index("gx")
     y_even, x_even = gy % 2 == 0, gx % 2 == 0
     y_odd, x_odd = jnp.logical_not(y_even), jnp.logical_not(x_even)
     is_top = gy == lax.axis_size("gy") - 1
+    corner = jnp.logical_and(is_far_row(gy), is_far_column(gx, cut))
+    straight = jnp.logical_and(gy < lax.axis_size("gy") // 2, gx % cut == 0)
 
     index = lax.broadcasted_iota(jnp.int32, (block, LANES), 0)
-
-    corner = jnp.logical_and(is_far_row(gy), is_far_column(gx, cut))
-
-    def rows(ref):
-        t, s, q = (ref[i * block : (i + 1) * block] for i in range(3))
-        return t, s, q, t[levels : levels + 1], t[levels + 1 : levels + 2]
+    height = level_heights(index, levels)
+    level = index.astype(jnp.float32)
+
+    def row_change(place, own_ref, t, s, q, own_left, fold):
+        own = [own_ref[i * block : (i + 1) * block] for i in range(7)]
+        diffus, depth = t[levels : levels + 1], t[levels + 1 : levels + 2]
+        own_diffus, own_depth = own[0][levels : levels + 1], own[0][levels + 1 : levels + 2]
+        changes = edge_change(
+            own, side(t, s, depth, level, height, 0), own[6], q,
+            0.5 * (own_diffus + diffus), level < jnp.minimum(own_depth, depth), own_left, fold,
+        )
+        for i in range(2):
+            change_ref[place, i] = changes[i]
 
     whole = levels // ROWS * ROWS
     t, s = got_a[:block], got_a[block : 2 * block]
     q = jnp.concatenate(
         [got_a[2 * block :], t[block - (levels - whole) :], jnp.zeros((block - levels, LANES), jnp.float32)], 0
     )
-    near = t, s, q, t[levels : levels + 1], t[levels + 1 : levels + 2]
-    flux_a = edge_flux(levels, 0, index, rows(own_a), near, y_even, None)
-    flux_b = edge_flux(levels, 0, index, rows(own_b), rows(got_b), y_odd, is_top)
-    for i in range(2):
-        north_ref[i] = -jnp.where(y_even, flux_a[i], flux_b[i])
-        south_ref[i] = jnp.where(y_even, flux_b[i], flux_a[i])
+    row_change(0, own_a, t, s, q, y_even, None)
+    row_change(1, own_b, *(got_b[i * block : (i + 1) * block] for i in range(3)), y_odd, is_top)
 
     lane = lax.broadcasted_iota(jnp.int32, (ROWS, LANES), 1)
     row = lax.broadcasted_iota(jnp.int32, (ROWS, LANES), 0)
 
-    def cols(ref, other=None):
-        t, s, q = (
-            ref[i * ROWS : (i + 1) * ROWS]
-            if other is None
-            else jnp.where(corner, other[i * ROWS : (i + 1) * ROWS], ref[i * ROWS : (i + 1) * ROWS])
-            for i in range(3)
+    def column_change(side_ref, got, own_left):
+        own = [side_ref[i * ROWS : (i + 1) * ROWS] for i in range(9)]
+        ahead = jnp.where(own_left, 0, 1)
+        diffus, depth = edge_values(got[0], levels, ahead)
+        level = (lane - ahead).astype(jnp.float32)
+        wet = jnp.logical_and(level >= 0.0, level < jnp.minimum(own[8], depth))
+        return edge_change(
+            own, column_side(got[0], got[1], levels, ahead), own[6], got[2], 0.5 * (own[7] + diffus), wet, own_left
         )
-        return t, s, q, t[:, levels : levels + 1], t[:, levels + 1 : levels + 2]
-
-    flux_xa = edge_flux(levels, 1, lane, cols(own_xa), cols(got_xa), x_even, None)
-    flux_xb = edge_flux(levels, 1, lane, cols(own_xb), cols(got_xb, got_relay), x_odd, None)
-    east = [-jnp.where(x_even, flux_xa[i], flux_xb[i]) for i in range(2)]
-    west = [jnp.where(x_even, flux_xb[i], flux_xa[i]) for i in range(2)]
-    last_lane, first_lane = lane == LANES - 1, lane == 0
-    last_row, first_row = row == ROWS - 1, row == 0
+
+    def thirds(ref):
+        return [ref[i * ROWS : (i + 1) * ROWS] for i in range(3)]
+
+    change_xa = column_change(side_xa, thirds(got_xa), x_even)
+    from_xb = [
+        jnp.where(corner, jnp.where(straight, a, b), c)
+        for a, b, c in zip(thirds(got_direct), thirds(got_relay), thirds(got_xb))
+    ]
+    change_xb = column_change(side_xb, from_xb, x_odd)
+    even_lane = lane % 2 == 0
+    paired = []
+    for i in range(2):
+        last = jnp.where(x_even, change_xa[i], change_xb[i])
+        first = jnp.where(x_even, change_xb[i], change_xa[i])
+        paired.append((jnp.where(even_lane, last, first), jnp.where(even_lane, first, last)))
+    at_side = jnp.logical_or(lane == 0, lane == LANES - 1)
+    row_a = row == jnp.where(y_even, ROWS - 1, 0)
+    row_b = row == jnp.where(y_even, 0, ROWS - 1)
 
     def right_side(i, k):
         ref = (star_t_ref, star_s_ref)[i]
-        x_part = jnp.where(
-            last_lane,
-            pltpu.roll(east[i], (LANES - 1 - k) % LANES, 1),
-            jnp.where(first_lane, pltpu.roll(west[i], (-k) % LANES, 1), 0.0),
-        )
+        x_part = jnp.where(at_side, pltpu.roll(paired[i][k % 2], (LANES - 1 - k) % LANES, 1), 0.0)
         y_part = jnp.where(
-            last_row,
-            north_ref[i, k : k + 1, :],
-            jnp.where(first_row, south_ref[i, k : k + 1, :], 0.0),
+            row_a, change_ref[0, i, k : k + 1, :], jnp.where(row_b, change_ref[1, i, k : k + 1, :], 0.0)
         )
         return (ref[k] + (x_part + y_part)) * inv_ref[k]
 
@@ -421,35 +480,37 @@
         return lax.ppermute(x, GRID_AXES, pairs[which])
 
     operands = tuple(pltpu.with_memory_space_constraint(x, pltpu.HBM) for x in (heat, salt, v, u, diff, depth))
-    pack_b, pack_xb, pack_xa, pack_a, heat, salt, v, u, diff, depth = call(
-        functools.partial(pack_kernel, levels), [wide, thin, thin, compact] + [(block, rows, lanes)] * 4 + [diff.shape, depth],
+    pack_b, pack_xb, pack_xa, pack_a, own_xa, own_xb, heat, salt, v, u, diff, depth = call(
+        functools.partial(pack_kernel, levels), [wide, thin, thin, compact, thin, thin] + [(block, rows, lanes)] * 4 + [diff.shape, depth],
         operands, pltpu.HBM, [pltpu.SemaphoreType.DMA((6,))], name="pack",
     )
     group = next(g for g in (5, 3, 2, 1) if levels % g == 0)
-    operands = (heat, salt, u, v, w, kap, diff, depth)
-    results = [cube] * 5 + [wide, wide]
+    operands = (heat, salt, u, v, w, kap, diff, depth, own_xa, own_xb)
+    results = [cube] * 5 + [(7 * block, lanes)] * 2 + [(9 * rows, lanes)] * 2
     early = list(
         call(functools.partial(early_kernel, levels, group, cut), results, operands, pltpu.VMEM, name="early")
     )
+    direct = moved(pack_xb, "direct")
     pack_b, early[0] = lax.optimization_barrier((pack_b, early[0]))
     got_b = moved(pack_b, "b")
     relayed = moved(pack_xb, "relay")
     got_xb = moved(pack_xb, "xb")
     got_xa = moved(pack_xa, "xa")
     got_a = moved(pack_a, "a")
-    star_t, star_s, inv, low, ratio, own_a, own_b = call(
+    direct, early[0] = lax.optimization_barrier((direct, early[0]))
+    star_t, star_s, inv, low, ratio, own_a, own_b, side_xa, side_xb = call(
         functools.partial(late_kernel, levels, group, cut), results, operands + tuple(early), pltpu.VMEM,
-        flops=1_142_000_000, name="late", aliases={8 + i: i for i in range(7)},
+        flops=1_145_000_000, name="late", aliases={10 + i: i for i in range(9)},
     )
     relayed, star_t = lax.optimization_barrier((relayed, star_t))
     got_relay = moved(relayed, "hand_on")
     operands = (
-        got_b, got_relay, got_xb, got_xa, got_a, own_a, own_b, pack_xa, pack_xb,
+        direct, got_b, got_relay, got_xb, got_xa, got_a, own_a, own_b, side_xa, side_xb, pack_xa,
         star_t, star_s, inv, low, ratio,
     )
     return call(
         functools.partial(final_kernel, levels, cut),
-        [cube] * 2, operands, pltpu.VMEM, [pltpu.VMEM((2, block, lanes), jnp.float32)] * 2, name="final",
+        [cube] * 2, operands, pltpu.VMEM, [pltpu.VMEM((2, 2, block, lanes), jnp.float32)], name="final",
     )
 
 
@@ -482,8 +543,9 @@
         "b": [(at(y, x), at(to_y, to_x)) for y, to_y, x, to_x in second],
         "xa": [(at(y, x), at(y, x ^ 1)) for y in range(ny) for x in range(nx)],
         "xb": [(at(y, x), at(y, beside(x))) for y in range(ny) for x in range(nx) if (y, x) not in corners],
-        "relay": [(at(y, x), at(y ^ 1, beside(x))) for y, x in corners],
-        "hand_on": [(at(y ^ 1, x), at(y, x)) for y, x in corners],
+        "direct": [(at(y, x), at(y, beside(x))) for y, x in corners if y < ny // 2 and x % cut == cut - 1],
+        "relay": [(at(y, x), at(y ^ 1, beside(x))) for y, x in corners if y >= ny // 2 or x % cut == 0],
+        "hand_on": [(at(y ^ 1, x), at(y, x)) for y, x in corners if y >= ny // 2 or x % cut == cut - 1],
     }
     cube = P(None, "gy", "gx")
     sheet = P("gy", "gx")

time: 31.7 us -> 30.7 us (0.968)
  the two profiles are of different devices: /device:TPU:7 before, /device:TPU:1 now
where the time goes in v4:
time: 30.7 us; the launch traced here: 30.4 us
  starting transfers between devices  22.3 us (73%)
  Pallas kernels  6.75 us (22%)
  between operations  0.77 us (3%)
  waiting for transfers between devices  0.58 us (2%)
    ppermute x7, starting transfers between devices, moved(): return lax.ppermute(x, GRID_AXES, pairs[which])  22.3 us
    pallas_call x4, Pallas kernels, call(): pl.pallas_call(kernel, out_shape=[jax.ShapeDtypeStruct(getattr(s, 'shape'...  6.75 us
  transfers between devices with their start and end apart: 7, of which 2 were waited for; matrix products, arithmetic and copies ran while one was open for 0% of the time, Pallas kernels for 11%

profile of v4, /device:TPU:1, one launch (start us, length us, event | category | flops | bytes accessed | tf_op | source)
XLA Modules:
  0.0 30.4 jit_solution(11188510827213267997)
XLA Ops:
  0.6 0.0 copy-start
  0.6 0.0 copy-start.1
  0.7 1.8 %pack.1 = (f32[240,128]{1,0:T(8,128)S(1)}, f32[24,128]{1,0:T(8,128)S(1)}, f32[24,128]{1,0:T(8,128)S(1)}, f32[232,128]{1,0:T(8,128)S(1)}, f32[24,128]{1,0:T(8,128...) custom-call(f32[75,8,128]{2,1,0:T(8,128)} %t_hbm.1, ...), custom_call_target="tpu_custom_call" | custom-call | bytes 4194304 | tf_op jit(solution)/shard_map/pack/pallas_call | solution.py:460
  2.5 0.7 %collective-permute-start = (f32[24,128]{1,0:T(8,128)S(1)}, f32[24,128]{1,0:T(8,128)S(1)}, u32[]{:S(2)}, u32[]{:S(2)}) collective-permute-start(f32[24,128]{1,0:T(8,128)S(1)} %get-tuple-element.38), channel_id=1, source_target_pairs={{231,232},{239,240},{247,248},{255,224}} | collective-permute-start | bytes 36872 | tf_op jit(solution)/shard_map/ppermute | solution.py:480
  3.2 0.0 copy-done
  3.2 0.0 copy-done.1
  3.2 3.4 %early.1 = (f32[75,8,128]{2,1,0:T(8,128)S(1)}, f32[75,8,128]{2,1,0:T(8,128)S(1)}, f32[75,8,128]{2,1,0:T(8,128)S(1)}, f32[75,8,128]{2,1,0:T(8,128)S(1)}, f32[75,8...) custom-call(f32[80,8,128]{2,1,0:T(8,128)S(1)} %get-tuple-element.40., ...), custom_call_target="tpu_custom_call" | custom-call | bytes 4194304 | tf_op jit(solution)/shard_map/early/pallas_call | solution.py:460
  6.6 4.5 %collective-permute-start.1 = (f32[240,128]{1,0:T(8,128)S(1)}, f32[240,128]{1,0:T(8,128)S(1)}, u32[]{:S(2)}, u32[]{:S(2)}) collective-permute-start(f32[240,128]{1,0:T(8,128)S(1)} %get-tuple-element.51), channel_id=1, source_target_pairs={{32,64},{33,65},{34,66},{35,67},{36,68},{37,69},{38,70},{39,71},{4... | collective-permute-start | bytes 368648 | tf_op jit(solution)/shard_map/ppermute | solution.py:480
  11.1 0.7 %collective-permute-start.2 = (f32[24,128]{1,0:T(8,128)S(1)}, f32[24,128]{1,0:T(8,128)S(1)}, u32[]{:S(2)}, u32[]{:S(2)}) collective-permute-start(f32[24,128]{1,0:T(8,128)S(1)} %get-tuple-element.38), channel_id=1, source_target_pairs={{224,223},{232,199},{240,207},{248,215},{256,319},{263,296},{264,2... | collective-permute-start | bytes 36872 | tf_op jit(solution)/shard_map/ppermute | solution.py:480
  11.8 12.0 %collective-permute-start.4 = (f32[24,128]{1,0:T(8,128)S(1)}, f32[24,128]{1,0:T(8,128)S(1)}, u32[]{:S(2)}, u32[]{:S(2)}) collective-permute-start(f32[24,128]{1,0:T(8,128)S(1)} %get-tuple-element.38), channel_id=1, source_target_pairs={{0,31},{1,2},{2,1},{3,4},{4,3},{5,6},{6,5},{7,8},{8,7},{9,10},{10,... | collective-permute-start | bytes 36872 | tf_op jit(solution)/shard_map/ppermute | solution.py:480
  23.7 1.9 %collective-permute-start.5 = (f32[24,128]{1,0:T(8,128)S(1)}, f32[24,128]{1,0:T(8,128)S(1)}, u32[]{:S(2)}, u32[]{:S(2)}) collective-permute-start(f32[24,128]{1,0:T(8,128)S(1)} %get-tuple-element.63._), channel_id=1, source_target_pairs={{0,1},{1,0},{2,3},{3,2},{4,5},{5,4},{6,7},{7,6},{8,9},{9,8},{10,11... | collective-permute-start | bytes 36872 | tf_op jit(solution)/shard_map/ppermute | solution.py:480
  25.7 0.0 collective-permute-done.got_direct
  25.7 1.9 %collective-permute-start.6 = (f32[232,128]{1,0:T(8,128)S(1)}, f32[232,128]{1,0:T(8,128)S(1)}, u32[]{:S(2)}, u32[]{:S(2)}) collective-permute-start(f32[232,128]{1,0:T(8,128)S(1)} %get-tuple-element.64), channel_id=1, source_target_pairs={{0,32},{1,33},{2,34},{3,35},{4,36},{5,37},{6,38},{7,39},{8,40},{9,... | collective-permute-start | bytes 356360 | tf_op jit(solution)/shard_map/ppermute | solution.py:480
  27.7 0.0 collective-permute-done.2
  27.7 0.7 %collective-permute-start.3 = (f32[24,128]{1,0:T(8,128)S(1)}, f32[24,128]{1,0:T(8,128)S(1)}, u32[]{:S(2)}, u32[]{:S(2)}) collective-permute-start(f32[24,128]{1,0:T(8,128)S(1)} %collective-permute-done.2), channel_id=1, source_target_pairs={{199,231},{207,239},{215,247},{223,255},{288,256},{295,263},{296,2... | collective-permute-start | bytes 36872 | tf_op jit(solution)/shard_map/ppermute | solution.py:480
  28.3 0.0 collective-permute-done.4.got_xb
  28.3 0.1 collective-permute-done.5.got_xa
  28.5 0.0 collective-permute-done.3.got_relay
  28.5 0.4 %collective-permute-done.6.got_a = f32[232,128]{1,0:T(8,128)S(1)} collective-permute-done((f32[232,128]{1,0:T(8,128)S(1)}, f32[232,128]{1,0:T(8,128)S(1)}, u32[]{:S(2)}, u32[]{:S(2)}) %collective-permute-start.6) | collective-permute-done | bytes 118816 | tf_op jit(solution)/shard_map/ppermute | solution.py:480
  28.9 0.0 collective-permute-done.1.got_b
  28.9 1.5 %final.1 = (f32[75,8,128]{2,1,0:T(8,128)}, f32[75,8,128]{2,1,0:T(8,128)}) custom-call(f32[24,128]{1,0:T(8,128)S(1)} %collective-permute-done.got_direct, f32[240,128]{1,0:T(8,128)S(1)} %collective-permute-done.1.got_b, f32[24,128]{1,0:T(8,128)S(1)} %collective-permute-done.3.got_relay, f32[24,128]{1,0:T(8,128)S(1)} %collective-permute-done.4.got_xb, ...), custom_call_target="tpu_custom_call" | custom-call | bytes 4194304 | tf_op jit(solution)/shard_map/final/pallas_call | solution.py:460
  (1 shorter events, 0.0 us)
Async XLA Ops:
  0.6 2.5 %copy-start = (f32[75,8,128]{2,1,0:T(8,128)S(1)}, f32[75,8,128]{2,1,0:T(8,128)}, u32[]{:S(2)}) copy-start(f32[75,8,128]{2,1,0:T(8,128)} %refs_4_.3) | copy-start | bytes 921604
  0.6 2.5 %copy-start.1 = (f32[75,8,128]{2,1,0:T(8,128)S(1)}, f32[75,8,128]{2,1,0:T(8,128)}, u32[]{:S(2)}) copy-start(f32[75,8,128]{2,1,0:T(8,128)} %refs_5_.3) | copy-start | bytes 921604
  2.5 23.2 %collective-permute-start = (f32[24,128]{1,0:T(8,128)S(1)}, f32[24,128]{1,0:T(8,128)S(1)}, u32[]{:S(2)}, u32[]{:S(2)}) collective-permute-start(f32[24,128]{1,0:T(8,128)S(1)} %get-tuple-element.38), channel_id=1, source_target_pairs={{231,232},{239,240},{247,248},{255,224}} | collective-permute-start | bytes 36872 | tf_op jit(solution)/shard_map/ppermute | solution.py:480
  6.6 22.3 %collective-permute-start.1 = (f32[240,128]{1,0:T(8,128)S(1)}, f32[240,128]{1,0:T(8,128)S(1)}, u32[]{:S(2)}, u32[]{:S(2)}) collective-permute-start(f32[240,128]{1,0:T(8,128)S(1)} %get-tuple-element.51), channel_id=1, source_target_pairs={{32,64},{33,65},{34,66},{35,67},{36,68},{37,69},{38,70},{39,71},{4... | collective-permute-start | bytes 368648 | tf_op jit(solution)/shard_map/ppermute | solution.py:480
  11.1 16.5 %collective-permute-start.2 = (f32[24,128]{1,0:T(8,128)S(1)}, f32[24,128]{1,0:T(8,128)S(1)}, u32[]{:S(2)}, u32[]{:S(2)}) collective-permute-start(f32[24,128]{1,0:T(8,128)S(1)} %get-tuple-element.38), channel_id=1, source_target_pairs={{224,223},{232,199},{240,207},{248,215},{256,319},{263,296},{264,2... | collective-permute-start | bytes 36872 | tf_op jit(solution)/shard_map/ppermute | solution.py:480
  11.8 16.6 %collective-permute-start.4 = (f32[24,128]{1,0:T(8,128)S(1)}, f32[24,128]{1,0:T(8,128)S(1)}, u32[]{:S(2)}, u32[]{:S(2)}) collective-permute-start(f32[24,128]{1,0:T(8,128)S(1)} %get-tuple-element.38), channel_id=1, source_target_pairs={{0,31},{1,2},{2,1},{3,4},{4,3},{5,6},{6,5},{7,8},{8,7},{9,10},{10,... | collective-permute-start | bytes 36872 | tf_op jit(solution)/shard_map/ppermute | solution.py:480
  23.7 4.7 %collective-permute-start.5 = (f32[24,128]{1,0:T(8,128)S(1)}, f32[24,128]{1,0:T(8,128)S(1)}, u32[]{:S(2)}, u32[]{:S(2)}) collective-permute-start(f32[24,128]{1,0:T(8,128)S(1)} %get-tuple-element.63._), channel_id=1, source_target_pairs={{0,1},{1,0},{2,3},{3,2},{4,5},{5,4},{6,7},{7,6},{8,9},{9,8},{10,11... | collective-permute-start | bytes 36872 | tf_op jit(solution)/shard_map/ppermute | solution.py:480
  25.7 3.2 %collective-permute-start.6 = (f32[232,128]{1,0:T(8,128)S(1)}, f32[232,128]{1,0:T(8,128)S(1)}, u32[]{:S(2)}, u32[]{:S(2)}) collective-permute-start(f32[232,128]{1,0:T(8,128)S(1)} %get-tuple-element.64), channel_id=1, source_target_pairs={{0,32},{1,33},{2,34},{3,35},{4,36},{5,37},{6,38},{7,39},{8,40},{9,... | collective-permute-start | bytes 356360 | tf_op jit(solution)/shard_map/ppermute | solution.py:480
  27.7 0.8 %collective-permute-start.3 = (f32[24,128]{1,0:T(8,128)S(1)}, f32[24,128]{1,0:T(8,128)S(1)}, u32[]{:S(2)}, u32[]{:S(2)}) collective-permute-start(f32[24,128]{1,0:T(8,128)S(1)} %collective-permute-done.2), channel_id=1, source_target_pairs={{199,231},{207,239},{215,247},{223,255},{288,256},{295,263},{296,2... | collective-permute-start | bytes 36872 | tf_op jit(solution)/shard_map/ppermute | solution.py:480

commit v5 on v4

--- a/solution.py
+++ b/solution.py
@@ -61,7 +61,7 @@
 
 def pack_kernel(
     levels, t_hbm, s_hbm, v_hbm, u_hbm, diff_hbm, depth_hbm,
-    b_ref, xb_ref, xa_ref, a_ref, own_xa_ref, own_xb_ref, t_ref, s_ref, v_ref, u_ref, diff_ref, depth_ref, sems,
+    b_ref, xb_ref, xa_ref, a_ref, own_xa_ref, own_xb_ref, first_ref, t_ref, s_ref, v_ref, u_ref, diff_ref, depth_ref, sems,
 ):
     copies = fetch(
         (t_hbm, s_hbm, v_hbm, u_hbm, diff_hbm, depth_hbm),
@@ -117,8 +117,10 @@
         own_xa_ref[part] = jnp.where(x_even, east, west)
         own_xb_ref[part] = jnp.where(x_even, west, east)
         east, west = pltpu.roll(east, 1, 1), pltpu.roll(west, LANES - 1, 1)
-        xa_ref[part] = jnp.where(x_even, east, west)
-        xb_ref[part] = jnp.where(x_even, west, east)
+        xa, xb = jnp.where(x_even, east, west), jnp.where(x_even, west, east)
+        xa_ref[part] = xa
+        xb_ref[part] = xb
+        first_ref[part] = jnp.where(below_middle(gy), xb, xa)
 
     copies[0].wait()
     copies[1].wait()
@@ -129,6 +131,10 @@
     copies[3].wait()
     row_part(v_ref, 2)
     column_part(u_ref, 2)
+
+
+def below_middle(gy):
+    return gy == lax.axis_size("gy") // 2 - 1
 
 
 def starts_early(gy, gx, cut):
@@ -234,8 +240,8 @@
         return under, ratio, over, ratio_up
 
     rounds = levels // group
-    pairs = -(-middle // rounds)
-    whole = middle // pairs
+    pairs = min((middle // rounds, -(-middle // rounds)), key=lambda p: middle - min(rounds, middle // p) * p)
+    whole = min(rounds, middle // pairs)
 
     def both(i, carry):
         one, two = carry
@@ -356,7 +362,7 @@
 
 
 def final_kernel(
-    levels, cut, got_direct, got_b, got_relay, got_xb, got_xa, got_a, own_a, own_b, side_xa, side_xb, _,
+    levels, cut, got_first, got_b, got_relay, got_xb, got_xa, got_a, own_a, own_b, side_xa, side_xb, _,
     star_t_ref, star_s_ref, inv_ref, low_ref, ratio_ref,
     out_t_ref, out_s_ref, change_ref,
 ):
@@ -366,7 +372,8 @@
     y_odd, x_odd = jnp.logical_not(y_even), jnp.logical_not(x_even)
     is_top = gy == lax.axis_size("gy") - 1
     corner = jnp.logical_and(is_far_row(gy), is_far_column(gx, cut))
-    straight = jnp.logical_and(gy < lax.axis_size("gy") // 2, gx % cut == 0)
+    xb_first = jnp.logical_and(below_middle(gy), gx % cut < 3)
+    xa_first = jnp.logical_and(starts_early(gy, gx, cut), jnp.logical_not(below_middle(gy)))
 
     index = lax.broadcasted_iota(jnp.int32, (block, LANES), 0)
     height = level_heights(index, levels)
@@ -407,11 +414,12 @@
     def thirds(ref):
         return [ref[i * ROWS : (i + 1) * ROWS] for i in range(3)]
 
-    change_xa = column_change(side_xa, thirds(got_xa), x_even)
+    first, relay = thirds(got_first), thirds(got_relay)
+    from_xa = [jnp.where(xa_first, a, b) for a, b in zip(first, thirds(got_xa))]
     from_xb = [
-        jnp.where(corner, jnp.where(straight, a, b), c)
-        for a, b, c in zip(thirds(got_direct), thirds(got_relay), thirds(got_xb))
+        jnp.where(xb_first, a, jnp.where(corner, b, c)) for a, b, c in zip(first, relay, thirds(got_xb))
     ]
+    change_xa = column_change(side_xa, from_xa, x_even)
     change_xb = column_change(side_xb, from_xb, x_odd)
     even_lane = lane % 2 == 0
     paired = []
@@ -480,24 +488,24 @@
         return lax.ppermute(x, GRID_AXES, pairs[which])
 
     operands = tuple(pltpu.with_memory_space_constraint(x, pltpu.HBM) for x in (heat, salt, v, u, diff, depth))
-    pack_b, pack_xb, pack_xa, pack_a, own_xa, own_xb, heat, salt, v, u, diff, depth = call(
-        functools.partial(pack_kernel, levels), [wide, thin, thin, compact, thin, thin] + [(block, rows, lanes)] * 4 + [diff.shape, depth],
+    pack_b, pack_xb, pack_xa, pack_a, own_xa, own_xb, pack_first, heat, salt, v, u, diff, depth = call(
+        functools.partial(pack_kernel, levels), [wide, thin, thin, compact, thin, thin, thin] + [(block, rows, lanes)] * 4 + [diff.shape, depth],
         operands, pltpu.HBM, [pltpu.SemaphoreType.DMA((6,))], name="pack",
     )
-    group = next(g for g in (5, 3, 2, 1) if levels % g == 0)
+    group = next(g for g in (15, 5, 3, 2, 1) if levels % g == 0)
     operands = (heat, salt, u, v, w, kap, diff, depth, own_xa, own_xb)
     results = [cube] * 5 + [(7 * block, lanes)] * 2 + [(9 * rows, lanes)] * 2
     early = list(
         call(functools.partial(early_kernel, levels, group, cut), results, operands, pltpu.VMEM, name="early")
     )
-    direct = moved(pack_xb, "direct")
+    got_first = moved(pack_first, "first")
     pack_b, early[0] = lax.optimization_barrier((pack_b, early[0]))
     got_b = moved(pack_b, "b")
     relayed = moved(pack_xb, "relay")
     got_xb = moved(pack_xb, "xb")
     got_xa = moved(pack_xa, "xa")
     got_a = moved(pack_a, "a")
-    direct, early[0] = lax.optimization_barrier((direct, early[0]))
+    got_first, early[0] = lax.optimization_barrier((got_first, early[0]))
     star_t, star_s, inv, low, ratio, own_a, own_b, side_xa, side_xb = call(
         functools.partial(late_kernel, levels, group, cut), results, operands + tuple(early), pltpu.VMEM,
         flops=1_145_000_000, name="late", aliases={10 + i: i for i in range(9)},
@@ -505,7 +513,7 @@
     relayed, star_t = lax.optimization_barrier((relayed, star_t))
     got_relay = moved(relayed, "hand_on")
     operands = (
-        direct, got_b, got_relay, got_xb, got_xa, got_a, own_a, own_b, side_xa, side_xb, pack_xa,
+        got_first, got_b, got_relay, got_xb, got_xa, got_a, own_a, own_b, side_xa, side_xb, pack_xa,
         star_t, star_s, inv, low, ratio,
     )
     return call(
@@ -541,9 +549,10 @@
     pairs = {
         "a": [(at(y, x), at(y ^ 1, x)) for y in range(ny) for x in range(nx)],
         "b": [(at(y, x), at(to_y, to_x)) for y, to_y, x, to_x in second],
-        "xa": [(at(y, x), at(y, x ^ 1)) for y in range(ny) for x in range(nx)],
-        "xb": [(at(y, x), at(y, beside(x))) for y in range(ny) for x in range(nx) if (y, x) not in corners],
-        "direct": [(at(y, x), at(y, beside(x))) for y, x in corners if y < ny // 2 and x % cut == cut - 1],
+        "first": [(at(y, x), at(y, x ^ 1)) for y in range(ny // 2 - 1) for x in range(nx) if x % cut < cut // 2]
+        + [(at(y, x), at(y, beside(x))) for y in (ny // 2 - 1,) for x in range(nx) if x % cut in (1, 2, cut - 1)],
+        "xa": [(at(y, x), at(y, x ^ 1)) for y in range(ny) for x in range(nx) if y >= ny // 2 - 1 or x % cut >= cut // 2],
+        "xb": [(at(y, x), at(y, beside(x))) for y in range(ny) for x in range(nx) if (y, x) not in corners and (y != ny // 2 - 1 or x % cut > 2)],
         "relay": [(at(y, x), at(y ^ 1, beside(x))) for y, x in corners if y >= ny // 2 or x % cut == 0],
         "hand_on": [(at(y ^ 1, x), at(y, x)) for y, x in corners if y >= ny // 2 or x % cut == cut - 1],
     }

time: 30.7 us -> 29.4 us (0.958)
  Pallas kernels: 6.75 us -> 5.34 us
    pallas_call x4, Pallas kernels: 6.75 us -> 5.34 us  [call(): pl.pallas_call(kernel, out_shape=[jax.ShapeDtypeStruct(getattr(s, 'shape'...]
  transfers between devices with their start and end apart: 7 -> 7, of which waited for: 2 -> 1; matrix products, arithmetic and copies ran while one was open for 0% -> 0% of each run, Pallas kernels for 11% -> 7%
where the time goes in v5:
time: 29.4 us; the launch traced here: 29.1 us
  starting transfers between devices  22.5 us (77%)
  Pallas kernels  5.34 us (18%)
  between operations  0.78 us (3%)
  waiting for transfers between devices  0.56 us (2%)
    ppermute x7, starting transfers between devices, moved(): return lax.ppermute(x, GRID_AXES, pairs[which])  22.5 us
    pallas_call x4, Pallas kernels, call(): pl.pallas_call(kernel, out_shape=[jax.ShapeDtypeStruct(getattr(s, 'shape'...  5.34 us
  transfers between devices with their start and end apart: 7, of which 1 were waited for; matrix products, arithmetic and copies ran while one was open for 0% of the time, Pallas kernels for 7%

profile of v5, /device:TPU:1, one launch (start us, length us, event | category | flops | bytes accessed | tf_op | source)
XLA Modules:
  0.0 29.1 jit_solution(12528956722245544339)
XLA Ops:
  0.6 0.0 copy-start
  0.6 0.0 copy-start.1
  0.7 1.8 %pack.1 = (f32[240,128]{1,0:T(8,128)S(1)}, f32[24,128]{1,0:T(8,128)S(1)}, f32[24,128]{1,0:T(8,128)S(1)}, f32[232,128]{1,0:T(8,128)S(1)}, f32[24,128]{1,0:T(8,128...) custom-call(f32[75,8,128]{2,1,0:T(8,128)} %t_hbm.1, ...), custom_call_target="tpu_custom_call" | custom-call | bytes 4194304 | tf_op jit(solution)/shard_map/pack/pallas_call | solution.py:468
  2.5 4.4 %collective-permute-start = (f32[24,128]{1,0:T(8,128)S(1)}, f32[24,128]{1,0:T(8,128)S(1)}, u32[]{:S(2)}, u32[]{:S(2)}) collective-permute-start(f32[24,128]{1,0:T(8,128)S(1)} %get-tuple-element.39), channel_id=1, source_target_pairs={{0,1},{1,0},{2,3},{3,2},{8,9},{9,8},{10,11},{11,10},{16,17},{17,16... | collective-permute-start | bytes 36872 | tf_op jit(solution)/shard_map/ppermute | solution.py:488
  6.9 0.0 copy-done
  6.9 0.0 copy-done.1
  6.9 2.0 %early.1 = (f32[75,8,128]{2,1,0:T(8,128)S(1)}, f32[75,8,128]{2,1,0:T(8,128)S(1)}, f32[75,8,128]{2,1,0:T(8,128)S(1)}, f32[75,8,128]{2,1,0:T(8,128)S(1)}, f32[75,8...) custom-call(f32[80,8,128]{2,1,0:T(8,128)S(1)} %get-tuple-element.41., ...), custom_call_target="tpu_custom_call" | custom-call | bytes 4194304 | tf_op jit(solution)/shard_map/early/pallas_call | solution.py:468
  8.9 4.0 %collective-permute-start.1 = (f32[240,128]{1,0:T(8,128)S(1)}, f32[240,128]{1,0:T(8,128)S(1)}, u32[]{:S(2)}, u32[]{:S(2)}) collective-permute-start(f32[240,128]{1,0:T(8,128)S(1)} %get-tuple-element.52), channel_id=1, source_target_pairs={{32,64},{33,65},{34,66},{35,67},{36,68},{37,69},{38,70},{39,71},{4... | collective-permute-start | bytes 368648 | tf_op jit(solution)/shard_map/ppermute | solution.py:488
  12.9 0.7 %collective-permute-start.2 = (f32[24,128]{1,0:T(8,128)S(1)}, f32[24,128]{1,0:T(8,128)S(1)}, u32[]{:S(2)}, u32[]{:S(2)}) collective-permute-start(f32[24,128]{1,0:T(8,128)S(1)} %get-tuple-element.53), channel_id=1, source_target_pairs={{224,223},{232,199},{240,207},{248,215},{256,319},{263,296},{264,2... | collective-permute-start | bytes 36872 | tf_op jit(solution)/shard_map/ppermute | solution.py:488
  13.5 10.2 %collective-permute-start.4 = (f32[24,128]{1,0:T(8,128)S(1)}, f32[24,128]{1,0:T(8,128)S(1)}, u32[]{:S(2)}, u32[]{:S(2)}) collective-permute-start(f32[24,128]{1,0:T(8,128)S(1)} %get-tuple-element.53), channel_id=1, source_target_pairs={{0,31},{1,2},{2,1},{3,4},{4,3},{5,6},{6,5},{7,8},{8,7},{9,10},{10,... | collective-permute-start | bytes 36872 | tf_op jit(solution)/shard_map/ppermute | solution.py:488
  23.8 0.7 %collective-permute-start.5 = (f32[24,128]{1,0:T(8,128)S(1)}, f32[24,128]{1,0:T(8,128)S(1)}, u32[]{:S(2)}, u32[]{:S(2)}) collective-permute-start(f32[24,128]{1,0:T(8,128)S(1)} %get-tuple-element.65._), channel_id=1, source_target_pairs={{4,5},{5,4},{6,7},{7,6},{12,13},{13,12},{14,15},{15,14},{20,21},{2... | collective-permute-start | bytes 36872 | tf_op jit(solution)/shard_map/ppermute | solution.py:488
  24.4 0.0 collective-permute-done.got_first
  24.4 1.9 %collective-permute-start.6 = (f32[232,128]{1,0:T(8,128)S(1)}, f32[232,128]{1,0:T(8,128)S(1)}, u32[]{:S(2)}, u32[]{:S(2)}) collective-permute-start(f32[232,128]{1,0:T(8,128)S(1)} %get-tuple-element.66), channel_id=1, source_target_pairs={{0,32},{1,33},{2,34},{3,35},{4,36},{5,37},{6,38},{7,39},{8,40},{9,... | collective-permute-start | bytes 356360 | tf_op jit(solution)/shard_map/ppermute | solution.py:488
  26.4 0.0 collective-permute-done.2
  26.4 0.7 %collective-permute-start.3 = (f32[24,128]{1,0:T(8,128)S(1)}, f32[24,128]{1,0:T(8,128)S(1)}, u32[]{:S(2)}, u32[]{:S(2)}) collective-permute-start(f32[24,128]{1,0:T(8,128)S(1)} %collective-permute-done.2), channel_id=1, source_target_pairs={{199,231},{207,239},{215,247},{223,255},{288,256},{295,263},{296,2... | collective-permute-start | bytes 36872 | tf_op jit(solution)/shard_map/ppermute | solution.py:488
  27.1 0.0 collective-permute-done.4.got_xb
  27.1 0.0 collective-permute-done.5.got_xa
  27.1 0.0 collective-permute-done.3.got_relay
  27.1 0.5 %collective-permute-done.6.got_a = f32[232,128]{1,0:T(8,128)S(1)} collective-permute-done((f32[232,128]{1,0:T(8,128)S(1)}, f32[232,128]{1,0:T(8,128)S(1)}, u32[]{:S(2)}, u32[]{:S(2)}) %collective-permute-start.6) | collective-permute-done | bytes 118816 | tf_op jit(solution)/shard_map/ppermute | solution.py:488
  27.7 0.0 collective-permute-done.1.got_b
  27.7 1.5 %final.1 = (f32[75,8,128]{2,1,0:T(8,128)}, f32[75,8,128]{2,1,0:T(8,128)}) custom-call(f32[24,128]{1,0:T(8,128)S(1)} %collective-permute-done.got_first, f32[240,128]{1,0:T(8,128)S(1)} %collective-permute-done.1.got_b, f32[24,128]{1,0:T(8,128)S(1)} %collective-permute-done.3.got_relay, f32[24,128]{1,0:T(8,128)S(1)} %collective-permute-done.4.got_xb, ...), custom_call_target="tpu_custom_call" | custom-call | bytes 4194304 | tf_op jit(solution)/shard_map/final/pallas_call | solution.py:468
  (1 shorter events, 0.0 us)
Async XLA Ops:
  0.6 6.3 %copy-start = (f32[75,8,128]{2,1,0:T(8,128)S(1)}, f32[75,8,128]{2,1,0:T(8,128)}, u32[]{:S(2)}) copy-start(f32[75,8,128]{2,1,0:T(8,128)} %refs_4_.3) | copy-start | bytes 921604
  0.6 6.3 %copy-start.1 = (f32[75,8,128]{2,1,0:T(8,128)S(1)}, f32[75,8,128]{2,1,0:T(8,128)}, u32[]{:S(2)}) copy-start(f32[75,8,128]{2,1,0:T(8,128)} %refs_5_.3) | copy-start | bytes 921604
  2.5 21.9 %collective-permute-start = (f32[24,128]{1,0:T(8,128)S(1)}, f32[24,128]{1,0:T(8,128)S(1)}, u32[]{:S(2)}, u32[]{:S(2)}) collective-permute-start(f32[24,128]{1,0:T(8,128)S(1)} %get-tuple-element.39), channel_id=1, source_target_pairs={{0,1},{1,0},{2,3},{3,2},{8,9},{9,8},{10,11},{11,10},{16,17},{17,16... | collective-permute-start | bytes 36872 | tf_op jit(solution)/shard_map/ppermute | solution.py:488
  8.9 18.8 %collective-permute-start.1 = (f32[240,128]{1,0:T(8,128)S(1)}, f32[240,128]{1,0:T(8,128)S(1)}, u32[]{:S(2)}, u32[]{:S(2)}) collective-permute-start(f32[240,128]{1,0:T(8,128)S(1)} %get-tuple-element.52), channel_id=1, source_target_pairs={{32,64},{33,65},{34,66},{35,67},{36,68},{37,69},{38,70},{39,71},{4... | collective-permute-start | bytes 368648 | tf_op jit(solution)/shard_map/ppermute | solution.py:488
  12.9 13.5 %collective-permute-start.2 = (f32[24,128]{1,0:T(8,128)S(1)}, f32[24,128]{1,0:T(8,128)S(1)}, u32[]{:S(2)}, u32[]{:S(2)}) collective-permute-start(f32[24,128]{1,0:T(8,128)S(1)} %get-tuple-element.53), channel_id=1, source_target_pairs={{224,223},{232,199},{240,207},{248,215},{256,319},{263,296},{264,2... | collective-permute-start | bytes 36872 | tf_op jit(solution)/shard_map/ppermute | solution.py:488
  13.5 13.5 %collective-permute-start.4 = (f32[24,128]{1,0:T(8,128)S(1)}, f32[24,128]{1,0:T(8,128)S(1)}, u32[]{:S(2)}, u32[]{:S(2)}) collective-permute-start(f32[24,128]{1,0:T(8,128)S(1)} %get-tuple-element.53), channel_id=1, source_target_pairs={{0,31},{1,2},{2,1},{3,4},{4,3},{5,6},{6,5},{7,8},{8,7},{9,10},{10,... | collective-permute-start | bytes 36872 | tf_op jit(solution)/shard_map/ppermute | solution.py:488
  23.8 3.3 %collective-permute-start.5 = (f32[24,128]{1,0:T(8,128)S(1)}, f32[24,128]{1,0:T(8,128)S(1)}, u32[]{:S(2)}, u32[]{:S(2)}) collective-permute-start(f32[24,128]{1,0:T(8,128)S(1)} %get-tuple-element.65._), channel_id=1, source_target_pairs={{4,5},{5,4},{6,7},{7,6},{12,13},{13,12},{14,15},{15,14},{20,21},{2... | collective-permute-start | bytes 36872 | tf_op jit(solution)/shard_map/ppermute | solution.py:488
  24.4 3.2 %collective-permute-start.6 = (f32[232,128]{1,0:T(8,128)S(1)}, f32[232,128]{1,0:T(8,128)S(1)}, u32[]{:S(2)}, u32[]{:S(2)}) collective-permute-start(f32[232,128]{1,0:T(8,128)S(1)} %get-tuple-element.66), channel_id=1, source_target_pairs={{0,32},{1,33},{2,34},{3,35},{4,36},{5,37},{6,38},{7,39},{8,40},{9,... | collective-permute-start | bytes 356360 | tf_op jit(solution)/shard_map/ppermute | solution.py:488
  26.4 0.7 %collective-permute-start.3 = (f32[24,128]{1,0:T(8,128)S(1)}, f32[24,128]{1,0:T(8,128)S(1)}, u32[]{:S(2)}, u32[]{:S(2)}) collective-permute-start(f32[24,128]{1,0:T(8,128)S(1)} %collective-permute-done.2), channel_id=1, source_target_pairs={{199,231},{207,239},{215,247},{223,255},{288,256},{295,263},{296,2... | collective-permute-start | bytes 36872 | tf_op jit(solution)/shard_map/ppermute | solution.py:488

commit v6 on v5

--- a/solution.py
+++ b/solution.py
@@ -60,8 +60,8 @@
 
 
 def pack_kernel(
-    levels, t_hbm, s_hbm, v_hbm, u_hbm, diff_hbm, depth_hbm,
-    b_ref, xb_ref, xa_ref, a_ref, own_xa_ref, own_xb_ref, first_ref, t_ref, s_ref, v_ref, u_ref, diff_ref, depth_ref, sems,
+    levels, cut, t_hbm, s_hbm, v_hbm, u_hbm, diff_hbm, depth_hbm,
+    b_ref, xb_ref, xa_ref, a_ref, own_xa_ref, own_xb_ref, first_ref, second_ref, t_ref, s_ref, v_ref, u_ref, diff_ref, depth_ref, sems,
 ):
     copies = fetch(
         (t_hbm, s_hbm, v_hbm, u_hbm, diff_hbm, depth_hbm),
@@ -121,6 +121,7 @@
         xa_ref[part] = xa
         xb_ref[part] = xb
         first_ref[part] = jnp.where(below_middle(gy), xb, xa)
+        second_ref[part] = jnp.where(jnp.logical_and(below_middle(gy), gx % cut < 2), xa, xb)
 
     copies[0].wait()
     copies[1].wait()
@@ -361,20 +362,58 @@
     return one(0), one(1)
 
 
+def columns_kernel(levels, cut, got_first, got_relay, got_xb, got_xa, side_xa, side_xb, pair_ref):
+    gy, gx = lax.axis_index("gy"), lax.axis_index("gx")
+    x_even = gx % 2 == 0
+    x_odd = jnp.logical_not(x_even)
+    corner = jnp.logical_and(is_far_row(gy), is_far_column(gx, cut))
+    xb_first = jnp.logical_and(below_middle(gy), gx % cut < 3)
+    xa_first = jnp.logical_and(starts_early(gy, gx, cut), jnp.logical_not(below_middle(gy)))
+
+    lane = lax.broadcasted_iota(jnp.int32, (ROWS, LANES), 1)
+
+    def column_change(side_ref, got, own_left):
+        own = [side_ref[i * ROWS : (i + 1) * ROWS] for i in range(9)]
+        ahead = jnp.where(own_left, 0, 1)
+        diffus, depth = edge_values(got[0], levels, ahead)
+        level = (lane - ahead).astype(jnp.float32)
+        wet = jnp.logical_and(level >= 0.0, level < jnp.minimum(own[8], depth))
+        return edge_change(
+            own, column_side(got[0], got[1], levels, ahead), own[6], got[2], 0.5 * (own[7] + diffus), wet, own_left
+        )
+
+    def thirds(ref):
+        return [ref[i * ROWS : (i + 1) * ROWS] for i in range(3)]
+
+    first, relay = thirds(got_first), thirds(got_relay)
+    xa_second = jnp.logical_and(below_middle(gy), gx % cut < 2)
+    from_xa = [
+        jnp.where(xa_first, a, jnp.where(xa_second, b, c))
+        for a, b, c in zip(first, thirds(got_xb), thirds(got_xa))
+    ]
+    from_xb = [
+        jnp.where(xb_first, a, jnp.where(corner, b, c)) for a, b, c in zip(first, relay, thirds(got_xb))
+    ]
+    change_xa = column_change(side_xa, from_xa, x_even)
+    change_xb = column_change(side_xb, from_xb, x_odd)
+    even_lane = lane % 2 == 0
+    for i in range(2):
+        last = jnp.where(x_even, change_xa[i], change_xb[i])
+        first = jnp.where(x_even, change_xb[i], change_xa[i])
+        pair_ref[i, 0] = jnp.where(even_lane, last, first)
+        pair_ref[i, 1] = jnp.where(even_lane, first, last)
+
+
 def final_kernel(
-    levels, cut, got_first, got_b, got_relay, got_xb, got_xa, got_a, own_a, own_b, side_xa, side_xb, _,
+    levels, got_b, got_a, own_a, own_b, pair_ref,
     star_t_ref, star_s_ref, inv_ref, low_ref, ratio_ref,
     out_t_ref, out_s_ref, change_ref,
 ):
     block = padded(levels)
-    gy, gx = lax.axis_index("gy"), lax.axis_index("gx")
-    y_even, x_even = gy % 2 == 0, gx % 2 == 0
-    y_odd, x_odd = jnp.logical_not(y_even), jnp.logical_not(x_even)
+    gy = lax.axis_index("gy")
+    y_even = gy % 2 == 0
+    y_odd = jnp.logical_not(y_even)
     is_top = gy == lax.axis_size("gy") - 1
-    corner = jnp.logical_and(is_far_row(gy), is_far_column(gx, cut))
-    xb_first = jnp.logical_and(below_middle(gy), gx % cut < 3)
-    xa_first = jnp.logical_and(starts_early(gy, gx, cut), jnp.logical_not(below_middle(gy)))
-
     index = lax.broadcasted_iota(jnp.int32, (block, LANES), 0)
     height = level_heights(index, levels)
     level = index.astype(jnp.float32)
@@ -400,40 +439,13 @@
 
     lane = lax.broadcasted_iota(jnp.int32, (ROWS, LANES), 1)
     row = lax.broadcasted_iota(jnp.int32, (ROWS, LANES), 0)
-
-    def column_change(side_ref, got, own_left):
-        own = [side_ref[i * ROWS : (i + 1) * ROWS] for i in range(9)]
-        ahead = jnp.where(own_left, 0, 1)
-        diffus, depth = edge_values(got[0], levels, ahead)
-        level = (lane - ahead).astype(jnp.float32)
-        wet = jnp.logical_and(level >= 0.0, level < jnp.minimum(own[8], depth))
-        return edge_change(
-            own, column_side(got[0], got[1], levels, ahead), own[6], got[2], 0.5 * (own[7] + diffus), wet, own_left
-        )
-
-    def thirds(ref):
-        return [ref[i * ROWS : (i + 1) * ROWS] for i in range(3)]
-
-    first, relay = thirds(got_first), thirds(got_relay)
-    from_xa = [jnp.where(xa_first, a, b) for a, b in zip(first, thirds(got_xa))]
-    from_xb = [
-        jnp.where(xb_first, a, jnp.where(corner, b, c)) for a, b, c in zip(first, relay, thirds(got_xb))
-    ]
-    change_xa = column_change(side_xa, from_xa, x_even)
-    change_xb = column_change(side_xb, from_xb, x_odd)
-    even_lane = lane % 2 == 0
-    paired = []
-    for i in range(2):
-        last = jnp.where(x_even, change_xa[i], change_xb[i])
-        first = jnp.where(x_even, change_xb[i], change_xa[i])
-        paired.append((jnp.where(even_lane, last, first), jnp.where(even_lane, first, last)))
     at_side = jnp.logical_or(lane == 0, lane == LANES - 1)
     row_a = row == jnp.where(y_even, ROWS - 1, 0)
     row_b = row == jnp.where(y_even, 0, ROWS - 1)
 
     def right_side(i, k):
         ref = (star_t_ref, star_s_ref)[i]
-        x_part = jnp.where(at_side, pltpu.roll(paired[i][k % 2], (LANES - 1 - k) % LANES, 1), 0.0)
+        x_part = jnp.where(at_side, pltpu.roll(pair_ref[i, k % 2], (LANES - 1 - k) % LANES, 1), 0.0)
         y_part = jnp.where(
             row_a, change_ref[0, i, k : k + 1, :], jnp.where(row_b, change_ref[1, i, k : k + 1, :], 0.0)
         )
@@ -488,8 +500,8 @@
         return lax.ppermute(x, GRID_AXES, pairs[which])
 
     operands = tuple(pltpu.with_memory_space_constraint(x, pltpu.HBM) for x in (heat, salt, v, u, diff, depth))
-    pack_b, pack_xb, pack_xa, pack_a, own_xa, own_xb, pack_first, heat, salt, v, u, diff, depth = call(
-        functools.partial(pack_kernel, levels), [wide, thin, thin, compact, thin, thin, thin] + [(block, rows, lanes)] * 4 + [diff.shape, depth],
+    pack_b, pack_xb, pack_xa, pack_a, own_xa, own_xb, pack_first, pack_second, heat, salt, v, u, diff, depth = call(
+        functools.partial(pack_kernel, levels, cut), [wide, thin, thin, compact, thin, thin, thin, thin] + [(block, rows, lanes)] * 4 + [diff.shape, depth],
         operands, pltpu.HBM, [pltpu.SemaphoreType.DMA((6,))], name="pack",
     )
     group = next(g for g in (15, 5, 3, 2, 1) if levels % g == 0)
@@ -502,7 +514,7 @@
     pack_b, early[0] = lax.optimization_barrier((pack_b, early[0]))
     got_b = moved(pack_b, "b")
     relayed = moved(pack_xb, "relay")
-    got_xb = moved(pack_xb, "xb")
+    got_xb = moved(pack_second, "xb")
     got_xa = moved(pack_xa, "xa")
     got_a = moved(pack_a, "a")
     got_first, early[0] = lax.optimization_barrier((got_first, early[0]))
@@ -512,12 +524,16 @@
     )
     relayed, star_t = lax.optimization_barrier((relayed, star_t))
     got_relay = moved(relayed, "hand_on")
+    pair = call(
+        functools.partial(columns_kernel, levels, cut), [(2, 2, rows, lanes)],
+        (got_first, got_relay, got_xb, got_xa, side_xa, side_xb), pltpu.VMEM, name="columns",
+    )[0]
     operands = (
-        got_first, got_b, got_relay, got_xb, got_xa, got_a, own_a, own_b, side_xa, side_xb, pack_xa,
+        got_b, got_a, own_a, own_b, pair,
         star_t, star_s, inv, low, ratio,
     )
     return call(
-        functools.partial(final_kernel, levels, cut),
+        functools.partial(final_kernel, levels),
         [cube] * 2, operands, pltpu.VMEM, [pltpu.VMEM((2, 2, block, lanes), jnp.float32)], name="final",
     )
 
@@ -551,8 +567,9 @@
         "b": [(at(y, x), at(to_y, to_x)) for y, to_y, x, to_x in second],
         "first": [(at(y, x), at(y, x ^ 1)) for y in range(ny // 2 - 1) for x in range(nx) if x % cut < cut // 2]
         + [(at(y, x), at(y, beside(x))) for y in (ny // 2 - 1,) for x in range(nx) if x % cut in (1, 2, cut - 1)],
-        "xa": [(at(y, x), at(y, x ^ 1)) for y in range(ny) for x in range(nx) if y >= ny // 2 - 1 or x % cut >= cut // 2],
-        "xb": [(at(y, x), at(y, beside(x))) for y in range(ny) for x in range(nx) if (y, x) not in corners and (y != ny // 2 - 1 or x % cut > 2)],
+        "xa": [(at(y, x), at(y, x ^ 1)) for y in range(ny) for x in range(nx) if y >= ny // 2 or x % cut >= (cut // 2 if y < ny // 2 - 1 else 2)],
+        "xb": [(at(y, x), at(y, beside(x))) for y in range(ny) for x in range(nx) if (y, x) not in corners and (y != ny // 2 - 1 or x % cut > 2)]
+        + [(at(ny // 2 - 1, x), at(ny // 2 - 1, x ^ 1)) for x in range(nx) if x % cut < 2],
         "relay": [(at(y, x), at(y ^ 1, beside(x))) for y, x in corners if y >= ny // 2 or x % cut == 0],
         "hand_on": [(at(y ^ 1, x), at(y, x)) for y, x in corners if y >= ny // 2 or x % cut == cut - 1],
     }

time: 29.4 us -> 29.3 us (level)
    pallas_call x4 -> x5, Pallas kernels: 5.34 us -> 5.4 us  [call(): pl.pallas_call(kernel, out_shape=[jax.ShapeDtypeStruct(getattr(s, 'shape'...]
  transfers between devices with their start and end apart: 7 -> 7, of which waited for: 1 -> 1; matrix products, arithmetic and copies ran while one was open for 0% -> 0% of each run, Pallas kernels for 7% -> 8%
where the time goes in v6:
time: 29.3 us; the launch traced here: 29 us
  starting transfers between devices  22.5 us (77%)
  Pallas kernels  5.4 us (18%)
  between operations  0.79 us (3%)
  waiting for transfers between devices  0.38 us (1%)
    ppermute x7, starting transfers between devices, moved(): return lax.ppermute(x, GRID_AXES, pairs[which])  22.5 us
    pallas_call x5, Pallas kernels, call(): pl.pallas_call(kernel, out_shape=[jax.ShapeDtypeStruct(getattr(s, 'shape'...  5.4 us
  transfers between devices with their start and end apart: 7, of which 1 were waited for; matrix products, arithmetic and copies ran while one was open for 0% of the time, Pallas kernels for 8%

profile of v6, /device:TPU:1, one launch (start us, length us, event | category | flops | bytes accessed | tf_op | source)
XLA Modules:
  0.0 29.0 jit_solution(4721597955171435714)
XLA Ops:
  0.6 0.0 copy-start.1
  0.6 0.0 copy-start
  0.7 1.8 %pack.1 = (f32[240,128]{1,0:T(8,128)S(1)}, f32[24,128]{1,0:T(8,128)S(1)}, f32[24,128]{1,0:T(8,128)S(1)}, f32[232,128]{1,0:T(8,128)S(1)}, f32[24,128]{1,0:T(8,128...) custom-call(f32[75,8,128]{2,1,0:T(8,128)} %t_hbm.1, ...), custom_call_target="tpu_custom_call" | custom-call | bytes 4194304 | tf_op jit(solution)/shard_map/pack/pallas_call | solution.py:480
  2.5 4.4 %collective-permute-start.2 = (f32[24,128]{1,0:T(8,128)S(1)}, f32[24,128]{1,0:T(8,128)S(1)}, u32[]{:S(2)}, u32[]{:S(2)}) collective-permute-start(f32[24,128]{1,0:T(8,128)S(1)} %get-tuple-element.52), channel_id=1, source_target_pairs={{0,1},{1,0},{2,3},{3,2},{8,9},{9,8},{10,11},{11,10},{16,17},{17,16... | collective-permute-start | bytes 36872 | tf_op jit(solution)/shard_map/ppermute | solution.py:500
  6.9 0.0 copy-done.1
  6.9 0.0 copy-done
  6.9 2.0 %early.1 = (f32[75,8,128]{2,1,0:T(8,128)S(1)}, f32[75,8,128]{2,1,0:T(8,128)S(1)}, f32[75,8,128]{2,1,0:T(8,128)S(1)}, f32[75,8,128]{2,1,0:T(8,128)S(1)}, f32[75,8...) custom-call(f32[80,8,128]{2,1,0:T(8,128)S(1)} %get-tuple-element.41., ...), custom_call_target="tpu_custom_call" | custom-call | bytes 4194304 | tf_op jit(solution)/shard_map/early/pallas_call | solution.py:480
  8.9 4.0 %collective-permute-start = (f32[240,128]{1,0:T(8,128)S(1)}, f32[240,128]{1,0:T(8,128)S(1)}, u32[]{:S(2)}, u32[]{:S(2)}) collective-permute-start(f32[240,128]{1,0:T(8,128)S(1)} %get-tuple-element.50), channel_id=1, source_target_pairs={{32,64},{33,65},{34,66},{35,67},{36,68},{37,69},{38,70},{39,71},{4... | collective-permute-start | bytes 368648 | tf_op jit(solution)/shard_map/ppermute | solution.py:500
  12.9 0.7 %collective-permute-start.3 = (f32[24,128]{1,0:T(8,128)S(1)}, f32[24,128]{1,0:T(8,128)S(1)}, u32[]{:S(2)}, u32[]{:S(2)}) collective-permute-start(f32[24,128]{1,0:T(8,128)S(1)} %get-tuple-element.66), channel_id=1, source_target_pairs={{224,223},{232,199},{240,207},{248,215},{256,319},{263,296},{264,2... | collective-permute-start | bytes 36872 | tf_op jit(solution)/shard_map/ppermute | solution.py:500
  13.5 10.2 %collective-permute-start.5 = (f32[24,128]{1,0:T(8,128)S(1)}, f32[24,128]{1,0:T(8,128)S(1)}, u32[]{:S(2)}, u32[]{:S(2)}) collective-permute-start(f32[24,128]{1,0:T(8,128)S(1)} %get-tuple-element.69), channel_id=1, source_target_pairs={{0,31},{1,2},{2,1},{3,4},{4,3},{5,6},{6,5},{7,8},{8,7},{9,10},{10,... | collective-permute-start | bytes 36872 | tf_op jit(solution)/shard_map/ppermute | solution.py:500
  23.8 0.7 %collective-permute-start.6 = (f32[24,128]{1,0:T(8,128)S(1)}, f32[24,128]{1,0:T(8,128)S(1)}, u32[]{:S(2)}, u32[]{:S(2)}) collective-permute-start(f32[24,128]{1,0:T(8,128)S(1)} %get-tuple-element.70), channel_id=1, source_target_pairs={{4,5},{5,4},{6,7},{7,6},{12,13},{13,12},{14,15},{15,14},{20,21},{2... | collective-permute-start | bytes 36872 | tf_op jit(solution)/shard_map/ppermute | solution.py:500
  24.4 0.0 collective-permute-done.2.got_first
  24.4 1.9 %collective-permute-start.1 = (f32[232,128]{1,0:T(8,128)S(1)}, f32[232,128]{1,0:T(8,128)S(1)}, u32[]{:S(2)}, u32[]{:S(2)}) collective-permute-start(f32[232,128]{1,0:T(8,128)S(1)} %get-tuple-element.51), channel_id=1, source_target_pairs={{0,32},{1,33},{2,34},{3,35},{4,36},{5,37},{6,38},{7,39},{8,40},{9,... | collective-permute-start | bytes 356360 | tf_op jit(solution)/shard_map/ppermute | solution.py:500
  26.4 0.0 collective-permute-done.3
  26.4 0.7 %collective-permute-start.4 = (f32[24,128]{1,0:T(8,128)S(1)}, f32[24,128]{1,0:T(8,128)S(1)}, u32[]{:S(2)}, u32[]{:S(2)}) collective-permute-start(f32[24,128]{1,0:T(8,128)S(1)} %collective-permute-done.3), channel_id=1, source_target_pairs={{199,231},{207,239},{215,247},{223,255},{288,256},{295,263},{296,2... | collective-permute-start | bytes 36872 | tf_op jit(solution)/shard_map/ppermute | solution.py:500
  27.1 0.0 collective-permute-done.5.got_xb
  27.1 0.0 collective-permute-done.6.got_xa
  27.1 0.0 collective-permute-done.4.got_relay
  27.1 0.2 columns.1.pair_ref
  27.3 0.4 %collective-permute-done.1.got_a = f32[232,128]{1,0:T(8,128)S(1)} collective-permute-done((f32[232,128]{1,0:T(8,128)S(1)}, f32[232,128]{1,0:T(8,128)S(1)}, u32[]{:S(2)}, u32[]{:S(2)}) %collective-permute-start.1) | collective-permute-done | bytes 118816 | tf_op jit(solution)/shard_map/ppermute | solution.py:500
  27.7 0.0 collective-permute-done.got_b
  27.7 1.4 %final.1 = (f32[75,8,128]{2,1,0:T(8,128)}, f32[75,8,128]{2,1,0:T(8,128)}) custom-call(f32[240,128]{1,0:T(8,128)S(1)} %collective-permute-done.got_b, f32[232,128]{1,0:T(8,128)S(1)} %collective-permute-done.1.got_a, f32[560,128]{1,0:T(8,128)S(1)} %get-tuple-element.63.own_a, f32[560,128]{1,0:T(8,128)S(1)} %get-tuple-element.64.own_b, ...), custom_call_target="tpu_custom_call" | custom-call | bytes 4194304 | tf_op jit(solution)/shard_map/final/pallas_call | solution.py:480
  (1 shorter events, 0.0 us)
Async XLA Ops:
  0.6 6.3 %copy-start.1 = (f32[75,8,128]{2,1,0:T(8,128)S(1)}, f32[75,8,128]{2,1,0:T(8,128)}, u32[]{:S(2)}) copy-start(f32[75,8,128]{2,1,0:T(8,128)} %refs_5_.3) | copy-start | bytes 921604
  0.6 6.3 %copy-start = (f32[75,8,128]{2,1,0:T(8,128)S(1)}, f32[75,8,128]{2,1,0:T(8,128)}, u32[]{:S(2)}) copy-start(f32[75,8,128]{2,1,0:T(8,128)} %refs_4_.3) | copy-start | bytes 921604
  2.5 21.9 %collective-permute-start.2 = (f32[24,128]{1,0:T(8,128)S(1)}, f32[24,128]{1,0:T(8,128)S(1)}, u32[]{:S(2)}, u32[]{:S(2)}) collective-permute-start(f32[24,128]{1,0:T(8,128)S(1)} %get-tuple-element.52), channel_id=1, source_target_pairs={{0,1},{1,0},{2,3},{3,2},{8,9},{9,8},{10,11},{11,10},{16,17},{17,16... | collective-permute-start | bytes 36872 | tf_op jit(solution)/shard_map/ppermute | solution.py:500
  8.9 18.8 %collective-permute-start = (f32[240,128]{1,0:T(8,128)S(1)}, f32[240,128]{1,0:T(8,128)S(1)}, u32[]{:S(2)}, u32[]{:S(2)}) collective-permute-start(f32[240,128]{1,0:T(8,128)S(1)} %get-tuple-element.50), channel_id=1, source_target_pairs={{32,64},{33,65},{34,66},{35,67},{36,68},{37,69},{38,70},{39,71},{4... | collective-permute-start | bytes 368648 | tf_op jit(solution)/shard_map/ppermute | solution.py:500
  12.9 13.5 %collective-permute-start.3 = (f32[24,128]{1,0:T(8,128)S(1)}, f32[24,128]{1,0:T(8,128)S(1)}, u32[]{:S(2)}, u32[]{:S(2)}) collective-permute-start(f32[24,128]{1,0:T(8,128)S(1)} %get-tuple-element.66), channel_id=1, source_target_pairs={{224,223},{232,199},{240,207},{248,215},{256,319},{263,296},{264,2... | collective-permute-start | bytes 36872 | tf_op jit(solution)/shard_map/ppermute | solution.py:500
  13.5 13.5 %collective-permute-start.5 = (f32[24,128]{1,0:T(8,128)S(1)}, f32[24,128]{1,0:T(8,128)S(1)}, u32[]{:S(2)}, u32[]{:S(2)}) collective-permute-start(f32[24,128]{1,0:T(8,128)S(1)} %get-tuple-element.69), channel_id=1, source_target_pairs={{0,31},{1,2},{2,1},{3,4},{4,3},{5,6},{6,5},{7,8},{8,7},{9,10},{10,... | collective-permute-start | bytes 36872 | tf_op jit(solution)/shard_map/ppermute | solution.py:500
  23.8 3.3 %collective-permute-start.6 = (f32[24,128]{1,0:T(8,128)S(1)}, f32[24,128]{1,0:T(8,128)S(1)}, u32[]{:S(2)}, u32[]{:S(2)}) collective-permute-start(f32[24,128]{1,0:T(8,128)S(1)} %get-tuple-element.70), channel_id=1, source_target_pairs={{4,5},{5,4},{6,7},{7,6},{12,13},{13,12},{14,15},{15,14},{20,21},{2... | collective-permute-start | bytes 36872 | tf_op jit(solution)/shard_map/ppermute | solution.py:500
  24.4 3.2 %collective-permute-start.1 = (f32[232,128]{1,0:T(8,128)S(1)}, f32[232,128]{1,0:T(8,128)S(1)}, u32[]{:S(2)}, u32[]{:S(2)}) collective-permute-start(f32[232,128]{1,0:T(8,128)S(1)} %get-tuple-element.51), channel_id=1, source_target_pairs={{0,32},{1,33},{2,34},{3,35},{4,36},{5,37},{6,38},{7,39},{8,40},{9,... | collective-permute-start | bytes 356360 | tf_op jit(solution)/shard_map/ppermute | solution.py:500
  26.4 0.7 %collective-permute-start.4 = (f32[24,128]{1,0:T(8,128)S(1)}, f32[24,128]{1,0:T(8,128)S(1)}, u32[]{:S(2)}, u32[]{:S(2)}) collective-permute-start(f32[24,128]{1,0:T(8,128)S(1)} %collective-permute-done.3), channel_id=1, source_target_pairs={{199,231},{207,239},{215,247},{223,255},{288,256},{295,263},{296,2... | collective-permute-start | bytes 36872 | tf_op jit(solution)/shard_map/ppermute | solution.py:500

commit v7 on v6

--- a/solution.py
+++ b/solution.py
@@ -105,14 +105,14 @@
         if i == 0:
             planes += [diff, depth]
         zero = jnp.zeros((ROWS, LANES), jnp.float32)
-        east, west = [zero] * 4, [zero] * 4
+        east, west = [zero] * 8, [zero] * 8
         for k, plane in enumerate(planes):
             moved = pltpu.roll(plane, k + 1, 1)
-            east[k % 4] = jnp.where(one_lane == k, moved, east[k % 4])
+            east[k % 8] = jnp.where(one_lane == k, moved, east[k % 8])
             if i < 2:
-                west[k % 4] = jnp.where(one_lane == k + 1, moved, west[k % 4])
-        east = (east[0] + east[1]) + (east[2] + east[3])
-        west = (west[0] + west[1]) + (west[2] + west[3])
+                west[k % 8] = jnp.where(one_lane == k + 1, moved, west[k % 8])
+        east = functools.reduce(jnp.add, east)
+        west = functools.reduce(jnp.add, west)
         part = slice(i * ROWS, (i + 1) * ROWS)
         own_xa_ref[part] = jnp.where(x_even, east, west)
         own_xb_ref[part] = jnp.where(x_even, west, east)

time: 29.3 us -> 29.3 us (level)
  no operation moved by 1% of the time
where the time goes in v7:
time: 29.3 us; the launch traced here: 29 us
  starting transfers between devices  22.5 us (77%)
  Pallas kernels  5.4 us (18%)
  between operations  0.79 us (3%)
  waiting for transfers between devices  0.38 us (1%)
    ppermute x7, starting transfers between devices, moved(): return lax.ppermute(x, GRID_AXES, pairs[which])  22.5 us
    pallas_call x5, Pallas kernels, call(): pl.pallas_call(kernel, out_shape=[jax.ShapeDtypeStruct(getattr(s, 'shape'...  5.4 us
  transfers between devices with their start and end apart: 7, of which 1 were waited for; matrix products, arithmetic and copies ran while one was open for 0% of the time, Pallas kernels for 8%

profile of v7, /device:TPU:1, one launch (start us, length us, event | category | flops | bytes accessed | tf_op | source)
XLA Modules:
  0.0 29.0 jit_solution(17756797477762391124)
XLA Ops:
  0.6 0.0 copy-start.1
  0.6 0.0 copy-start
  0.7 1.8 %pack.1 = (f32[240,128]{1,0:T(8,128)S(1)}, f32[24,128]{1,0:T(8,128)S(1)}, f32[24,128]{1,0:T(8,128)S(1)}, f32[232,128]{1,0:T(8,128)S(1)}, f32[24,128]{1,0:T(8,128...) custom-call(f32[75,8,128]{2,1,0:T(8,128)} %t_hbm.1, ...), custom_call_target="tpu_custom_call" | custom-call | bytes 4194304 | tf_op jit(solution)/shard_map/pack/pallas_call | solution.py:480
  2.5 4.4 %collective-permute-start.2 = (f32[24,128]{1,0:T(8,128)S(1)}, f32[24,128]{1,0:T(8,128)S(1)}, u32[]{:S(2)}, u32[]{:S(2)}) collective-permute-start(f32[24,128]{1,0:T(8,128)S(1)} %get-tuple-element.52), channel_id=1, source_target_pairs={{0,1},{1,0},{2,3},{3,2},{8,9},{9,8},{10,11},{11,10},{16,17},{17,16... | collective-permute-start | bytes 36872 | tf_op jit(solution)/shard_map/ppermute | solution.py:500
  6.9 0.0 copy-done.1
  6.9 0.0 copy-done
  6.9 2.0 %early.1 = (f32[75,8,128]{2,1,0:T(8,128)S(1)}, f32[75,8,128]{2,1,0:T(8,128)S(1)}, f32[75,8,128]{2,1,0:T(8,128)S(1)}, f32[75,8,128]{2,1,0:T(8,128)S(1)}, f32[75,8...) custom-call(f32[80,8,128]{2,1,0:T(8,128)S(1)} %get-tuple-element.41., ...), custom_call_target="tpu_custom_call" | custom-call | bytes 4194304 | tf_op jit(solution)/shard_map/early/pallas_call | solution.py:480
  8.9 4.0 %collective-permute-start = (f32[240,128]{1,0:T(8,128)S(1)}, f32[240,128]{1,0:T(8,128)S(1)}, u32[]{:S(2)}, u32[]{:S(2)}) collective-permute-start(f32[240,128]{1,0:T(8,128)S(1)} %get-tuple-element.50), channel_id=1, source_target_pairs={{32,64},{33,65},{34,66},{35,67},{36,68},{37,69},{38,70},{39,71},{4... | collective-permute-start | bytes 368648 | tf_op jit(solution)/shard_map/ppermute | solution.py:500
  12.9 0.7 %collective-permute-start.3 = (f32[24,128]{1,0:T(8,128)S(1)}, f32[24,128]{1,0:T(8,128)S(1)}, u32[]{:S(2)}, u32[]{:S(2)}) collective-permute-start(f32[24,128]{1,0:T(8,128)S(1)} %get-tuple-element.66), channel_id=1, source_target_pairs={{224,223},{232,199},{240,207},{248,215},{256,319},{263,296},{264,2... | collective-permute-start | bytes 36872 | tf_op jit(solution)/shard_map/ppermute | solution.py:500
  13.5 10.2 %collective-permute-start.5 = (f32[24,128]{1,0:T(8,128)S(1)}, f32[24,128]{1,0:T(8,128)S(1)}, u32[]{:S(2)}, u32[]{:S(2)}) collective-permute-start(f32[24,128]{1,0:T(8,128)S(1)} %get-tuple-element.69), channel_id=1, source_target_pairs={{0,31},{1,2},{2,1},{3,4},{4,3},{5,6},{6,5},{7,8},{8,7},{9,10},{10,... | collective-permute-start | bytes 36872 | tf_op jit(solution)/shard_map/ppermute | solution.py:500
  23.8 0.7 %collective-permute-start.6 = (f32[24,128]{1,0:T(8,128)S(1)}, f32[24,128]{1,0:T(8,128)S(1)}, u32[]{:S(2)}, u32[]{:S(2)}) collective-permute-start(f32[24,128]{1,0:T(8,128)S(1)} %get-tuple-element.70), channel_id=1, source_target_pairs={{4,5},{5,4},{6,7},{7,6},{12,13},{13,12},{14,15},{15,14},{20,21},{2... | collective-permute-start | bytes 36872 | tf_op jit(solution)/shard_map/ppermute | solution.py:500
  24.4 0.0 collective-permute-done.2.got_first
  24.4 1.9 %collective-permute-start.1 = (f32[232,128]{1,0:T(8,128)S(1)}, f32[232,128]{1,0:T(8,128)S(1)}, u32[]{:S(2)}, u32[]{:S(2)}) collective-permute-start(f32[232,128]{1,0:T(8,128)S(1)} %get-tuple-element.51), channel_id=1, source_target_pairs={{0,32},{1,33},{2,34},{3,35},{4,36},{5,37},{6,38},{7,39},{8,40},{9,... | collective-permute-start | bytes 356360 | tf_op jit(solution)/shard_map/ppermute | solution.py:500
  26.4 0.0 collective-permute-done.3
  26.4 0.7 %collective-permute-start.4 = (f32[24,128]{1,0:T(8,128)S(1)}, f32[24,128]{1,0:T(8,128)S(1)}, u32[]{:S(2)}, u32[]{:S(2)}) collective-permute-start(f32[24,128]{1,0:T(8,128)S(1)} %collective-permute-done.3), channel_id=1, source_target_pairs={{199,231},{207,239},{215,247},{223,255},{288,256},{295,263},{296,2... | collective-permute-start | bytes 36872 | tf_op jit(solution)/shard_map/ppermute | solution.py:500
  27.1 0.0 collective-permute-done.5.got_xb
  27.1 0.0 collective-permute-done.6.got_xa
  27.1 0.0 collective-permute-done.4.got_relay
  27.1 0.2 columns.1.pair_ref
  27.3 0.4 %collective-permute-done.1.got_a = f32[232,128]{1,0:T(8,128)S(1)} collective-permute-done((f32[232,128]{1,0:T(8,128)S(1)}, f32[232,128]{1,0:T(8,128)S(1)}, u32[]{:S(2)}, u32[]{:S(2)}) %collective-permute-start.1) | collective-permute-done | bytes 118816 | tf_op jit(solution)/shard_map/ppermute | solution.py:500
  27.7 0.0 collective-permute-done.got_b
  27.7 1.4 %final.1 = (f32[75,8,128]{2,1,0:T(8,128)}, f32[75,8,128]{2,1,0:T(8,128)}) custom-call(f32[240,128]{1,0:T(8,128)S(1)} %collective-permute-done.got_b, f32[232,128]{1,0:T(8,128)S(1)} %collective-permute-done.1.got_a, f32[560,128]{1,0:T(8,128)S(1)} %get-tuple-element.63.own_a, f32[560,128]{1,0:T(8,128)S(1)} %get-tuple-element.64.own_b, ...), custom_call_target="tpu_custom_call" | custom-call | bytes 4194304 | tf_op jit(solution)/shard_map/final/pallas_call | solution.py:480
  (1 shorter events, 0.0 us)
Async XLA Ops:
  0.6 6.3 %copy-start.1 = (f32[75,8,128]{2,1,0:T(8,128)S(1)}, f32[75,8,128]{2,1,0:T(8,128)}, u32[]{:S(2)}) copy-start(f32[75,8,128]{2,1,0:T(8,128)} %refs_5_.3) | copy-start | bytes 921604
  0.6 6.3 %copy-start = (f32[75,8,128]{2,1,0:T(8,128)S(1)}, f32[75,8,128]{2,1,0:T(8,128)}, u32[]{:S(2)}) copy-start(f32[75,8,128]{2,1,0:T(8,128)} %refs_4_.3) | copy-start | bytes 921604
  2.5 21.9 %collective-permute-start.2 = (f32[24,128]{1,0:T(8,128)S(1)}, f32[24,128]{1,0:T(8,128)S(1)}, u32[]{:S(2)}, u32[]{:S(2)}) collective-permute-start(f32[24,128]{1,0:T(8,128)S(1)} %get-tuple-element.52), channel_id=1, source_target_pairs={{0,1},{1,0},{2,3},{3,2},{8,9},{9,8},{10,11},{11,10},{16,17},{17,16... | collective-permute-start | bytes 36872 | tf_op jit(solution)/shard_map/ppermute | solution.py:500
  8.9 18.8 %collective-permute-start = (f32[240,128]{1,0:T(8,128)S(1)}, f32[240,128]{1,0:T(8,128)S(1)}, u32[]{:S(2)}, u32[]{:S(2)}) collective-permute-start(f32[240,128]{1,0:T(8,128)S(1)} %get-tuple-element.50), channel_id=1, source_target_pairs={{32,64},{33,65},{34,66},{35,67},{36,68},{37,69},{38,70},{39,71},{4... | collective-permute-start | bytes 368648 | tf_op jit(solution)/shard_map/ppermute | solution.py:500
  12.9 13.5 %collective-permute-start.3 = (f32[24,128]{1,0:T(8,128)S(1)}, f32[24,128]{1,0:T(8,128)S(1)}, u32[]{:S(2)}, u32[]{:S(2)}) collective-permute-start(f32[24,128]{1,0:T(8,128)S(1)} %get-tuple-element.66), channel_id=1, source_target_pairs={{224,223},{232,199},{240,207},{248,215},{256,319},{263,296},{264,2... | collective-permute-start | bytes 36872 | tf_op jit(solution)/shard_map/ppermute | solution.py:500
  13.5 13.5 %collective-permute-start.5 = (f32[24,128]{1,0:T(8,128)S(1)}, f32[24,128]{1,0:T(8,128)S(1)}, u32[]{:S(2)}, u32[]{:S(2)}) collective-permute-start(f32[24,128]{1,0:T(8,128)S(1)} %get-tuple-element.69), channel_id=1, source_target_pairs={{0,31},{1,2},{2,1},{3,4},{4,3},{5,6},{6,5},{7,8},{8,7},{9,10},{10,... | collective-permute-start | bytes 36872 | tf_op jit(solution)/shard_map/ppermute | solution.py:500
  23.8 3.3 %collective-permute-start.6 = (f32[24,128]{1,0:T(8,128)S(1)}, f32[24,128]{1,0:T(8,128)S(1)}, u32[]{:S(2)}, u32[]{:S(2)}) collective-permute-start(f32[24,128]{1,0:T(8,128)S(1)} %get-tuple-element.70), channel_id=1, source_target_pairs={{4,5},{5,4},{6,7},{7,6},{12,13},{13,12},{14,15},{15,14},{20,21},{2... | collective-permute-start | bytes 36872 | tf_op jit(solution)/shard_map/ppermute | solution.py:500
  24.4 3.2 %collective-permute-start.1 = (f32[232,128]{1,0:T(8,128)S(1)}, f32[232,128]{1,0:T(8,128)S(1)}, u32[]{:S(2)}, u32[]{:S(2)}) collective-permute-start(f32[232,128]{1,0:T(8,128)S(1)} %get-tuple-element.51), channel_id=1, source_target_pairs={{0,32},{1,33},{2,34},{3,35},{4,36},{5,37},{6,38},{7,39},{8,40},{9,... | collective-permute-start | bytes 356360 | tf_op jit(solution)/shard_map/ppermute | solution.py:500
  26.4 0.7 %collective-permute-start.4 = (f32[24,128]{1,0:T(8,128)S(1)}, f32[24,128]{1,0:T(8,128)S(1)}, u32[]{:S(2)}, u32[]{:S(2)}) collective-permute-start(f32[24,128]{1,0:T(8,128)S(1)} %collective-permute-done.3), channel_id=1, source_target_pairs={{199,231},{207,239},{215,247},{223,255},{288,256},{295,263},{296,2... | collective-permute-start | bytes 36872 | tf_op jit(solution)/shard_map/ppermute | solution.py:500
